TPU v7x, 32 devices: a whole 2x2x4 slice. The times are simulated.
32 devices in a mesh: gx: 4 (over z), gy: 8 (over y, x, core).
Axes of the slice: x: 2, y: 2, z: 4, core: 2. Of those that a mesh axis runs over, the one named last changes fastest.
Arguments:
- scalars: float32 [4, 64, 64, 1024], P(None, None, 'gx', 'gy'), may hold values from -6 to 6
- winds: float32 [2, 64, 64, 1024], P(None, None, 'gx', 'gy'), may hold values from -0.6 to 0.6
- map_factor: float32 [64, 1024], P('gx', 'gy'), may hold values from 0.7 to 1.3
- urban_counts: int32 [32], P(('gx', 'gy')), may hold values from 64 to 256, as said below
- urban_cols: int32 [8192], P(('gx', 'gy')), may hold values from 0 to 2047, as said below
- street_class: int32 [8192], P(('gx', 'gy')), may hold values from 0 to 9
- area_table: float32 [10, 10], replicated, may hold values from 0.2 to 1
- wall_temp: float32 [10, 8192], P(None, ('gx', 'gy')), may hold values from -6 to 6
- indoor_temp: float32 [8192], P(('gx', 'gy')), may hold values from -6 to 6
Outputs:
- scalars_out: float32 [4, 64, 64, 1024], P(None, None, 'gx', 'gy')
- wall_out: float32 [10, 8192], P(None, ('gx', 'gy'))
- indoor_out: float32 [8192], P(('gx', 'gy'))
Inputs may be any that keep to these rules, and one draw needn't show every extreme that they name: `urban_counts`: some tile has exactly 256 live urban columns. `urban_cols`: the 256 entries of each tile are distinct cells of that tile, numbered x * 128 + y within it.
All inputs are finite; a program needn't handle non-finite values.
Results may differ from a plain program's by a relative error of at most 0.000056.
Values sent between devices are 32-bit elements; how exact they have to be, the bound alone decides.
No kernel may reach another device: no remote copies, remote signals or barrier semaphores. Data moves between devices by JAX's collectives and lax.ppermute only.
A program may use at most 192 MiB of HBM per device.

v0:
```python
import functools

import jax
import jax.numpy as jnp
import ml_dtypes
import numpy as np
from jax import lax
from jax.experimental import pallas as pl
from jax.experimental.pallas import tpu as pltpu
from jax.sharding import PartitionSpec as P

UL = 10
NWL = 10
NCLS = 10
WIDTH = 3
GROUP = 8
CHUNKS = 2
PIECE = 512
UNROLL = 2
DIVISORS = (3.0, 2.0, 1.0)
HIGH = (1, -8, 37, 37, -8, 1)
DAMP = (-1, 5, -10, 10, -5, 1)

heat_coef = 0.5
wall_coef = 0.05
conduct = 0.3
inner_coef = 0.2
room_coef = 0.1
flux_coef = 0.5
face_scale = 0.5 / 60.0


def lane_index(shape):
    return lax.broadcasted_iota(jnp.int32, shape, 1)


def rolled(array, shift):
    return pltpu.roll(array, shift % array.shape[1], 1)


def pack_edges(packed, row, x):
    moved = rolled(row, GROUP * x + WIDTH)
    lane = lane_index(row.shape)
    here = (lane >= GROUP * x) & (lane < GROUP * x + 2 * WIDTH)
    return moved if packed is None else jnp.where(here, moved, packed)


def ahead(row, halo, lane, k):
    if k > 0:
        return rolled(jnp.where(lane < k, halo, row), -k)
    return rolled(jnp.where(lane >= row.shape[1] + k, halo, row), -k)


def first_rows_kernel(x_size, rows, levels, pieces, odd, field, wind, to_a, to_b, field_here, wind_here, sems):
    size = rows * x_size // pieces
    copies = [
        pltpu.make_async_copy(field.at[pl.ds(p * size, size), :], field_here.at[pl.ds(p * size, size), :], sems.at[p])
        for p in range(pieces)
    ]
    copies.append(pltpu.make_async_copy(wind.at[pl.ds(0, levels * x_size), :], wind_here, sems.at[pieces]))
    for copy in copies:
        copy.start()
    even = odd[0] == 0
    for p in range(pieces):
        copies[p].wait()
        for t in range(p * rows // pieces // 8, (p + 1) * rows // pieces // 8):
            for j in range(WIDTH):
                low = field_here[pl.ds(t * 8 * x_size + j, 8, stride=x_size), :]
                high = field_here[pl.ds(t * 8 * x_size + x_size - WIDTH + j, 8, stride=x_size), :]
                to_a[j * rows + t * 8 : j * rows + t * 8 + 8, :] = jnp.where(even, high, low)
                to_b[j * rows + t * 8 : j * rows + t * 8 + 8, :] = jnp.where(even, low, high)
    copies[pieces].wait()
    for t in range(levels // 8):
        low = wind_here[pl.ds(t * 8 * x_size, 8, stride=x_size), :]
        high = wind_here[pl.ds(t * 8 * x_size + x_size - 1, 8, stride=x_size), :]
        at = WIDTH * rows + t * 8
        to_a[at : at + 8, :] = jnp.where(even, high, low)
        to_b[at : at + 8, :] = jnp.where(even, low, high)


def extract_kernel(x_size, chunk, with_wind, odd, field, *refs):
    if with_wind:
        wind, packed = refs
    else:
        to_a, to_b, packed = refs
    rows = packed.shape[0]
    if with_wind:
        levels = wind.shape[0] // (2 * x_size)
        rows = rows - levels
    even = odd[0] == 0

    def one(t, carry):
        base = pl.multiple_of((chunk * rows + t * 8) * x_size, 8 * x_size)
        edges = None
        for x in range(x_size):
            edges = pack_edges(edges, field[pl.ds(base + x, 8, stride=x_size), :], x)
        packed[pl.ds(pl.multiple_of(t * 8, 8), 8), :] = edges
        if not with_wind:
            for j in range(WIDTH):
                low = field[pl.ds(base + j, 8, stride=x_size), :]
                high = field[pl.ds(base + x_size - WIDTH + j, 8, stride=x_size), :]
                at = pl.ds(pl.multiple_of(j * rows + t * 8, 8), 8)
                to_a[at, :] = jnp.where(even, high, low)
                to_b[at, :] = jnp.where(even, low, high)
        return carry

    lax.fori_loop(0, rows // 8, one, 0, unroll=4)
    if with_wind:

        def one_wind(t, carry):
            base = pl.multiple_of((levels + t * 8) * x_size, 8 * x_size)
            edges = None
            for x in range(x_size):
                edges = pack_edges(edges, wind[pl.ds(base + x, 8, stride=x_size), :], x)
            packed[pl.ds(pl.multiple_of(rows + t * 8, 8), 8), :] = edges
            return carry

        lax.fori_loop(0, levels // 8, one_wind, 0, unroll=4)


def join_packs(even, from_a, from_b):
    south = jnp.where(even, from_b, from_a)
    north = jnp.where(even, from_a, from_b)
    return jnp.where((lane_index(south.shape) & (GROUP - 1)) < WIDTH, south, north)


def wind_kernel(x_size, rows, odd, wind, factor, from_a, from_b, pack_a, pack_b, *outs):
    speed_x, ahead_y, behind_y, edge_ahead, edge_behind, scales = outs
    levels = speed_x.shape[1]
    even_x, even_y = odd[0] == 0, odd[1] == 0
    for x in range(x_size):
        mapped = factor[pl.ds(x, 1), :]
        for k, divisor in enumerate(DIVISORS):
            scales[k, x] = jnp.broadcast_to(mapped * mapped * (-1.0 / divisor), scales.shape[2:])

    def one(t, carry):
        base = pl.multiple_of(t * 8 * x_size, 8 * x_size)
        at = pl.ds(pl.multiple_of(t * 8, 8), 8)
        there = pl.ds(pl.multiple_of(WIDTH * rows + t * 8, 8), 8)
        before = jnp.where(even_x, from_b[there, :], from_a[there, :])
        east = jnp.where(even_x, from_a[there, :], from_b[there, :])
        for x in range(x_size + 1):
            now = east if x == x_size else wind[pl.ds(base + x, 8, stride=x_size), :]
            speed_x[x, at, :] = face_scale * (before + now)
            before = now
        base = base + levels * x_size
        lane = lane_index(before.shape)
        there = pl.ds(pl.multiple_of(rows + t * 8, 8), 8)
        halo = join_packs(even_y, pack_a[there, :], pack_b[there, :])
        forward, backward = None, None
        for x in range(x_size):
            row = wind[pl.ds(base + x, 8, stride=x_size), :]
            edge = rolled(halo, -(GROUP * x + WIDTH))
            front = face_scale * (row + ahead(row, edge, lane, 1))
            back = face_scale * (row + ahead(row, edge, lane, -1))
            ahead_y[x, at, :] = front
            behind_y[x, at, :] = back
            forward = pack_edges(forward, front, x)
            backward = pack_edges(backward, back, x)
        edge_ahead[at, :] = forward
        edge_behind[at, :] = backward
        return carry

    lax.fori_loop(0, levels // 8, one, 0, unroll=UNROLL)


def stencil_matrices(y_size):
    inner = np.zeros((y_size, 4 * y_size), np.float32)
    edges = np.zeros((y_size, 4 * y_size), np.float32)
    for part, (taps, offset) in enumerate(((HIGH, -2), (DAMP, -2), (HIGH, -3), (DAMP, -3))):
        for n, tap in enumerate(taps):
            k = n + offset
            for j in range(y_size):
                if 0 <= j + k < y_size:
                    inner[j + k, part * y_size + j] = tap
            for g in range(0, y_size, GROUP):
                for j in range(WIDTH):
                    if j + k < 0:
                        edges[g + WIDTH + j + k, part * y_size + g + WIDTH + j] = tap
                    if j - WIDTH + k >= 0:
                        edges[g + j + k, part * y_size + g + j] = tap
    return [jnp.asarray(np.concatenate([m, m]).astype(ml_dtypes.bfloat16)) for m in (inner, edges)]


def split_halves(values):
    leading = values.astype(jnp.bfloat16)
    trailing = (values - leading.astype(jnp.float32)).astype(jnp.bfloat16)
    return jnp.concatenate([leading, trailing], axis=1)


def stencil_product(halves, matrix, columns=slice(None)):
    return jnp.dot(halves, matrix[:, columns], preferred_element_type=jnp.float32)


def section_kernel(x_size, k, chunk, last, with_city, odd, *refs):
    refs = list(refs)
    first = k == 0
    section = refs.pop(0)
    base_ref = section if first else refs.pop(0)
    from_a, from_b, pack_a, pack_b = [refs.pop(0) for _ in range(4)]
    speed_x, ahead_y, behind_y, edge_ahead, edge_behind, scales = [refs.pop(0) for _ in range(6)]
    inner_matrix, edge_matrix = [refs.pop(0) for _ in range(2)]
    parts = refs[-4:]
    share = refs[-5]
    refs = refs[:-5]
    if last:
        if with_city:
            city = [refs.pop(0) for _ in range(6)]
            out, wall_out, indoor_out = refs
        else:
            refs.pop(0)
            (out,) = refs
    else:
        out, to_a, to_b, packed = refs
    levels, y_size = edge_ahead.shape
    chunk_rows = base_ref.shape[0] // (CHUNKS * x_size)
    even_x, even_y = odd[0] == 0, odd[1] == 0

    def block(g, carry):
        corner = pl.multiple_of((chunk * chunk_rows + g * levels) * x_size, levels * x_size)
        here = pl.multiple_of(g * levels, levels)
        for p in range(levels * x_size // PIECE):
            if first:
                values = section[pl.ds(pl.multiple_of(corner + p * PIECE, PIECE), PIECE), :]
            else:
                n = PIECE // levels
                values = section[p * n : (p + 1) * n, pl.ds(here, levels), :].reshape(PIECE, y_size)
            halves = split_halves(values)
            for pair in range(2):
                product = stencil_product(halves, inner_matrix, slice(2 * pair * y_size, 2 * (pair + 1) * y_size))
                for j, part in enumerate(parts[2 * pair : 2 * pair + 2]):
                    part[p * PIECE : (p + 1) * PIECE, :] = product[:, j * y_size : (j + 1) * y_size]
        halo = join_packs(even_y, pack_a[pl.ds(here, levels), :], pack_b[pl.ds(here, levels), :])
        product = stencil_product(split_halves(halo), edge_matrix)
        after, before = edge_ahead[...], edge_behind[...]
        share[...] = (
            after * product[:, :y_size]
            - jnp.abs(after) * product[:, y_size : 2 * y_size]
            - before * product[:, 2 * y_size : 3 * y_size]
            + jnp.abs(before) * product[:, 3 * y_size :]
        )

        def one(t, carry):
            at = pl.ds(pl.multiple_of(t * 8, 8), 8)
            rows_at = pl.ds(pl.multiple_of(here + t * 8, 8), 8)
            start = pl.multiple_of(corner + t * 8 * x_size, 8 * x_size)

            def halo_rows(mine, other, j):
                edge_at = pl.ds(pl.multiple_of(j * chunk_rows + here + t * 8, 8), 8)
                return jnp.where(even_x, mine[edge_at, :], other[edge_at, :])

            def cell(x):
                if x < 0:
                    return halo_rows(from_b, from_a, x + WIDTH)
                if x >= x_size:
                    return halo_rows(from_a, from_b, x - x_size)
                return section[pl.ds(start + x, 8, stride=x_size), :] if first else section[x, rows_at, :]

            lane = lane_index((8, y_size))
            edge_lane = (lane < WIDTH) | (lane >= y_size - WIDTH)
            edge_share = share[at, :]
            q = [cell(x) for x in range(-3, 2)]
            d1 = [q[i + 1] - q[i] for i in range(4)]
            d2 = [d1[i + 1] - d1[i] for i in range(3)]
            d3 = [d2[i + 1] - d2[i] for i in range(2)]
            d4 = d3[1] - d3[0]
            smooth = d4 - 5.0 * d2[1] + 30.0 * q[2]
            q, d1, d2, d3 = q[3:], d1[-1], d2[-1], d3[-1]
            flux_before = None
            edges, lows = None, []
            for x in range(-1, x_size):
                q.append(cell(x + WIDTH))
                new1 = q[-1] - q[-2]
                new2 = new1 - d1
                new3 = new2 - d2
                new4 = new3 - d3
                new_smooth = new4 - 5.0 * d2 + 30.0 * q[0]
                speed = speed_x[x + 1, at, :]
                flux = speed * (smooth + new_smooth) - jnp.abs(speed) * (new4 - d4)
                d1, d2, d3, d4, smooth = new1, new2, new3, new4, new_smooth
                if x >= 0:
                    if first:
                        lines = [part[pl.ds(t * 8 * x_size + x, 8, stride=x_size), :] for part in parts]
                    else:
                        lines = [part[pl.ds(pl.multiple_of(x * levels + t * 8, 8), 8), :] for part in parts]
                    after, before = ahead_y[x, at, :], behind_y[x, at, :]
                    moved = rolled(edge_share, -(GROUP * x + WIDTH))
                    divergence = (
                        (flux - flux_before)
                        + (after * lines[0] - jnp.abs(after) * lines[1])
                        - (before * lines[2] - jnp.abs(before) * lines[3])
                        + jnp.where(edge_lane, moved, 0.0)
                    )
                    base = base_ref[pl.ds(start + x, 8, stride=x_size), :]
                    new = base + scales[k, x] * divergence
                    if last:
                        out[pl.ds(pl.multiple_of(t * 8 * x_size, 8 * x_size) + x, 8, stride=x_size), :] = new
                    else:
                        out[x, rows_at, :] = new
                        edges = pack_edges(edges, new, x)
                        if x < WIDTH:
                            lows.append(new)
                        if x >= x_size - WIDTH:
                            j = x - x_size + WIDTH
                            edge_at = pl.ds(pl.multiple_of(j * chunk_rows + here + t * 8, 8), 8)
                            to_a[edge_at, :] = jnp.where(even_x, new, lows[j])
                            to_b[edge_at, :] = jnp.where(even_x, lows[j], new)
                flux_before = flux
                q = q[1:]
            if not last:
                packed[rows_at, :] = edges
            return carry

        lax.fori_loop(0, levels // 8, one, 0, unroll=UNROLL)
        return carry

    if last:
        block(pl.program_id(0), 0)
    else:
        lax.fori_loop(0, chunk_rows // levels, block, 0)
    if last and with_city:

        @pl.when(pl.program_id(0) == 0)
        def _():
            city_step(x_size, out, *city, wall_out, indoor_out)


def dot(a, b, dims):
    return lax.dot_general(
        a, b, (dims, ((), ())), precision=lax.Precision.HIGHEST, preferred_element_type=jnp.float32
    )


def city_step(x_size, out, counts, cols_ref, class_ref, table, wall_ref, indoor_ref, wall_out, indoor_out):
    deep = 16
    cols = cols_ref[...]
    slots = cols.shape[1]
    y_size = out.shape[1]
    cell_x = lax.div(cols, y_size)
    cell_y = lax.rem(cols, y_size)
    lower = [
        jnp.concatenate([out[pl.ds(8 * x_size * t + x, 8, stride=x_size), :] for t in range(deep // 8)], axis=0)
        for x in range(x_size)
    ]
    at_y = (lax.broadcasted_iota(jnp.int32, (y_size, slots), 0) == cell_y).astype(jnp.float32)
    gathered = dot(jnp.concatenate(lower, axis=0), at_y, ((1,), (0,)))
    air = jnp.zeros((deep, slots), jnp.float32)
    for x in range(x_size):
        air = jnp.where(cell_x == x, gathered[deep * x : deep * (x + 1)], air)
    air = air[:UL]
    onehot = (lax.broadcasted_iota(jnp.int32, (NCLS, slots), 0) == class_ref[...]).astype(jnp.float32)
    areas = dot(table[...], onehot, ((0,), (0,)))
    walls = wall_ref[...]
    indoor = indoor_ref[...]
    heat = heat_coef * areas * (walls[0:1] - air)
    wall_first = walls[0:1] - wall_coef * jnp.sum(heat, axis=0, keepdims=True) + conduct * (walls[1:2] - walls[0:1])
    middle = walls[1:-1] + conduct * (walls[:-2] - 2.0 * walls[1:-1] + walls[2:])
    last = walls[-1:] + conduct * (walls[-2:-1] - walls[-1:]) + inner_coef * (indoor - walls[-1:])
    indoor_new = indoor + room_coef * (walls[-1:] - indoor)
    live = lax.broadcasted_iota(jnp.int32, (1, slots), 1) < counts[0]
    wall_out[...] = jnp.where(live, jnp.concatenate([wall_first, middle, last], axis=0), walls)
    indoor_out[...] = jnp.where(live, indoor_new, indoor)
    heating = jnp.where(live, flux_coef * heat, 0.0)
    heating = jnp.concatenate([heating, jnp.zeros((deep - UL, slots), jnp.float32)], axis=0)
    spread = jnp.concatenate([jnp.where(cell_x == x, heating, 0.0) for x in range(x_size)], axis=0)
    added = dot(spread, at_y, ((1,), (1,)))
    for x in range(x_size):
        for t in range(deep // 8):
            out[pl.ds(8 * x_size * t + x, 8, stride=x_size), :] = (
                lower[x][8 * t : 8 * t + 8] + added[deep * x + 8 * t : deep * x + 8 * t + 8]
            )


def exchange(axis, to_a, to_b):
    size = lax.axis_size(axis)
    pairs_a = [(i, i + 1) for i in range(0, size, 2)]
    pairs_b = [(i, (i + 1) % size) for i in range(1, size, 2)]
    both = [pairs + [(j, i) for i, j in pairs] for pairs in (pairs_a, pairs_b)]
    return lax.ppermute(to_a, axis, both[0]), lax.ppermute(to_b, axis, both[1])


def per_device(
    scalars,
    winds,
    map_factor,
    urban_counts,
    urban_cols,
    street_class,
    area_table,
    wall_temp,
    indoor_temp,
):
    n_scalars, levels, x_size, y_size = scalars.shape
    slots = urban_cols.shape[0]
    rows = n_scalars * levels // CHUNKS
    f32 = functools.partial(jax.ShapeDtypeStruct, dtype=jnp.float32)
    field = scalars.reshape(n_scalars * levels * x_size, y_size)
    wind = winds.reshape(2 * levels * x_size, y_size)
    params = pltpu.CompilerParams(vmem_limit_bytes=40 * 2**20)
    whole = pl.BlockSpec(memory_space=pltpu.VMEM)

    smem = pl.BlockSpec(memory_space=pltpu.SMEM)
    hbm = pl.BlockSpec(memory_space=pltpu.HBM)
    odd = jnp.stack([lax.axis_index("gx") % 2, lax.axis_index("gy") % 2]).astype(jnp.int32)
    cheap = pl.CostEstimate(flops=1000, bytes_accessed=1000, transcendentals=0)

    pieces = 4
    first_rows = pl.pallas_call(
        functools.partial(first_rows_kernel, x_size, rows, levels, pieces),
        in_specs=[smem, hbm, hbm],
        out_specs=[whole] * 2,
        out_shape=[f32((WIDTH * rows + levels, y_size))] * 2,
        scratch_shapes=[
            pltpu.VMEM((rows * x_size, y_size), jnp.float32),
            pltpu.VMEM((levels * x_size, y_size), jnp.float32),
            pltpu.SemaphoreType.DMA((pieces + 1,)),
        ],
        compiler_params=pltpu.CompilerParams(vmem_limit_bytes=62 * 2**20),
        cost_estimate=cheap,
        name="first_rows",
    )(odd, field, wind)
    received = [None] * CHUNKS
    received[0] = exchange("gx", *first_rows)
    for c in range(CHUNKS):
        extra = levels if c == 0 else 0
        outs = pl.pallas_call(
            functools.partial(extract_kernel, x_size, c, c == 0),
            in_specs=[smem, whole] + [whole] * (c == 0),
            out_specs=[whole] * (1 if c == 0 else 3),
            out_shape=[f32((WIDTH * rows, y_size))] * (0 if c == 0 else 2) + [f32((rows + extra, y_size))],
            compiler_params=params,
            cost_estimate=cheap,
            name=f"extract_{c}",
        )(odd, field, *([wind] if c == 0 else []))
        if c > 0:
            received[c] = exchange("gx", *outs[:2])
        received[c] = (*received[c], *exchange("gy", outs[-1], outs[-1]))

    speeds = pl.pallas_call(
        functools.partial(wind_kernel, x_size, rows),
        in_specs=[smem] + [whole] * 6,
        out_specs=[whole] * 6,
        out_shape=[
            f32((x_size + 1, levels, y_size)),
            f32((x_size, levels, y_size)),
            f32((x_size, levels, y_size)),
            f32((levels, y_size)),
            f32((levels, y_size)),
            f32((len(DIVISORS), x_size, 8, y_size)),
        ],
        compiler_params=params,
        cost_estimate=cheap,
        name="speeds",
    )(odd, wind, map_factor, *received[0])
    matrices = stencil_matrices(y_size)

    steps = rows // levels
    sections = [None] * CHUNKS
    result = None
    for k in range(len(DIVISORS)):
        last = k == len(DIVISORS) - 1
        for c in range(CHUNKS):
            operands = [odd] + ([field] if k == 0 else [sections[c], field])
            operands += [*received[c], *speeds, *matrices]
            specs = [smem] + [whole] * (len(operands) - 1)
            city = last and c == 0
            aliases = {}
            flat_c = pl.BlockSpec((levels * x_size, y_size), lambda g, c=c: (c * steps + g, 0))
            if city:
                operands += [
                    urban_counts,
                    urban_cols[None],
                    street_class[None],
                    area_table,
                    wall_temp,
                    indoor_temp[None],
                ]
                specs += [smem] + [whole] * 5
                out_specs = [flat_c, whole, whole]
                out_shape = [f32(field.shape), f32(wall_temp.shape), f32((1, slots))]
            elif last:
                aliases = {len(operands): 0}
                operands += [result]
                specs += [pl.BlockSpec(memory_space=pl.ANY)]
                out_specs = [flat_c]
                out_shape = [f32(field.shape)]
            else:
                out_specs = [whole] * 4
                out_shape = [
                    f32((x_size, rows, y_size)),
                    f32((WIDTH * rows, y_size)),
                    f32((WIDTH * rows, y_size)),
                    f32((rows, y_size)),
                ]
            outs = pl.pallas_call(
                functools.partial(section_kernel, x_size, k, c, last, city),
                grid=(steps,) if last else (),
                in_specs=specs,
                out_specs=out_specs,
                out_shape=out_shape,
                scratch_shapes=[pltpu.VMEM((levels, y_size), jnp.float32)]
                + [pltpu.VMEM((levels * x_size, y_size), jnp.float32)] * 4,
                input_output_aliases=aliases,
                compiler_params=params,
                cost_estimate=cheap,
                name=f"section_{k}_{c}",
            )(*operands)
            if city:
                result, wall_out, indoor_out = outs
            elif last:
                (result,) = outs
            else:
                sections[c], *outgoing, packed = outs
                received[c] = (*exchange("gx", *outgoing), *exchange("gy", packed, packed))
    return (result.reshape(scalars.shape), wall_out, indoor_out[0])


def solution(mesh):
    in_specs = (
        P(None, None, "gx", "gy"),
        P(None, None, "gx", "gy"),
        P("gx", "gy"),
        P(("gx", "gy")),
        P(("gx", "gy")),
        P(("gx", "gy")),
        P(),
        P(None, ("gx", "gy")),
        P(("gx", "gy")),
    )
    out_specs = (P(None, None, "gx", "gy"), P(None, ("gx", "gy")), P(("gx", "gy")))
    return jax.shard_map(
        per_device, mesh=mesh, in_specs=in_specs, out_specs=out_specs, check_vma=False
    )
```

profile of v0, /device:TPU:0, one launch (start us, length us, event | category | flops | bytes accessed | tf_op | source)
XLA Modules:
  0.0 70.3 jit_solution(14758218273697658414)
XLA Ops:
  0.7 0.6 pad_add_fusion.odd
  1.3 3.0 %first_rows.1 = (f32[448,128]{1,0:T(8,128)}, f32[448,128]{1,0:T(8,128)}) custom-call(s32[2]{0:T(128)} %pad_add_fusion.odd, f32[4096,128]{1,0:T(8,128)} %bitcast.9, f32[2048,128]{1,0:T(8,128)} %bitcast.18), custom_call_target="tpu_custom_call" | custom-call | flops 1000 | bytes 1000 | tf_op jit(solution)/shard_map/first_rows/pallas_call | solution.py:408
  4.3 3.1 %collective-permute-start.4 = (f32[448,128]{1,0:T(8,128)}, f32[448,128]{1,0:T(8,128)S(1)}, u32[]{:S(2)}, u32[]{:S(2)}) collective-permute-start(f32[448,128]{1,0:T(8,128)} %get-tuple-element.36), channel_id=1, source_target_pairs={{0,8},{16,24},{8,0},{24,16},{1,9},{17,25},{9,1},{25,17},{2,10},{18... | collective-permute-start | bytes 688136 | tf_op jit(solution)/shard_map/ppermute | solution.py:379
  7.4 2.5 %collective-permute-start.5 = (f32[448,128]{1,0:T(8,128)}, f32[448,128]{1,0:T(8,128)S(1)}, u32[]{:S(2)}, u32[]{:S(2)}) collective-permute-start(f32[448,128]{1,0:T(8,128)} %get-tuple-element.37), channel_id=1, source_target_pairs={{8,16},{24,0},{16,8},{0,24},{9,17},{25,1},{17,9},{1,25},{10,18},{2... | collective-permute-start | bytes 688136 | tf_op jit(solution)/shard_map/ppermute | solution.py:379
  9.9 1.6 %copy-done = f32[4,64,16,128]{3,2,1,0:T(8,128)S(1)} copy-done((f32[4,64,16,128]{3,2,1,0:T(8,128)S(1)}, f32[4,64,16,128]{3,2,1,0:T(8,128)}, u32[]{:S(2)}) %copy-start) | copy-done | bytes 2097176
  11.5 1.4 %extract_0.1 = f32[192,128]{1,0:T(8,128)S(1)} custom-call(s32[2]{0:T(128)S(1)} %copy-done.5, f32[4096,128]{1,0:T(8,128)S(1)} %bitcast.10, f32[2048,128]{1,0:T(8,128)S(1)} %bitcast.19), custom_call_target="tpu_custom_call" | custom-call | flops 1000 | bytes 1000 | tf_op jit(solution)/shard_map/extract_0/pallas_call | solution.py:426
  12.9 1.4 %collective-permute-start.7 = (f32[192,128]{1,0:T(8,128)S(1)}, f32[192,128]{1,0:T(8,128)S(1)}, u32[]{:S(2)}, u32[]{:S(2)}) collective-permute-start(f32[192,128]{1,0:T(8,128)S(1)} %extract_0.1), channel_id=1, source_target_pairs={{1,2},{3,4},{5,6},{7,0},{2,1},{4,3},{6,5},{0,7},{9,10},{11,12},{13... | collective-permute-start | bytes 294920 | tf_op jit(solution)/shard_map/ppermute | solution.py:379
  14.6 1.1 %extract_1.1 = (f32[384,128]{1,0:T(8,128)S(1)}, f32[384,128]{1,0:T(8,128)S(1)}, f32[128,128]{1,0:T(8,128)S(1)}) custom-call(s32[2]{0:T(128)S(1)} %copy-done.5, f32[4096,128]{1,0:T(8,128)S(1)} %bitcast.11), custom_call_target="tpu_custom_call" | custom-call | flops 1000 | bytes 1000 | tf_op jit(solution)/shard_map/extract_1/pallas_call | solution.py:426
  15.7 0.7 %collective-permute-start = (f32[384,128]{1,0:T(8,128)S(1)}, f32[384,128]{1,0:T(8,128)S(1)}, u32[]{:S(2)}, u32[]{:S(2)}) collective-permute-start(f32[384,128]{1,0:T(8,128)S(1)} %get-tuple-element.33), channel_id=1, source_target_pairs={{0,8},{16,24},{8,0},{24,16},{1,9},{17,25},{9,1},{25,17},{2,10},{18... | collective-permute-start | bytes 589832 | tf_op jit(solution)/shard_map/ppermute | solution.py:379
  16.4 2.4 %collective-permute-done.7.pack_b.refs_4_ = f32[192,128]{1,0:T(8,128)S(1)} collective-permute-done((f32[192,128]{1,0:T(8,128)S(1)}, f32[192,128]{1,0:T(8,128)S(1)}, u32[]{:S(2)}, u32[]{:S(2)}) %collective-permute-start.7) | collective-permute-done | bytes 98336 | tf_op jit(solution)/shard_map/ppermute | solution.py:379
  18.9 1.3 %collective-permute-start.1 = (f32[384,128]{1,0:T(8,128)S(1)}, f32[384,128]{1,0:T(8,128)S(1)}, u32[]{:S(2)}, u32[]{:S(2)}) collective-permute-start(f32[384,128]{1,0:T(8,128)S(1)} %get-tuple-element.34), channel_id=1, source_target_pairs={{8,16},{24,0},{16,8},{0,24},{9,17},{25,1},{17,9},{1,25},{10,18},{2... | collective-permute-start | bytes 589832 | tf_op jit(solution)/shard_map/ppermute | solution.py:379
  20.2 1.0 %collective-permute-start.3 = (f32[128,128]{1,0:T(8,128)S(1)}, f32[128,128]{1,0:T(8,128)S(1)}, u32[]{:S(2)}, u32[]{:S(2)}) collective-permute-start(f32[128,128]{1,0:T(8,128)S(1)} %get-tuple-element.35), channel_id=1, source_target_pairs={{1,2},{3,4},{5,6},{7,0},{2,1},{4,3},{6,5},{0,7},{9,10},{11,12},{13... | collective-permute-start | bytes 196616 | tf_op jit(solution)/shard_map/ppermute | solution.py:379
  21.5 1.7 %speeds.1 = (f32[17,64,128]{2,1,0:T(8,128)S(1)}, f32[16,64,128]{2,1,0:T(8,128)S(1)}, f32[16,64,128]{2,1,0:T(8,128)S(1)}, f32[64,128]{1,0:T(8,128)S(1)}, f32[64,1...) custom-call(s32[2]{0:T(128)S(1)} %copy-done.5, f32[2048,128]{1,0:T(8,128)S(1)} %bitcast.20, f32[16,128]{1,0:T(8,128)S(1)} %copy-done.7, ...), custom_call_target="tpu_custom_call" | custom-call | flops 1000 | bytes 1000 | tf_op jit(solution)/shard_map/speeds/pallas_call | solution.py:439
  23.2 4.8 %section_0_0.1 = (f32[16,128,128]{2,1,0:T(8,128)S(1)}, f32[384,128]{1,0:T(8,128)S(1)}, f32[384,128]{1,0:T(8,128)S(1)}, f32[128,128]{1,0:T(8,128)S(1)}) custom-call(s32[2]{0:T(128)S(1)} %copy-done.5, f32[4096,128]{1,0:T(8,128)S(1)} %bitcast.12, f32[448,128]{1,0:T(8,128)S(1)} %collective-permute-done.4.from_a.refs_1_, ...), custom_call_target="tpu_custom_call" | custom-call | flops 1000 | bytes 1000 | tf_op jit(solution)/shard_map/section_0_0/pallas_call | solution.py:495
  28.1 3.3 %collective-permute-start.17 = (f32[384,128]{1,0:T(8,128)S(1)}, f32[384,128]{1,0:T(8,128)S(1)}, u32[]{:S(2)}, u32[]{:S(2)}) collective-permute-start(f32[384,128]{1,0:T(8,128)S(1)} %get-tuple-element.54), channel_id=1, source_target_pairs={{8,16},{24,0},{16,8},{0,24},{9,17},{25,1},{17,9},{1,25},{10,18},{2... | collective-permute-start | bytes 589832 | tf_op jit(solution)/shard_map/ppermute | solution.py:379
  31.7 4.8 %section_0_1.1 = (f32[16,128,128]{2,1,0:T(8,128)S(1)}, f32[384,128]{1,0:T(8,128)S(1)}, f32[384,128]{1,0:T(8,128)S(1)}, f32[128,128]{1,0:T(8,128)S(1)}) custom-call(s32[2]{0:T(128)S(1)} %copy-done.5, f32[4096,128]{1,0:T(8,128)S(1)} %bitcast.13, f32[384,128]{1,0:T(8,128)S(1)} %collective-permute-done.refs_1_, f32[384,128]{1,0:T(8,128)S(1)} %collective-permute-done.1.refs_2_, ...), custom_call_target="tpu_custom_call" | custom-call | flops 1000 | bytes 1000 | tf_op jit(solution)/shard_map/section_0_1/pallas_call | solution.py:495
  36.5 0.8 %collective-permute-start.8 = (f32[384,128]{1,0:T(8,128)S(1)}, f32[384,128]{1,0:T(8,128)S(1)}, u32[]{:S(2)}, u32[]{:S(2)}) collective-permute-start(f32[384,128]{1,0:T(8,128)S(1)} %get-tuple-element.45), channel_id=1, source_target_pairs={{0,8},{16,24},{8,0},{24,16},{1,9},{17,25},{9,1},{25,17},{2,10},{18... | collective-permute-start | bytes 589832 | tf_op jit(solution)/shard_map/ppermute | solution.py:379
  37.3 1.4 %collective-permute-start.9 = (f32[384,128]{1,0:T(8,128)S(1)}, f32[384,128]{1,0:T(8,128)S(1)}, u32[]{:S(2)}, u32[]{:S(2)}) collective-permute-start(f32[384,128]{1,0:T(8,128)S(1)} %get-tuple-element.46), channel_id=1, source_target_pairs={{8,16},{24,0},{16,8},{0,24},{9,17},{25,1},{17,9},{1,25},{10,18},{2... | collective-permute-start | bytes 589832 | tf_op jit(solution)/shard_map/ppermute | solution.py:379
  38.9 1.0 %collective-permute-done.18.refs_4_ = f32[128,128]{1,0:T(8,128)S(1)} collective-permute-done((f32[128,128]{1,0:T(8,128)S(1)}, f32[128,128]{1,0:T(8,128)S(1)}, u32[]{:S(2)}, u32[]{:S(2)}) %collective-permute-start.18) | collective-permute-done | bytes 65568 | tf_op jit(solution)/shard_map/ppermute | solution.py:379
  39.9 1.4 %collective-permute-start.11 = (f32[128,128]{1,0:T(8,128)S(1)}, f32[128,128]{1,0:T(8,128)S(1)}, u32[]{:S(2)}, u32[]{:S(2)}) collective-permute-start(f32[128,128]{1,0:T(8,128)S(1)} %get-tuple-element.47), channel_id=1, source_target_pairs={{1,2},{3,4},{5,6},{7,0},{2,1},{4,3},{6,5},{0,7},{9,10},{11,12},{13... | collective-permute-start | bytes 196616 | tf_op jit(solution)/shard_map/ppermute | solution.py:379
  41.4 3.6 %section_1_0.1 = (f32[16,128,128]{2,1,0:T(8,128)S(1)}, f32[384,128]{1,0:T(8,128)S(1)}, f32[384,128]{1,0:T(8,128)S(1)}, f32[128,128]{1,0:T(8,128)S(1)}) custom-call(s32[2]{0:T(128)S(1)} %copy-done.5, f32[16,128,128]{2,1,0:T(8,128)S(1)} %get-tuple-element.52.refs_0_, f32[4096,128]{1,0:T(8,128)S(1)} %bitcast.14, ...), custom_call_target="tpu_custom_call" | custom-call | flops 1000 | bytes 1000 | tf_op jit(solution)/shard_map/section_1_0/pallas_call | solution.py:495
  45.0 0.6 collective-permute-start.20
  45.5 2.6 %collective-permute-start.21 = (f32[384,128]{1,0:T(8,128)S(1)}, f32[384,128]{1,0:T(8,128)S(1)}, u32[]{:S(2)}, u32[]{:S(2)}) collective-permute-start(f32[384,128]{1,0:T(8,128)S(1)} %get-tuple-element.58), channel_id=1, source_target_pairs={{8,16},{24,0},{16,8},{0,24},{9,17},{25,1},{17,9},{1,25},{10,18},{2... | collective-permute-start | bytes 589832 | tf_op jit(solution)/shard_map/ppermute | solution.py:379
  48.2 0.6 collective-permute-start.23
  48.8 3.6 %section_1_1.1 = (f32[16,128,128]{2,1,0:T(8,128)S(1)}, f32[384,128]{1,0:T(8,128)S(1)}, f32[384,128]{1,0:T(8,128)S(1)}, f32[128,128]{1,0:T(8,128)S(1)}) custom-call(s32[2]{0:T(128)S(1)} %copy-done.5, f32[16,128,128]{2,1,0:T(8,128)S(1)} %get-tuple-element.44.refs_0_, f32[4096,128]{1,0:T(8,128)S(1)} %bitcast.15, f32[384,128]{1,0:T(8,128)S(1)} %collective-permute-done.8.refs_2_, ...), custom_call_target="tpu_custom_call" | custom-call | flops 1000 | bytes 1000 | tf_op jit(solution)/shard_map/section_1_1/pallas_call | solution.py:495
  52.4 1.8 %collective-permute-start.12 = (f32[384,128]{1,0:T(8,128)S(1)}, f32[384,128]{1,0:T(8,128)S(1)}, u32[]{:S(2)}, u32[]{:S(2)}) collective-permute-start(f32[384,128]{1,0:T(8,128)S(1)} %get-tuple-element.49), channel_id=1, source_target_pairs={{0,8},{16,24},{8,0},{24,16},{1,9},{17,25},{9,1},{25,17},{2,10},{18... | collective-permute-start | bytes 589832 | tf_op jit(solution)/shard_map/ppermute | solution.py:379
  54.2 1.4 %collective-permute-start.13 = (f32[384,128]{1,0:T(8,128)S(1)}, f32[384,128]{1,0:T(8,128)S(1)}, u32[]{:S(2)}, u32[]{:S(2)}) collective-permute-start(f32[384,128]{1,0:T(8,128)S(1)} %get-tuple-element.50), channel_id=1, source_target_pairs={{8,16},{24,0},{16,8},{0,24},{9,17},{25,1},{17,9},{1,25},{10,18},{2... | collective-permute-start | bytes 589832 | tf_op jit(solution)/shard_map/ppermute | solution.py:379
  55.6 1.3 %collective-permute-done.22.refs_4_ = f32[128,128]{1,0:T(8,128)S(1)} collective-permute-done((f32[128,128]{1,0:T(8,128)S(1)}, f32[128,128]{1,0:T(8,128)S(1)}, u32[]{:S(2)}, u32[]{:S(2)}) %collective-permute-start.22) | collective-permute-done | bytes 65568 | tf_op jit(solution)/shard_map/ppermute | solution.py:379
  56.9 1.3 %collective-permute-start.15 = (f32[128,128]{1,0:T(8,128)S(1)}, f32[128,128]{1,0:T(8,128)S(1)}, u32[]{:S(2)}, u32[]{:S(2)}) collective-permute-start(f32[128,128]{1,0:T(8,128)S(1)} %get-tuple-element.51), channel_id=1, source_target_pairs={{1,2},{3,4},{5,6},{7,0},{2,1},{4,3},{6,5},{0,7},{9,10},{11,12},{13... | collective-permute-start | bytes 196616 | tf_op jit(solution)/shard_map/ppermute | solution.py:379
  58.9 5.2 %section_2_0.1 = (f32[4096,128]{1,0:T(8,128)}, f32[10,256]{1,0:T(8,128)}, f32[1,256]{1,0:T(1,128)}) custom-call(s32[2]{0:T(128)S(1)} %copy-done.5, f32[16,128,128]{2,1,0:T(8,128)S(1)} %get-tuple-element.56.refs_0_, f32[4096,128]{1,0:T(8,128)S(1)} %bitcast.16, f32[384,128]{1,0:T(8,128)S(1)} %collective-permute-done.20.refs_2_, ...), custom_call_target="tpu_custom_call" | custom-call | flops 1000 | bytes 1000 | tf_op jit(solution)/shard_map/section_2_0/pallas_call | solution.py:495
  64.1 2.1 %collective-permute-done.13.refs_3_ = f32[384,128]{1,0:T(8,128)S(1)} collective-permute-done((f32[384,128]{1,0:T(8,128)S(1)}, f32[384,128]{1,0:T(8,128)S(1)}, u32[]{:S(2)}, u32[]{:S(2)}) %collective-permute-start.13) | collective-permute-done | bytes 196640 | tf_op jit(solution)/shard_map/ppermute | solution.py:379
  66.2 4.1 %section_2_1.1 = f32[4096,128]{1,0:T(8,128)} custom-call(s32[2]{0:T(128)S(1)} %copy-done.5, f32[16,128,128]{2,1,0:T(8,128)S(1)} %get-tuple-element.48.refs_0_, f32[4096,128]{1,0:T(8,128)S(1)} %bitcast.17, f32[384,128]{1,0:T(8,128)S(1)} %collective-permute-done.12.refs_2_, ...), custom_call_target="tpu_custom_call", output_to_operand_aliasing={{}: (15, {})} | custom-call | flops 1000 | bytes 1000 | tf_op jit(solution)/shard_map/section_2_1/pallas_call | solution.py:495
  (51 shorter events, 1.4 us)
Async XLA Ops:
  4.3 16.9 %collective-permute-start.4 = (f32[448,128]{1,0:T(8,128)}, f32[448,128]{1,0:T(8,128)S(1)}, u32[]{:S(2)}, u32[]{:S(2)}) collective-permute-start(f32[448,128]{1,0:T(8,128)} %get-tuple-element.36), channel_id=1, source_target_pairs={{0,8},{16,24},{8,0},{24,16},{1,9},{17,25},{9,1},{25,17},{2,10},{18... | collective-permute-start | bytes 688136 | tf_op jit(solution)/shard_map/ppermute | solution.py:379
  7.4 14.1 %collective-permute-start.5 = (f32[448,128]{1,0:T(8,128)}, f32[448,128]{1,0:T(8,128)S(1)}, u32[]{:S(2)}, u32[]{:S(2)}) collective-permute-start(f32[448,128]{1,0:T(8,128)} %get-tuple-element.37), channel_id=1, source_target_pairs={{8,16},{24,0},{16,8},{0,24},{9,17},{25,1},{17,9},{1,25},{10,18},{2... | collective-permute-start | bytes 688136 | tf_op jit(solution)/shard_map/ppermute | solution.py:379
  11.5 10.0 %copy-start.7 = (f32[16,128]{1,0:T(8,128)S(1)}, f32[16,128]{1,0:T(8,128)}, u32[]{:S(2)}) copy-start(f32[16,128]{1,0:T(8,128)} %factor.1) | copy-start | bytes 24580
  12.9 10.3 %copy-start.1 = (f32[4,64,16,128]{3,2,1,0:T(8,128)S(1)}, f32[4,64,16,128]{3,2,1,0:T(8,128)}, u32[]{:S(2)}) copy-start(f32[4,64,16,128]{3,2,1,0:T(8,128)} %param.11) | copy-start | bytes 6291460
  12.9 10.3 %copy-start.3 = (bf16[256,512]{1,0:T(8,128)(2,1)S(1)}, bf16[256,512]{1,0:T(8,128)(2,1)}, u32[]{:S(2)}) copy-start(bf16[256,512]{1,0:T(8,128)(2,1)} %constant.30.clone.refs_12_.refs_13_) | copy-start | bytes 786436
  12.9 10.3 %copy-start.4 = (bf16[256,512]{1,0:T(8,128)(2,1)S(1)}, bf16[256,512]{1,0:T(8,128)(2,1)}, u32[]{:S(2)}) copy-start(bf16[256,512]{1,0:T(8,128)(2,1)} %constant.29.clone.refs_11_.refs_12_) | copy-start | bytes 786436
  12.9 6.0 %collective-permute-start.7 = (f32[192,128]{1,0:T(8,128)S(1)}, f32[192,128]{1,0:T(8,128)S(1)}, u32[]{:S(2)}, u32[]{:S(2)}) collective-permute-start(f32[192,128]{1,0:T(8,128)S(1)} %extract_0.1), channel_id=1, source_target_pairs={{1,2},{3,4},{5,6},{7,0},{2,1},{4,3},{6,5},{0,7},{9,10},{11,12},{13... | collective-permute-start | bytes 294920 | tf_op jit(solution)/shard_map/ppermute | solution.py:379
  14.3 5.9 %collective-permute-start.6 = (f32[192,128]{1,0:T(8,128)S(1)}, f32[192,128]{1,0:T(8,128)S(1)}, u32[]{:S(2)}, u32[]{:S(2)}) collective-permute-start(f32[192,128]{1,0:T(8,128)S(1)} %extract_0.1), channel_id=1, source_target_pairs={{0,1},{2,3},{4,5},{6,7},{1,0},{3,2},{5,4},{7,6},{8,9},{10,11},{12,... | collective-permute-start | bytes 294920 | tf_op jit(solution)/shard_map/ppermute | solution.py:379
  15.7 16.0 %collective-permute-start = (f32[384,128]{1,0:T(8,128)S(1)}, f32[384,128]{1,0:T(8,128)S(1)}, u32[]{:S(2)}, u32[]{:S(2)}) collective-permute-start(f32[384,128]{1,0:T(8,128)S(1)} %get-tuple-element.33), channel_id=1, source_target_pairs={{0,8},{16,24},{8,0},{24,16},{1,9},{17,25},{9,1},{25,17},{2,10},{18... | collective-permute-start | bytes 589832 | tf_op jit(solution)/shard_map/ppermute | solution.py:379
  18.9 12.8 %collective-permute-start.1 = (f32[384,128]{1,0:T(8,128)S(1)}, f32[384,128]{1,0:T(8,128)S(1)}, u32[]{:S(2)}, u32[]{:S(2)}) collective-permute-start(f32[384,128]{1,0:T(8,128)S(1)} %get-tuple-element.34), channel_id=1, source_target_pairs={{8,16},{24,0},{16,8},{0,24},{9,17},{25,1},{17,9},{1,25},{10,18},{2... | collective-permute-start | bytes 589832 | tf_op jit(solution)/shard_map/ppermute | solution.py:379
  20.2 7.9 %collective-permute-start.3 = (f32[128,128]{1,0:T(8,128)S(1)}, f32[128,128]{1,0:T(8,128)S(1)}, u32[]{:S(2)}, u32[]{:S(2)}) collective-permute-start(f32[128,128]{1,0:T(8,128)S(1)} %get-tuple-element.35), channel_id=1, source_target_pairs={{1,2},{3,4},{5,6},{7,0},{2,1},{4,3},{6,5},{0,7},{9,10},{11,12},{13... | collective-permute-start | bytes 196616 | tf_op jit(solution)/shard_map/ppermute | solution.py:379
  21.2 10.2 %collective-permute-start.2 = (f32[128,128]{1,0:T(8,128)S(1)}, f32[128,128]{1,0:T(8,128)S(1)}, u32[]{:S(2)}, u32[]{:S(2)}) collective-permute-start(f32[128,128]{1,0:T(8,128)S(1)} %get-tuple-element.35), channel_id=1, source_target_pairs={{0,1},{2,3},{4,5},{6,7},{1,0},{3,2},{5,4},{7,6},{8,9},{10,11},{12,... | collective-permute-start | bytes 196616 | tf_op jit(solution)/shard_map/ppermute | solution.py:379
  28.0 13.3 %collective-permute-start.16 = (f32[384,128]{1,0:T(8,128)S(1)}, f32[384,128]{1,0:T(8,128)S(1)}, u32[]{:S(2)}, u32[]{:S(2)}) collective-permute-start(f32[384,128]{1,0:T(8,128)S(1)} %get-tuple-element.53), channel_id=1, source_target_pairs={{0,8},{16,24},{8,0},{24,16},{1,9},{17,25},{9,1},{25,17},{2,10},{18... | collective-permute-start | bytes 589832 | tf_op jit(solution)/shard_map/ppermute | solution.py:379
  28.1 13.2 %collective-permute-start.17 = (f32[384,128]{1,0:T(8,128)S(1)}, f32[384,128]{1,0:T(8,128)S(1)}, u32[]{:S(2)}, u32[]{:S(2)}) collective-permute-start(f32[384,128]{1,0:T(8,128)S(1)} %get-tuple-element.54), channel_id=1, source_target_pairs={{8,16},{24,0},{16,8},{0,24},{9,17},{25,1},{17,9},{1,25},{10,18},{2... | collective-permute-start | bytes 589832 | tf_op jit(solution)/shard_map/ppermute | solution.py:379
  31.4 7.2 %collective-permute-start.19 = (f32[128,128]{1,0:T(8,128)S(1)}, f32[128,128]{1,0:T(8,128)S(1)}, u32[]{:S(2)}, u32[]{:S(2)}) collective-permute-start(f32[128,128]{1,0:T(8,128)S(1)} %get-tuple-element.55), channel_id=1, source_target_pairs={{1,2},{3,4},{5,6},{7,0},{2,1},{4,3},{6,5},{0,7},{9,10},{11,12},{13... | collective-permute-start | bytes 196616 | tf_op jit(solution)/shard_map/ppermute | solution.py:379
  36.5 12.3 %collective-permute-start.8 = (f32[384,128]{1,0:T(8,128)S(1)}, f32[384,128]{1,0:T(8,128)S(1)}, u32[]{:S(2)}, u32[]{:S(2)}) collective-permute-start(f32[384,128]{1,0:T(8,128)S(1)} %get-tuple-element.45), channel_id=1, source_target_pairs={{0,8},{16,24},{8,0},{24,16},{1,9},{17,25},{9,1},{25,17},{2,10},{18... | collective-permute-start | bytes 589832 | tf_op jit(solution)/shard_map/ppermute | solution.py:379
  37.3 11.5 %collective-permute-start.9 = (f32[384,128]{1,0:T(8,128)S(1)}, f32[384,128]{1,0:T(8,128)S(1)}, u32[]{:S(2)}, u32[]{:S(2)}) collective-permute-start(f32[384,128]{1,0:T(8,128)S(1)} %get-tuple-element.46), channel_id=1, source_target_pairs={{8,16},{24,0},{16,8},{0,24},{9,17},{25,1},{17,9},{1,25},{10,18},{2... | collective-permute-start | bytes 589832 | tf_op jit(solution)/shard_map/ppermute | solution.py:379
  38.6 1.3 %collective-permute-start.18 = (f32[128,128]{1,0:T(8,128)S(1)}, f32[128,128]{1,0:T(8,128)S(1)}, u32[]{:S(2)}, u32[]{:S(2)}) collective-permute-start(f32[128,128]{1,0:T(8,128)S(1)} %get-tuple-element.55), channel_id=1, source_target_pairs={{0,1},{2,3},{4,5},{6,7},{1,0},{3,2},{5,4},{7,6},{8,9},{10,11},{12,... | collective-permute-start | bytes 196616 | tf_op jit(solution)/shard_map/ppermute | solution.py:379
  39.9 5.7 %collective-permute-start.11 = (f32[128,128]{1,0:T(8,128)S(1)}, f32[128,128]{1,0:T(8,128)S(1)}, u32[]{:S(2)}, u32[]{:S(2)}) collective-permute-start(f32[128,128]{1,0:T(8,128)S(1)} %get-tuple-element.47), channel_id=1, source_target_pairs={{1,2},{3,4},{5,6},{7,0},{2,1},{4,3},{6,5},{0,7},{9,10},{11,12},{13... | collective-permute-start | bytes 196616 | tf_op jit(solution)/shard_map/ppermute | solution.py:379
  41.3 6.9 %collective-permute-start.10 = (f32[128,128]{1,0:T(8,128)S(1)}, f32[128,128]{1,0:T(8,128)S(1)}, u32[]{:S(2)}, u32[]{:S(2)}) collective-permute-start(f32[128,128]{1,0:T(8,128)S(1)} %get-tuple-element.47), channel_id=1, source_target_pairs={{0,1},{2,3},{4,5},{6,7},{1,0},{3,2},{5,4},{7,6},{8,9},{10,11},{12,... | collective-permute-start | bytes 196616 | tf_op jit(solution)/shard_map/ppermute | solution.py:379
  45.0 13.2 %collective-permute-start.20 = (f32[384,128]{1,0:T(8,128)S(1)}, f32[384,128]{1,0:T(8,128)S(1)}, u32[]{:S(2)}, u32[]{:S(2)}) collective-permute-start(f32[384,128]{1,0:T(8,128)S(1)} %get-tuple-element.57), channel_id=1, source_target_pairs={{0,8},{16,24},{8,0},{24,16},{1,9},{17,25},{9,1},{25,17},{2,10},{18... | collective-permute-start | bytes 589832 | tf_op jit(solution)/shard_map/ppermute | solution.py:379
  45.5 13.2 %collective-permute-start.21 = (f32[384,128]{1,0:T(8,128)S(1)}, f32[384,128]{1,0:T(8,128)S(1)}, u32[]{:S(2)}, u32[]{:S(2)}) collective-permute-start(f32[384,128]{1,0:T(8,128)S(1)} %get-tuple-element.58), channel_id=1, source_target_pairs={{8,16},{24,0},{16,8},{0,24},{9,17},{25,1},{17,9},{1,25},{10,18},{2... | collective-permute-start | bytes 589832 | tf_op jit(solution)/shard_map/ppermute | solution.py:379
  48.2 7.4 %collective-permute-start.23 = (f32[128,128]{1,0:T(8,128)S(1)}, f32[128,128]{1,0:T(8,128)S(1)}, u32[]{:S(2)}, u32[]{:S(2)}) collective-permute-start(f32[128,128]{1,0:T(8,128)S(1)} %get-tuple-element.59), channel_id=1, source_target_pairs={{1,2},{3,4},{5,6},{7,0},{2,1},{4,3},{6,5},{0,7},{9,10},{11,12},{13... | collective-permute-start | bytes 196616 | tf_op jit(solution)/shard_map/ppermute | solution.py:379
  48.8 10.0 %copy-start.6 = (f32[10,256]{1,0:T(8,128)S(1)}, f32[10,256]{1,0:T(8,128)}, u32[]{:S(2)}) copy-start(f32[10,256]{1,0:T(8,128)} %refs_18_.1) | copy-start | bytes 30724
  48.8 10.0 %copy-start.8 = (f32[10,10]{1,0:T(8,128)S(1)}, f32[10,10]{1,0:T(8,128)}, u32[]{:S(2)}) copy-start(f32[10,10]{1,0:T(8,128)} %refs_17_.1) | copy-start | bytes 1204
  48.8 10.0 %copy-start.9 = (s32[256]{0:T(256)S(1)}, s32[256]{0:T(256)}, u32[]{:S(2)}) copy-start(s32[256]{0:T(256)} %param.15) | copy-start | bytes 3076
  48.8 10.0 %copy-start.10 = (s32[256]{0:T(256)S(1)}, s32[256]{0:T(256)}, u32[]{:S(2)}) copy-start(s32[256]{0:T(256)} %param.16) | copy-start | bytes 3076
  52.4 11.7 %collective-permute-start.12 = (f32[384,128]{1,0:T(8,128)S(1)}, f32[384,128]{1,0:T(8,128)S(1)}, u32[]{:S(2)}, u32[]{:S(2)}) collective-permute-start(f32[384,128]{1,0:T(8,128)S(1)} %get-tuple-element.49), channel_id=1, source_target_pairs={{0,8},{16,24},{8,0},{24,16},{1,9},{17,25},{9,1},{25,17},{2,10},{18... | collective-permute-start | bytes 589832 | tf_op jit(solution)/shard_map/ppermute | solution.py:379
  54.2 12.1 %collective-permute-start.13 = (f32[384,128]{1,0:T(8,128)S(1)}, f32[384,128]{1,0:T(8,128)S(1)}, u32[]{:S(2)}, u32[]{:S(2)}) collective-permute-start(f32[384,128]{1,0:T(8,128)S(1)} %get-tuple-element.50), channel_id=1, source_target_pairs={{8,16},{24,0},{16,8},{0,24},{9,17},{25,1},{17,9},{1,25},{10,18},{2... | collective-permute-start | bytes 589832 | tf_op jit(solution)/shard_map/ppermute | solution.py:379
  55.6 1.3 %collective-permute-start.22 = (f32[128,128]{1,0:T(8,128)S(1)}, f32[128,128]{1,0:T(8,128)S(1)}, u32[]{:S(2)}, u32[]{:S(2)}) collective-permute-start(f32[128,128]{1,0:T(8,128)S(1)} %get-tuple-element.59), channel_id=1, source_target_pairs={{0,1},{2,3},{4,5},{6,7},{1,0},{3,2},{5,4},{7,6},{8,9},{10,11},{12,... | collective-permute-start | bytes 196616 | tf_op jit(solution)/shard_map/ppermute | solution.py:379
  56.9 7.2 %collective-permute-start.15 = (f32[128,128]{1,0:T(8,128)S(1)}, f32[128,128]{1,0:T(8,128)S(1)}, u32[]{:S(2)}, u32[]{:S(2)}) collective-permute-start(f32[128,128]{1,0:T(8,128)S(1)} %get-tuple-element.51), channel_id=1, source_target_pairs={{1,2},{3,4},{5,6},{7,0},{2,1},{4,3},{6,5},{0,7},{9,10},{11,12},{13... | collective-permute-start | bytes 196616 | tf_op jit(solution)/shard_map/ppermute | solution.py:379
  58.1 6.0 %collective-permute-start.14 = (f32[128,128]{1,0:T(8,128)S(1)}, f32[128,128]{1,0:T(8,128)S(1)}, u32[]{:S(2)}, u32[]{:S(2)}) collective-permute-start(f32[128,128]{1,0:T(8,128)S(1)} %get-tuple-element.51), channel_id=1, source_target_pairs={{0,1},{2,3},{4,5},{6,7},{1,0},{3,2},{5,4},{7,6},{8,9},{10,11},{12,... | collective-permute-start | bytes 196616 | tf_op jit(solution)/shard_map/ppermute | solution.py:379
  (4 other events, 29.4 us)
where the time goes:
time: 70.5 us; the launch traced here: 70.3 us
  Pallas kernels  33.1 us (47%)
  starting transfers between devices  26.3 us (37%)
  waiting for transfers between devices  7.14 us (10%)
  local copies, waits for them, and re-layouts  1.65 us (2%)
  between operations  1.5 us (2%)
    pallas_call x6, Pallas kernels, per_device(): pl.pallas_call(functools.partial(section_kernel, x_size, k, c, last, city...  26 us
    ppermute x12, starting transfers between devices, exchange(): lax.ppermute(to_b, axis, both[1])  18.5 us
    ppermute x12, starting transfers between devices, exchange(): lax.ppermute(to_a, axis, both[0])  7.76 us
    ppermute x12, waiting for transfers between devices, exchange(): lax.ppermute(to_b, axis, both[1])  4.84 us
    pallas_call x1, Pallas kernels, per_device(): pl.pallas_call(functools.partial(first_rows_kernel, x_size, rows, levels,...  2.98 us
    pallas_call x2, Pallas kernels, per_device(): pl.pallas_call(functools.partial(extract_kernel, x_size, c, c == 0), in_s...  2.5 us
    ppermute x12, waiting for transfers between devices, exchange(): lax.ppermute(to_a, axis, both[0])  2.3 us
    pallas_call x1, Pallas kernels, per_device(): pl.pallas_call(functools.partial(wind_kernel, x_size, rows), in_specs=[sm...  1.67 us
  transfers between devices with their start and end apart: 24, of which 5 were waited for; matrix products, arithmetic and copies ran while one was open for 0% of the time, Pallas kernels for 37%

commit v1 on v0

--- a/solution.py
+++ b/solution.py
@@ -51,7 +51,11 @@
     return rolled(jnp.where(lane >= row.shape[1] + k, halo, row), -k)
 
 
-def first_rows_kernel(x_size, rows, levels, pieces, odd, field, wind, to_a, to_b, field_here, wind_here, sems):
+def even_index(axis):
+    return lax.rem(lax.axis_index(axis), 2) == 0
+
+
+def first_rows_kernel(x_size, rows, levels, pieces, field, wind, to_a, to_b, field_here, wind_here, sems):
     size = rows * x_size // pieces
     copies = [
         pltpu.make_async_copy(field.at[pl.ds(p * size, size), :], field_here.at[pl.ds(p * size, size), :], sems.at[p])
@@ -60,7 +64,7 @@
     copies.append(pltpu.make_async_copy(wind.at[pl.ds(0, levels * x_size), :], wind_here, sems.at[pieces]))
     for copy in copies:
         copy.start()
-    even = odd[0] == 0
+    even = even_index("gx")
     for p in range(pieces):
         copies[p].wait()
         for t in range(p * rows // pieces // 8, (p + 1) * rows // pieces // 8):
@@ -78,7 +82,7 @@
         to_b[at : at + 8, :] = jnp.where(even, low, high)
 
 
-def extract_kernel(x_size, chunk, with_wind, odd, field, *refs):
+def extract_kernel(x_size, chunk, with_wind, field, *refs):
     if with_wind:
         wind, packed = refs
     else:
@@ -87,7 +91,7 @@
     if with_wind:
         levels = wind.shape[0] // (2 * x_size)
         rows = rows - levels
-    even = odd[0] == 0
+    even = even_index("gx")
 
     def one(t, carry):
         base = pl.multiple_of((chunk * rows + t * 8) * x_size, 8 * x_size)
@@ -124,10 +128,10 @@
     return jnp.where((lane_index(south.shape) & (GROUP - 1)) < WIDTH, south, north)
 
 
-def wind_kernel(x_size, rows, odd, wind, factor, from_a, from_b, pack_a, pack_b, *outs):
+def wind_kernel(x_size, rows, wind, factor, pack_a, pack_b, *outs):
     speed_x, ahead_y, behind_y, edge_ahead, edge_behind, scales = outs
     levels = speed_x.shape[1]
-    even_x, even_y = odd[0] == 0, odd[1] == 0
+    even_y = even_index("gy")
     for x in range(x_size):
         mapped = factor[pl.ds(x, 1), :]
         for k, divisor in enumerate(DIVISORS):
@@ -136,11 +140,9 @@
     def one(t, carry):
         base = pl.multiple_of(t * 8 * x_size, 8 * x_size)
         at = pl.ds(pl.multiple_of(t * 8, 8), 8)
-        there = pl.ds(pl.multiple_of(WIDTH * rows + t * 8, 8), 8)
-        before = jnp.where(even_x, from_b[there, :], from_a[there, :])
-        east = jnp.where(even_x, from_a[there, :], from_b[there, :])
+        before = jnp.zeros((8, wind.shape[1]), jnp.float32)
         for x in range(x_size + 1):
-            now = east if x == x_size else wind[pl.ds(base + x, 8, stride=x_size), :]
+            now = jnp.zeros_like(before) if x == x_size else wind[pl.ds(base + x, 8, stride=x_size), :]
             speed_x[x, at, :] = face_scale * (before + now)
             before = now
         base = base + levels * x_size
@@ -192,12 +194,13 @@
     return jnp.dot(halves, matrix[:, columns], preferred_element_type=jnp.float32)
 
 
-def section_kernel(x_size, k, chunk, last, with_city, odd, *refs):
+def section_kernel(x_size, k, chunk, last, with_city, *refs):
     refs = list(refs)
     first = k == 0
     section = refs.pop(0)
     base_ref = section if first else refs.pop(0)
     from_a, from_b, pack_a, pack_b = [refs.pop(0) for _ in range(4)]
+    wind_a, wind_b = [refs.pop(0) for _ in range(2)]
     speed_x, ahead_y, behind_y, edge_ahead, edge_behind, scales = [refs.pop(0) for _ in range(6)]
     inner_matrix, edge_matrix = [refs.pop(0) for _ in range(2)]
     parts = refs[-4:]
@@ -214,16 +217,17 @@
         out, to_a, to_b, packed = refs
     levels, y_size = edge_ahead.shape
     chunk_rows = base_ref.shape[0] // (CHUNKS * x_size)
-    even_x, even_y = odd[0] == 0, odd[1] == 0
+    even_x, even_y = even_index("gx"), even_index("gy")
 
     def block(g, carry):
         corner = pl.multiple_of((chunk * chunk_rows + g * levels) * x_size, levels * x_size)
         here = pl.multiple_of(g * levels, levels)
         for p in range(levels * x_size // PIECE):
+            n = PIECE // levels
             if first:
-                values = section[pl.ds(pl.multiple_of(corner + p * PIECE, PIECE), PIECE), :]
+                lines = [section[pl.ds(corner + x, levels, stride=x_size), :] for x in range(p * n, (p + 1) * n)]
+                values = jnp.concatenate(lines, axis=0)
             else:
-                n = PIECE // levels
                 values = section[p * n : (p + 1) * n, pl.ds(here, levels), :].reshape(PIECE, y_size)
             halves = split_halves(values)
             for pair in range(2):
@@ -248,6 +252,10 @@
             def halo_rows(mine, other, j):
                 edge_at = pl.ds(pl.multiple_of(j * chunk_rows + here + t * 8, 8), 8)
                 return jnp.where(even_x, mine[edge_at, :], other[edge_at, :])
+
+            def outer_wind(mine, other):
+                wind_at = pl.ds(pl.multiple_of(WIDTH * chunk_rows + t * 8, 8), 8)
+                return jnp.where(even_x, mine[wind_at, :], other[wind_at, :])
 
             def cell(x):
                 if x < 0:
@@ -276,13 +284,14 @@
                 new4 = new3 - d3
                 new_smooth = new4 - 5.0 * d2 + 30.0 * q[0]
                 speed = speed_x[x + 1, at, :]
+                if x == -1:
+                    speed = speed + face_scale * outer_wind(wind_b, wind_a)
+                if x == x_size - 1:
+                    speed = speed + face_scale * outer_wind(wind_a, wind_b)
                 flux = speed * (smooth + new_smooth) - jnp.abs(speed) * (new4 - d4)
                 d1, d2, d3, d4, smooth = new1, new2, new3, new4, new_smooth
                 if x >= 0:
-                    if first:
-                        lines = [part[pl.ds(t * 8 * x_size + x, 8, stride=x_size), :] for part in parts]
-                    else:
-                        lines = [part[pl.ds(pl.multiple_of(x * levels + t * 8, 8), 8), :] for part in parts]
+                    lines = [part[pl.ds(pl.multiple_of(x * levels + t * 8, 8), 8), :] for part in parts]
                     after, before = ahead_y[x, at, :], behind_y[x, at, :]
                     moved = rolled(edge_share, -(GROUP * x + WIDTH))
                     divergence = (
@@ -401,13 +410,12 @@
 
     smem = pl.BlockSpec(memory_space=pltpu.SMEM)
     hbm = pl.BlockSpec(memory_space=pltpu.HBM)
-    odd = jnp.stack([lax.axis_index("gx") % 2, lax.axis_index("gy") % 2]).astype(jnp.int32)
     cheap = pl.CostEstimate(flops=1000, bytes_accessed=1000, transcendentals=0)
 
     pieces = 4
     first_rows = pl.pallas_call(
         functools.partial(first_rows_kernel, x_size, rows, levels, pieces),
-        in_specs=[smem, hbm, hbm],
+        in_specs=[hbm, hbm],
         out_specs=[whole] * 2,
         out_shape=[f32((WIDTH * rows + levels, y_size))] * 2,
         scratch_shapes=[
@@ -418,27 +426,27 @@
         compiler_params=pltpu.CompilerParams(vmem_limit_bytes=62 * 2**20),
         cost_estimate=cheap,
         name="first_rows",
-    )(odd, field, wind)
+    )(field, wind)
     received = [None] * CHUNKS
     received[0] = exchange("gx", *first_rows)
     for c in range(CHUNKS):
         extra = levels if c == 0 else 0
         outs = pl.pallas_call(
             functools.partial(extract_kernel, x_size, c, c == 0),
-            in_specs=[smem, whole] + [whole] * (c == 0),
+            in_specs=[whole] + [whole] * (c == 0),
             out_specs=[whole] * (1 if c == 0 else 3),
             out_shape=[f32((WIDTH * rows, y_size))] * (0 if c == 0 else 2) + [f32((rows + extra, y_size))],
             compiler_params=params,
             cost_estimate=cheap,
             name=f"extract_{c}",
-        )(odd, field, *([wind] if c == 0 else []))
+        )(field, *([wind] if c == 0 else []))
         if c > 0:
             received[c] = exchange("gx", *outs[:2])
         received[c] = (*received[c], *exchange("gy", outs[-1], outs[-1]))
 
     speeds = pl.pallas_call(
         functools.partial(wind_kernel, x_size, rows),
-        in_specs=[smem] + [whole] * 6,
+        in_specs=[whole] * 4,
         out_specs=[whole] * 6,
         out_shape=[
             f32((x_size + 1, levels, y_size)),
@@ -451,7 +459,8 @@
         compiler_params=params,
         cost_estimate=cheap,
         name="speeds",
-    )(odd, wind, map_factor, *received[0])
+    )(wind, map_factor, *received[0][2:])
+    winds_beyond = received[0][:2]
     matrices = stencil_matrices(y_size)
 
     steps = rows // levels
@@ -460,9 +469,9 @@
     for k in range(len(DIVISORS)):
         last = k == len(DIVISORS) - 1
         for c in range(CHUNKS):
-            operands = [odd] + ([field] if k == 0 else [sections[c], field])
-            operands += [*received[c], *speeds, *matrices]
-            specs = [smem] + [whole] * (len(operands) - 1)
+            operands = [field] if k == 0 else [sections[c], field]
+            operands += [*received[c], *winds_beyond, *speeds, *matrices]
+            specs = [whole] * len(operands)
             city = last and c == 0
             aliases = {}
             flat_c = pl.BlockSpec((levels * x_size, y_size), lambda g, c=c: (c * steps + g, 0))

time: 70.5 us -> 65 us (0.922)
  Pallas kernels: 33.1 us -> 24.4 us
  waiting for transfers between devices: 7.14 us -> 9.11 us
  starting transfers between devices: 26.3 us -> 28.2 us
    pallas_call x6, Pallas kernels: 26 us -> 19.6 us  [per_device(): pl.pallas_call(functools.partial(section_kernel, x_size, k, c, last, city...]
    ppermute x12, starting transfers between devices: 18.5 us -> 22.9 us  [exchange(): lax.ppermute(to_b, axis, both[1])]
    ppermute x12, starting transfers between devices: 7.76 us -> 5.29 us  [exchange(): lax.ppermute(to_a, axis, both[0])]
    ppermute x12, waiting for transfers between devices: 4.84 us -> 6.58 us  [exchange(): lax.ppermute(to_b, axis, both[1])]
    pallas_call x2, Pallas kernels: 2.5 us -> 1.42 us  [per_device(): pl.pallas_call(functools.partial(extract_kernel, x_size, c, c == 0), in_s...]
    unnamed x24 -> x22, local copies, waits for them, and re-layouts: 1.65 us -> 1.64 us
  transfers between devices with their start and end apart: 24 -> 24, of which waited for: 5 -> 6; matrix products, arithmetic and copies ran while one was open for 0% -> 0% of each run, Pallas kernels for 37% -> 29%
where the time goes in v1:
time: 65 us; the launch traced here: 64.8 us
  starting transfers between devices  28.2 us (43%)
  Pallas kernels  24.4 us (38%)
  waiting for transfers between devices  9.11 us (14%)
  local copies, waits for them, and re-layouts  1.64 us (3%)
  between operations  1.51 us (2%)
    ppermute x12, starting transfers between devices, exchange(): lax.ppermute(to_b, axis, both[1])  22.9 us
    pallas_call x6, Pallas kernels, per_device(): pl.pallas_call(functools.partial(section_kernel, x_size, k, c, last, city...  19.6 us
    ppermute x12, waiting for transfers between devices, exchange(): lax.ppermute(to_b, axis, both[1])  6.58 us
    ppermute x12, starting transfers between devices, exchange(): lax.ppermute(to_a, axis, both[0])  5.29 us
    ppermute x12, waiting for transfers between devices, exchange(): lax.ppermute(to_a, axis, both[0])  2.53 us
    pallas_call x1, Pallas kernels, per_device(): pl.pallas_call(functools.partial(first_rows_kernel, x_size, rows, levels,...  2.28 us
    unnamed x22, local copies, waits for them, and re-layouts  1.64 us
    pallas_call x2, Pallas kernels, per_device(): pl.pallas_call(functools.partial(extract_kernel, x_size, c, c == 0), in_s...  1.42 us
  transfers between devices with their start and end apart: 24, of which 6 were waited for; matrix products, arithmetic and copies ran while one was open for 0% of the time, Pallas kernels for 29%

profile of v1, /device:TPU:0, one launch (start us, length us, event | category | flops | bytes accessed | tf_op | source)
XLA Modules:
  0.0 64.8 jit_solution(7320389341441682341)
XLA Ops:
  0.6 2.3 %first_rows.1 = (f32[448,128]{1,0:T(8,128)}, f32[448,128]{1,0:T(8,128)}) custom-call(f32[4096,128]{1,0:T(8,128)} %bitcast.7, f32[2048,128]{1,0:T(8,128)} %bitcast.16), custom_call_target="tpu_custom_call" | custom-call | flops 1000 | bytes 1000 | tf_op jit(solution)/shard_map/first_rows/pallas_call | solution.py:416
  2.9 3.1 %collective-permute-start.4 = (f32[448,128]{1,0:T(8,128)}, f32[448,128]{1,0:T(8,128)S(1)}, u32[]{:S(2)}, u32[]{:S(2)}) collective-permute-start(f32[448,128]{1,0:T(8,128)} %get-tuple-element.36), channel_id=1, source_target_pairs={{0,8},{16,24},{8,0},{24,16},{1,9},{17,25},{9,1},{25,17},{2,10},{18... | collective-permute-start | bytes 688136 | tf_op jit(solution)/shard_map/ppermute | solution.py:388
  6.0 2.5 %collective-permute-start.5 = (f32[448,128]{1,0:T(8,128)}, f32[448,128]{1,0:T(8,128)S(1)}, u32[]{:S(2)}, u32[]{:S(2)}) collective-permute-start(f32[448,128]{1,0:T(8,128)} %get-tuple-element.37), channel_id=1, source_target_pairs={{8,16},{24,0},{16,8},{0,24},{9,17},{25,1},{17,9},{1,25},{10,18},{2... | collective-permute-start | bytes 688136 | tf_op jit(solution)/shard_map/ppermute | solution.py:388
  8.5 1.6 %copy-done = f32[4,64,16,128]{3,2,1,0:T(8,128)S(1)} copy-done((f32[4,64,16,128]{3,2,1,0:T(8,128)S(1)}, f32[4,64,16,128]{3,2,1,0:T(8,128)}, u32[]{:S(2)}) %copy-start) | copy-done | bytes 2097176
  10.1 0.8 %extract_0.1 = f32[192,128]{1,0:T(8,128)S(1)} custom-call(f32[4096,128]{1,0:T(8,128)S(1)} %bitcast.8, f32[2048,128]{1,0:T(8,128)S(1)} %bitcast.17), custom_call_target="tpu_custom_call" | custom-call | flops 1000 | bytes 1000 | tf_op jit(solution)/shard_map/extract_0/pallas_call | solution.py:434
  11.0 1.4 %collective-permute-start.7 = (f32[192,128]{1,0:T(8,128)S(1)}, f32[192,128]{1,0:T(8,128)S(1)}, u32[]{:S(2)}, u32[]{:S(2)}) collective-permute-start(f32[192,128]{1,0:T(8,128)S(1)} %extract_0.1), channel_id=1, source_target_pairs={{1,2},{3,4},{5,6},{7,0},{2,1},{4,3},{6,5},{0,7},{9,10},{11,12},{13... | collective-permute-start | bytes 294920 | tf_op jit(solution)/shard_map/ppermute | solution.py:388
  12.4 0.3 collective-permute-start.6
  12.7 0.6 extract_1.1
  13.2 0.7 %collective-permute-start = (f32[384,128]{1,0:T(8,128)S(1)}, f32[384,128]{1,0:T(8,128)S(1)}, u32[]{:S(2)}, u32[]{:S(2)}) collective-permute-start(f32[384,128]{1,0:T(8,128)S(1)} %get-tuple-element.33), channel_id=1, source_target_pairs={{0,8},{16,24},{8,0},{24,16},{1,9},{17,25},{9,1},{25,17},{2,10},{18... | collective-permute-start | bytes 589832 | tf_op jit(solution)/shard_map/ppermute | solution.py:388
  14.0 3.0 %collective-permute-done.7.pack_b.refs_4_ = f32[192,128]{1,0:T(8,128)S(1)} collective-permute-done((f32[192,128]{1,0:T(8,128)S(1)}, f32[192,128]{1,0:T(8,128)S(1)}, u32[]{:S(2)}, u32[]{:S(2)}) %collective-permute-start.7) | collective-permute-done | bytes 98336 | tf_op jit(solution)/shard_map/ppermute | solution.py:388
  16.9 1.3 %collective-permute-start.1 = (f32[384,128]{1,0:T(8,128)S(1)}, f32[384,128]{1,0:T(8,128)S(1)}, u32[]{:S(2)}, u32[]{:S(2)}) collective-permute-start(f32[384,128]{1,0:T(8,128)S(1)} %get-tuple-element.34), channel_id=1, source_target_pairs={{8,16},{24,0},{16,8},{0,24},{9,17},{25,1},{17,9},{1,25},{10,18},{2... | collective-permute-start | bytes 589832 | tf_op jit(solution)/shard_map/ppermute | solution.py:388
  18.3 1.0 %collective-permute-start.3 = (f32[128,128]{1,0:T(8,128)S(1)}, f32[128,128]{1,0:T(8,128)S(1)}, u32[]{:S(2)}, u32[]{:S(2)}) collective-permute-start(f32[128,128]{1,0:T(8,128)S(1)} %get-tuple-element.35), channel_id=1, source_target_pairs={{1,2},{3,4},{5,6},{7,0},{2,1},{4,3},{6,5},{0,7},{9,10},{11,12},{13... | collective-permute-start | bytes 196616 | tf_op jit(solution)/shard_map/ppermute | solution.py:388
  19.3 1.1 %speeds.1 = (f32[17,64,128]{2,1,0:T(8,128)S(1)}, f32[16,64,128]{2,1,0:T(8,128)S(1)}, f32[16,64,128]{2,1,0:T(8,128)S(1)}, f32[64,128]{1,0:T(8,128)S(1)}, f32[64,1...) custom-call(f32[2048,128]{1,0:T(8,128)S(1)} %bitcast.18, f32[16,128]{1,0:T(8,128)S(1)} %copy-done.6, ...), custom_call_target="tpu_custom_call" | custom-call | flops 1000 | bytes 1000 | tf_op jit(solution)/shard_map/speeds/pallas_call | solution.py:447
  20.6 2.9 %section_0_0.1 = (f32[16,128,128]{2,1,0:T(8,128)S(1)}, f32[384,128]{1,0:T(8,128)S(1)}, f32[384,128]{1,0:T(8,128)S(1)}, f32[128,128]{1,0:T(8,128)S(1)}) custom-call(f32[4096,128]{1,0:T(8,128)S(1)} %bitcast.10, f32[448,128]{1,0:T(8,128)S(1)} %collective-permute-done.4.refs_5_.refs_6_.refs_1_, f32[448,128]{1,0:T(8,128)S(1)} %collective-permute-done.5.refs_6_.refs_7_.refs_2_, ...), custom_call_target="tpu_custom_call" | custom-call | flops 1000 | bytes 1000 | tf_op jit(solution)/shard_map/section_0_0/pallas_call | solution.py:504
  23.6 2.9 %collective-permute-start.17 = (f32[384,128]{1,0:T(8,128)S(1)}, f32[384,128]{1,0:T(8,128)S(1)}, u32[]{:S(2)}, u32[]{:S(2)}) collective-permute-start(f32[384,128]{1,0:T(8,128)S(1)} %get-tuple-element.54), channel_id=1, source_target_pairs={{8,16},{24,0},{16,8},{0,24},{9,17},{25,1},{17,9},{1,25},{10,18},{2... | collective-permute-start | bytes 589832 | tf_op jit(solution)/shard_map/ppermute | solution.py:388
  26.5 1.0 %collective-permute-start.19 = (f32[128,128]{1,0:T(8,128)S(1)}, f32[128,128]{1,0:T(8,128)S(1)}, u32[]{:S(2)}, u32[]{:S(2)}) collective-permute-start(f32[128,128]{1,0:T(8,128)S(1)} %get-tuple-element.55), channel_id=1, source_target_pairs={{1,2},{3,4},{5,6},{7,0},{2,1},{4,3},{6,5},{0,7},{9,10},{11,12},{13... | collective-permute-start | bytes 196616 | tf_op jit(solution)/shard_map/ppermute | solution.py:388
  27.6 2.9 %section_0_1.1 = (f32[16,128,128]{2,1,0:T(8,128)S(1)}, f32[384,128]{1,0:T(8,128)S(1)}, f32[384,128]{1,0:T(8,128)S(1)}, f32[128,128]{1,0:T(8,128)S(1)}) custom-call(f32[4096,128]{1,0:T(8,128)S(1)} %bitcast.11, f32[384,128]{1,0:T(8,128)S(1)} %collective-permute-done.refs_1_, f32[384,128]{1,0:T(8,128)S(1)} %collective-permute-done.1.refs_2_, ...), custom_call_target="tpu_custom_call" | custom-call | flops 1000 | bytes 1000 | tf_op jit(solution)/shard_map/section_0_1/pallas_call | solution.py:504
  30.5 0.7 %collective-permute-start.8 = (f32[384,128]{1,0:T(8,128)S(1)}, f32[384,128]{1,0:T(8,128)S(1)}, u32[]{:S(2)}, u32[]{:S(2)}) collective-permute-start(f32[384,128]{1,0:T(8,128)S(1)} %get-tuple-element.45), channel_id=1, source_target_pairs={{0,8},{16,24},{8,0},{24,16},{1,9},{17,25},{9,1},{25,17},{2,10},{18... | collective-permute-start | bytes 589832 | tf_op jit(solution)/shard_map/ppermute | solution.py:388
  31.2 2.4 %collective-permute-start.9 = (f32[384,128]{1,0:T(8,128)S(1)}, f32[384,128]{1,0:T(8,128)S(1)}, u32[]{:S(2)}, u32[]{:S(2)}) collective-permute-start(f32[384,128]{1,0:T(8,128)S(1)} %get-tuple-element.46), channel_id=1, source_target_pairs={{8,16},{24,0},{16,8},{0,24},{9,17},{25,1},{17,9},{1,25},{10,18},{2... | collective-permute-start | bytes 589832 | tf_op jit(solution)/shard_map/ppermute | solution.py:388
  33.6 1.3 %collective-permute-done.18.refs_4_ = f32[128,128]{1,0:T(8,128)S(1)} collective-permute-done((f32[128,128]{1,0:T(8,128)S(1)}, f32[128,128]{1,0:T(8,128)S(1)}, u32[]{:S(2)}, u32[]{:S(2)}) %collective-permute-start.18) | collective-permute-done | bytes 65568 | tf_op jit(solution)/shard_map/ppermute | solution.py:388
  34.9 2.7 %collective-permute-start.11 = (f32[128,128]{1,0:T(8,128)S(1)}, f32[128,128]{1,0:T(8,128)S(1)}, u32[]{:S(2)}, u32[]{:S(2)}) collective-permute-start(f32[128,128]{1,0:T(8,128)S(1)} %get-tuple-element.47), channel_id=1, source_target_pairs={{1,2},{3,4},{5,6},{7,0},{2,1},{4,3},{6,5},{0,7},{9,10},{11,12},{13... | collective-permute-start | bytes 196616 | tf_op jit(solution)/shard_map/ppermute | solution.py:388
  37.6 2.9 %section_1_0.1 = (f32[16,128,128]{2,1,0:T(8,128)S(1)}, f32[384,128]{1,0:T(8,128)S(1)}, f32[384,128]{1,0:T(8,128)S(1)}, f32[128,128]{1,0:T(8,128)S(1)}) custom-call(f32[16,128,128]{2,1,0:T(8,128)S(1)} %get-tuple-element.52.refs_0_, f32[4096,128]{1,0:T(8,128)S(1)} %bitcast.12, f32[384,128]{1,0:T(8,128)S(1)} %collective-permute-done.16.refs_2_, ...), custom_call_target="tpu_custom_call" | custom-call | flops 1000 | bytes 1000 | tf_op jit(solution)/shard_map/section_1_0/pallas_call | solution.py:504
  40.6 2.4 %collective-permute-start.21 = (f32[384,128]{1,0:T(8,128)S(1)}, f32[384,128]{1,0:T(8,128)S(1)}, u32[]{:S(2)}, u32[]{:S(2)}) collective-permute-start(f32[384,128]{1,0:T(8,128)S(1)} %get-tuple-element.58), channel_id=1, source_target_pairs={{8,16},{24,0},{16,8},{0,24},{9,17},{25,1},{17,9},{1,25},{10,18},{2... | collective-permute-start | bytes 589832 | tf_op jit(solution)/shard_map/ppermute | solution.py:388
  43.0 1.9 %collective-permute-done.9.refs_3_ = f32[384,128]{1,0:T(8,128)S(1)} collective-permute-done((f32[384,128]{1,0:T(8,128)S(1)}, f32[384,128]{1,0:T(8,128)S(1)}, u32[]{:S(2)}, u32[]{:S(2)}) %collective-permute-start.9) | collective-permute-done | bytes 196640 | tf_op jit(solution)/shard_map/ppermute | solution.py:388
  44.9 2.8 %section_1_1.1 = (f32[16,128,128]{2,1,0:T(8,128)S(1)}, f32[384,128]{1,0:T(8,128)S(1)}, f32[384,128]{1,0:T(8,128)S(1)}, f32[128,128]{1,0:T(8,128)S(1)}) custom-call(f32[16,128,128]{2,1,0:T(8,128)S(1)} %get-tuple-element.44.refs_0_, f32[4096,128]{1,0:T(8,128)S(1)} %bitcast.13, f32[384,128]{1,0:T(8,128)S(1)} %collective-permute-done.8.refs_2_, ...), custom_call_target="tpu_custom_call" | custom-call | flops 1000 | bytes 1000 | tf_op jit(solution)/shard_map/section_1_1/pallas_call | solution.py:504
  47.8 0.2 collective-permute-start.12
  48.0 3.4 %collective-permute-start.13 = (f32[384,128]{1,0:T(8,128)S(1)}, f32[384,128]{1,0:T(8,128)S(1)}, u32[]{:S(2)}, u32[]{:S(2)}) collective-permute-start(f32[384,128]{1,0:T(8,128)S(1)} %get-tuple-element.50), channel_id=1, source_target_pairs={{8,16},{24,0},{16,8},{0,24},{9,17},{25,1},{17,9},{1,25},{10,18},{2... | collective-permute-start | bytes 589832 | tf_op jit(solution)/shard_map/ppermute | solution.py:388
  51.4 1.3 %collective-permute-done.22.refs_4_ = f32[128,128]{1,0:T(8,128)S(1)} collective-permute-done((f32[128,128]{1,0:T(8,128)S(1)}, f32[128,128]{1,0:T(8,128)S(1)}, u32[]{:S(2)}, u32[]{:S(2)}) %collective-permute-start.22) | collective-permute-done | bytes 65568 | tf_op jit(solution)/shard_map/ppermute | solution.py:388
  52.6 1.8 %collective-permute-start.15 = (f32[128,128]{1,0:T(8,128)S(1)}, f32[128,128]{1,0:T(8,128)S(1)}, u32[]{:S(2)}, u32[]{:S(2)}) collective-permute-start(f32[128,128]{1,0:T(8,128)S(1)} %get-tuple-element.51), channel_id=1, source_target_pairs={{1,2},{3,4},{5,6},{7,0},{2,1},{4,3},{6,5},{0,7},{9,10},{11,12},{13... | collective-permute-start | bytes 196616 | tf_op jit(solution)/shard_map/ppermute | solution.py:388
  55.2 4.6 %section_2_0.1 = (f32[4096,128]{1,0:T(8,128)}, f32[10,256]{1,0:T(8,128)}, f32[1,256]{1,0:T(1,128)}) custom-call(f32[16,128,128]{2,1,0:T(8,128)S(1)} %get-tuple-element.56.refs_0_, f32[4096,128]{1,0:T(8,128)S(1)} %bitcast.14, f32[384,128]{1,0:T(8,128)S(1)} %collective-permute-done.20.refs_2_, f32[384,128]{1,0:T(8,128)S(1)} %collective-permute-done.21.refs_3_, ...), custom_call_target="tpu_custom_call" | custom-call | flops 1000 | bytes 1000 | tf_op jit(solution)/shard_map/section_2_0/pallas_call | solution.py:504
  59.8 1.6 %collective-permute-done.13.refs_3_ = f32[384,128]{1,0:T(8,128)S(1)} collective-permute-done((f32[384,128]{1,0:T(8,128)S(1)}, f32[384,128]{1,0:T(8,128)S(1)}, u32[]{:S(2)}, u32[]{:S(2)}) %collective-permute-start.13) | collective-permute-done | bytes 196640 | tf_op jit(solution)/shard_map/ppermute | solution.py:388
  61.4 3.4 %section_2_1.1 = f32[4096,128]{1,0:T(8,128)} custom-call(f32[16,128,128]{2,1,0:T(8,128)S(1)} %get-tuple-element.48.refs_0_, f32[4096,128]{1,0:T(8,128)S(1)} %bitcast.15, f32[384,128]{1,0:T(8,128)S(1)} %collective-permute-done.12.refs_2_, f32[384,128]{1,0:T(8,128)S(1)} %collective-permute-done.13.refs_3_, ...), custom_call_target="tpu_custom_call", output_to_operand_aliasing={{}: (16, {})} | custom-call | flops 1000 | bytes 1000 | tf_op jit(solution)/shard_map/section_2_1/pallas_call | solution.py:504
  (48 shorter events, 0.5 us)
Async XLA Ops:
  2.9 17.5 %collective-permute-start.4 = (f32[448,128]{1,0:T(8,128)}, f32[448,128]{1,0:T(8,128)S(1)}, u32[]{:S(2)}, u32[]{:S(2)}) collective-permute-start(f32[448,128]{1,0:T(8,128)} %get-tuple-element.36), channel_id=1, source_target_pairs={{0,8},{16,24},{8,0},{24,16},{1,9},{17,25},{9,1},{25,17},{2,10},{18... | collective-permute-start | bytes 688136 | tf_op jit(solution)/shard_map/ppermute | solution.py:388
  6.0 14.5 %collective-permute-start.5 = (f32[448,128]{1,0:T(8,128)}, f32[448,128]{1,0:T(8,128)S(1)}, u32[]{:S(2)}, u32[]{:S(2)}) collective-permute-start(f32[448,128]{1,0:T(8,128)} %get-tuple-element.37), channel_id=1, source_target_pairs={{8,16},{24,0},{16,8},{0,24},{9,17},{25,1},{17,9},{1,25},{10,18},{2... | collective-permute-start | bytes 688136 | tf_op jit(solution)/shard_map/ppermute | solution.py:388
  10.9 9.6 %copy-start.1 = (f32[4,64,16,128]{3,2,1,0:T(8,128)S(1)}, f32[4,64,16,128]{3,2,1,0:T(8,128)}, u32[]{:S(2)}) copy-start(f32[4,64,16,128]{3,2,1,0:T(8,128)} %param.11) | copy-start | bytes 6291460
  11.0 9.6 %copy-start.3 = (bf16[256,512]{1,0:T(8,128)(2,1)S(1)}, bf16[256,512]{1,0:T(8,128)(2,1)}, u32[]{:S(2)}) copy-start(bf16[256,512]{1,0:T(8,128)(2,1)} %constant.5.clone.refs_14_.refs_15_) | copy-start | bytes 786436
  11.0 9.6 %copy-start.4 = (bf16[256,512]{1,0:T(8,128)(2,1)S(1)}, bf16[256,512]{1,0:T(8,128)(2,1)}, u32[]{:S(2)}) copy-start(bf16[256,512]{1,0:T(8,128)(2,1)} %constant.4.clone.refs_13_.refs_14_) | copy-start | bytes 786436
  11.0 6.0 %collective-permute-start.7 = (f32[192,128]{1,0:T(8,128)S(1)}, f32[192,128]{1,0:T(8,128)S(1)}, u32[]{:S(2)}, u32[]{:S(2)}) collective-permute-start(f32[192,128]{1,0:T(8,128)S(1)} %extract_0.1), channel_id=1, source_target_pairs={{1,2},{3,4},{5,6},{7,0},{2,1},{4,3},{6,5},{0,7},{9,10},{11,12},{13... | collective-permute-start | bytes 294920 | tf_op jit(solution)/shard_map/ppermute | solution.py:388
  12.4 5.9 %collective-permute-start.6 = (f32[192,128]{1,0:T(8,128)S(1)}, f32[192,128]{1,0:T(8,128)S(1)}, u32[]{:S(2)}, u32[]{:S(2)}) collective-permute-start(f32[192,128]{1,0:T(8,128)S(1)} %extract_0.1), channel_id=1, source_target_pairs={{0,1},{2,3},{4,5},{6,7},{1,0},{3,2},{5,4},{7,6},{8,9},{10,11},{12,... | collective-permute-start | bytes 294920 | tf_op jit(solution)/shard_map/ppermute | solution.py:388
  13.2 14.2 %collective-permute-start = (f32[384,128]{1,0:T(8,128)S(1)}, f32[384,128]{1,0:T(8,128)S(1)}, u32[]{:S(2)}, u32[]{:S(2)}) collective-permute-start(f32[384,128]{1,0:T(8,128)S(1)} %get-tuple-element.33), channel_id=1, source_target_pairs={{0,8},{16,24},{8,0},{24,16},{1,9},{17,25},{9,1},{25,17},{2,10},{18... | collective-permute-start | bytes 589832 | tf_op jit(solution)/shard_map/ppermute | solution.py:388
  16.9 10.6 %collective-permute-start.1 = (f32[384,128]{1,0:T(8,128)S(1)}, f32[384,128]{1,0:T(8,128)S(1)}, u32[]{:S(2)}, u32[]{:S(2)}) collective-permute-start(f32[384,128]{1,0:T(8,128)S(1)} %get-tuple-element.34), channel_id=1, source_target_pairs={{8,16},{24,0},{16,8},{0,24},{9,17},{25,1},{17,9},{1,25},{10,18},{2... | collective-permute-start | bytes 589832 | tf_op jit(solution)/shard_map/ppermute | solution.py:388
  18.3 5.3 %collective-permute-start.3 = (f32[128,128]{1,0:T(8,128)S(1)}, f32[128,128]{1,0:T(8,128)S(1)}, u32[]{:S(2)}, u32[]{:S(2)}) collective-permute-start(f32[128,128]{1,0:T(8,128)S(1)} %get-tuple-element.35), channel_id=1, source_target_pairs={{1,2},{3,4},{5,6},{7,0},{2,1},{4,3},{6,5},{0,7},{9,10},{11,12},{13... | collective-permute-start | bytes 196616 | tf_op jit(solution)/shard_map/ppermute | solution.py:388
  20.5 6.0 %collective-permute-start.2 = (f32[128,128]{1,0:T(8,128)S(1)}, f32[128,128]{1,0:T(8,128)S(1)}, u32[]{:S(2)}, u32[]{:S(2)}) collective-permute-start(f32[128,128]{1,0:T(8,128)S(1)} %get-tuple-element.35), channel_id=1, source_target_pairs={{0,1},{2,3},{4,5},{6,7},{1,0},{3,2},{5,4},{7,6},{8,9},{10,11},{12,... | collective-permute-start | bytes 196616 | tf_op jit(solution)/shard_map/ppermute | solution.py:388
  23.5 14.1 %collective-permute-start.16 = (f32[384,128]{1,0:T(8,128)S(1)}, f32[384,128]{1,0:T(8,128)S(1)}, u32[]{:S(2)}, u32[]{:S(2)}) collective-permute-start(f32[384,128]{1,0:T(8,128)S(1)} %get-tuple-element.53), channel_id=1, source_target_pairs={{0,8},{16,24},{8,0},{24,16},{1,9},{17,25},{9,1},{25,17},{2,10},{18... | collective-permute-start | bytes 589832 | tf_op jit(solution)/shard_map/ppermute | solution.py:388
  23.6 14.0 %collective-permute-start.17 = (f32[384,128]{1,0:T(8,128)S(1)}, f32[384,128]{1,0:T(8,128)S(1)}, u32[]{:S(2)}, u32[]{:S(2)}) collective-permute-start(f32[384,128]{1,0:T(8,128)S(1)} %get-tuple-element.54), channel_id=1, source_target_pairs={{8,16},{24,0},{16,8},{0,24},{9,17},{25,1},{17,9},{1,25},{10,18},{2... | collective-permute-start | bytes 589832 | tf_op jit(solution)/shard_map/ppermute | solution.py:388
  26.5 7.2 %collective-permute-start.19 = (f32[128,128]{1,0:T(8,128)S(1)}, f32[128,128]{1,0:T(8,128)S(1)}, u32[]{:S(2)}, u32[]{:S(2)}) collective-permute-start(f32[128,128]{1,0:T(8,128)S(1)} %get-tuple-element.55), channel_id=1, source_target_pairs={{1,2},{3,4},{5,6},{7,0},{2,1},{4,3},{6,5},{0,7},{9,10},{11,12},{13... | collective-permute-start | bytes 196616 | tf_op jit(solution)/shard_map/ppermute | solution.py:388
  30.5 12.6 %collective-permute-start.8 = (f32[384,128]{1,0:T(8,128)S(1)}, f32[384,128]{1,0:T(8,128)S(1)}, u32[]{:S(2)}, u32[]{:S(2)}) collective-permute-start(f32[384,128]{1,0:T(8,128)S(1)} %get-tuple-element.45), channel_id=1, source_target_pairs={{0,8},{16,24},{8,0},{24,16},{1,9},{17,25},{9,1},{25,17},{2,10},{18... | collective-permute-start | bytes 589832 | tf_op jit(solution)/shard_map/ppermute | solution.py:388
  31.2 13.7 %collective-permute-start.9 = (f32[384,128]{1,0:T(8,128)S(1)}, f32[384,128]{1,0:T(8,128)S(1)}, u32[]{:S(2)}, u32[]{:S(2)}) collective-permute-start(f32[384,128]{1,0:T(8,128)S(1)} %get-tuple-element.46), channel_id=1, source_target_pairs={{8,16},{24,0},{16,8},{0,24},{9,17},{25,1},{17,9},{1,25},{10,18},{2... | collective-permute-start | bytes 589832 | tf_op jit(solution)/shard_map/ppermute | solution.py:388
  33.6 1.3 %collective-permute-start.18 = (f32[128,128]{1,0:T(8,128)S(1)}, f32[128,128]{1,0:T(8,128)S(1)}, u32[]{:S(2)}, u32[]{:S(2)}) collective-permute-start(f32[128,128]{1,0:T(8,128)S(1)} %get-tuple-element.55), channel_id=1, source_target_pairs={{0,1},{2,3},{4,5},{6,7},{1,0},{3,2},{5,4},{7,6},{8,9},{10,11},{12,... | collective-permute-start | bytes 196616 | tf_op jit(solution)/shard_map/ppermute | solution.py:388
  34.9 5.7 %collective-permute-start.11 = (f32[128,128]{1,0:T(8,128)S(1)}, f32[128,128]{1,0:T(8,128)S(1)}, u32[]{:S(2)}, u32[]{:S(2)}) collective-permute-start(f32[128,128]{1,0:T(8,128)S(1)} %get-tuple-element.47), channel_id=1, source_target_pairs={{1,2},{3,4},{5,6},{7,0},{2,1},{4,3},{6,5},{0,7},{9,10},{11,12},{13... | collective-permute-start | bytes 196616 | tf_op jit(solution)/shard_map/ppermute | solution.py:388
  37.6 5.3 %collective-permute-start.10 = (f32[128,128]{1,0:T(8,128)S(1)}, f32[128,128]{1,0:T(8,128)S(1)}, u32[]{:S(2)}, u32[]{:S(2)}) collective-permute-start(f32[128,128]{1,0:T(8,128)S(1)} %get-tuple-element.47), channel_id=1, source_target_pairs={{0,1},{2,3},{4,5},{6,7},{1,0},{3,2},{5,4},{7,6},{8,9},{10,11},{12,... | collective-permute-start | bytes 196616 | tf_op jit(solution)/shard_map/ppermute | solution.py:388
  40.5 13.9 %collective-permute-start.20 = (f32[384,128]{1,0:T(8,128)S(1)}, f32[384,128]{1,0:T(8,128)S(1)}, u32[]{:S(2)}, u32[]{:S(2)}) collective-permute-start(f32[384,128]{1,0:T(8,128)S(1)} %get-tuple-element.57), channel_id=1, source_target_pairs={{0,8},{16,24},{8,0},{24,16},{1,9},{17,25},{9,1},{25,17},{2,10},{18... | collective-permute-start | bytes 589832 | tf_op jit(solution)/shard_map/ppermute | solution.py:388
  40.6 14.5 %collective-permute-start.21 = (f32[384,128]{1,0:T(8,128)S(1)}, f32[384,128]{1,0:T(8,128)S(1)}, u32[]{:S(2)}, u32[]{:S(2)}) collective-permute-start(f32[384,128]{1,0:T(8,128)S(1)} %get-tuple-element.58), channel_id=1, source_target_pairs={{8,16},{24,0},{16,8},{0,24},{9,17},{25,1},{17,9},{1,25},{10,18},{2... | collective-permute-start | bytes 589832 | tf_op jit(solution)/shard_map/ppermute | solution.py:388
  42.9 8.4 %collective-permute-start.23 = (f32[128,128]{1,0:T(8,128)S(1)}, f32[128,128]{1,0:T(8,128)S(1)}, u32[]{:S(2)}, u32[]{:S(2)}) collective-permute-start(f32[128,128]{1,0:T(8,128)S(1)} %get-tuple-element.59), channel_id=1, source_target_pairs={{1,2},{3,4},{5,6},{7,0},{2,1},{4,3},{6,5},{0,7},{9,10},{11,12},{13... | collective-permute-start | bytes 196616 | tf_op jit(solution)/shard_map/ppermute | solution.py:388
  44.9 10.2 %copy-start.5 = (f32[10,256]{1,0:T(8,128)S(1)}, f32[10,256]{1,0:T(8,128)}, u32[]{:S(2)}) copy-start(f32[10,256]{1,0:T(8,128)} %refs_20_.1) | copy-start | bytes 30724
  44.9 10.2 %copy-start.7 = (f32[10,10]{1,0:T(8,128)S(1)}, f32[10,10]{1,0:T(8,128)}, u32[]{:S(2)}) copy-start(f32[10,10]{1,0:T(8,128)} %refs_19_.1) | copy-start | bytes 1204
  44.9 10.2 %copy-start.8 = (s32[256]{0:T(256)S(1)}, s32[256]{0:T(256)}, u32[]{:S(2)}) copy-start(s32[256]{0:T(256)} %param.15) | copy-start | bytes 3076
  44.9 10.2 %copy-start.9 = (s32[256]{0:T(256)S(1)}, s32[256]{0:T(256)}, u32[]{:S(2)}) copy-start(s32[256]{0:T(256)} %param.16) | copy-start | bytes 3076
  44.9 10.2 %copy-start.10 = (f32[256]{0:T(256)S(1)}, f32[256]{0:T(256)}, u32[]{:S(2)}) copy-start(f32[256]{0:T(256)} %param.19) | copy-start | bytes 3076
  47.8 12.0 %collective-permute-start.12 = (f32[384,128]{1,0:T(8,128)S(1)}, f32[384,128]{1,0:T(8,128)S(1)}, u32[]{:S(2)}, u32[]{:S(2)}) collective-permute-start(f32[384,128]{1,0:T(8,128)S(1)} %get-tuple-element.49), channel_id=1, source_target_pairs={{0,8},{16,24},{8,0},{24,16},{1,9},{17,25},{9,1},{25,17},{2,10},{18... | collective-permute-start | bytes 589832 | tf_op jit(solution)/shard_map/ppermute | solution.py:388
  48.0 13.4 %collective-permute-start.13 = (f32[384,128]{1,0:T(8,128)S(1)}, f32[384,128]{1,0:T(8,128)S(1)}, u32[]{:S(2)}, u32[]{:S(2)}) collective-permute-start(f32[384,128]{1,0:T(8,128)S(1)} %get-tuple-element.50), channel_id=1, source_target_pairs={{8,16},{24,0},{16,8},{0,24},{9,17},{25,1},{17,9},{1,25},{10,18},{2... | collective-permute-start | bytes 589832 | tf_op jit(solution)/shard_map/ppermute | solution.py:388
  51.4 1.3 %collective-permute-start.22 = (f32[128,128]{1,0:T(8,128)S(1)}, f32[128,128]{1,0:T(8,128)S(1)}, u32[]{:S(2)}, u32[]{:S(2)}) collective-permute-start(f32[128,128]{1,0:T(8,128)S(1)} %get-tuple-element.59), channel_id=1, source_target_pairs={{0,1},{2,3},{4,5},{6,7},{1,0},{3,2},{5,4},{7,6},{8,9},{10,11},{12,... | collective-permute-start | bytes 196616 | tf_op jit(solution)/shard_map/ppermute | solution.py:388
  52.6 7.1 %collective-permute-start.15 = (f32[128,128]{1,0:T(8,128)S(1)}, f32[128,128]{1,0:T(8,128)S(1)}, u32[]{:S(2)}, u32[]{:S(2)}) collective-permute-start(f32[128,128]{1,0:T(8,128)S(1)} %get-tuple-element.51), channel_id=1, source_target_pairs={{1,2},{3,4},{5,6},{7,0},{2,1},{4,3},{6,5},{0,7},{9,10},{11,12},{13... | collective-permute-start | bytes 196616 | tf_op jit(solution)/shard_map/ppermute | solution.py:388
  54.4 5.3 %collective-permute-start.14 = (f32[128,128]{1,0:T(8,128)S(1)}, f32[128,128]{1,0:T(8,128)S(1)}, u32[]{:S(2)}, u32[]{:S(2)}) collective-permute-start(f32[128,128]{1,0:T(8,128)S(1)} %get-tuple-element.51), channel_id=1, source_target_pairs={{0,1},{2,3},{4,5},{6,7},{1,0},{3,2},{5,4},{7,6},{8,9},{10,11},{12,... | collective-permute-start | bytes 196616 | tf_op jit(solution)/shard_map/ppermute | solution.py:388
  (3 other events, 18.7 us)

commit v2 on v1

--- a/solution.py
+++ b/solution.py
@@ -51,8 +51,11 @@
     return rolled(jnp.where(lane >= row.shape[1] + k, halo, row), -k)
 
 
-def even_index(axis):
-    return lax.rem(lax.axis_index(axis), 2) == 0
+AFTER_FIRST = {"gx": 1, "gy": 0}
+
+
+def after_in_a(axis):
+    return lax.rem(lax.axis_index(axis), 2) == AFTER_FIRST[axis]
 
 
 def first_rows_kernel(x_size, rows, levels, pieces, field, wind, to_a, to_b, field_here, wind_here, sems):
@@ -64,22 +67,22 @@
     copies.append(pltpu.make_async_copy(wind.at[pl.ds(0, levels * x_size), :], wind_here, sems.at[pieces]))
     for copy in copies:
         copy.start()
-    even = even_index("gx")
+    after = after_in_a("gx")
     for p in range(pieces):
         copies[p].wait()
         for t in range(p * rows // pieces // 8, (p + 1) * rows // pieces // 8):
             for j in range(WIDTH):
                 low = field_here[pl.ds(t * 8 * x_size + j, 8, stride=x_size), :]
                 high = field_here[pl.ds(t * 8 * x_size + x_size - WIDTH + j, 8, stride=x_size), :]
-                to_a[j * rows + t * 8 : j * rows + t * 8 + 8, :] = jnp.where(even, high, low)
-                to_b[j * rows + t * 8 : j * rows + t * 8 + 8, :] = jnp.where(even, low, high)
+                to_a[j * rows + t * 8 : j * rows + t * 8 + 8, :] = jnp.where(after, high, low)
+                to_b[j * rows + t * 8 : j * rows + t * 8 + 8, :] = jnp.where(after, low, high)
     copies[pieces].wait()
     for t in range(levels // 8):
         low = wind_here[pl.ds(t * 8 * x_size, 8, stride=x_size), :]
         high = wind_here[pl.ds(t * 8 * x_size + x_size - 1, 8, stride=x_size), :]
         at = WIDTH * rows + t * 8
-        to_a[at : at + 8, :] = jnp.where(even, high, low)
-        to_b[at : at + 8, :] = jnp.where(even, low, high)
+        to_a[at : at + 8, :] = jnp.where(after, high, low)
+        to_b[at : at + 8, :] = jnp.where(after, low, high)
 
 
 def extract_kernel(x_size, chunk, with_wind, field, *refs):
@@ -91,7 +94,7 @@
     if with_wind:
         levels = wind.shape[0] // (2 * x_size)
         rows = rows - levels
-    even = even_index("gx")
+    after = after_in_a("gx")
 
     def one(t, carry):
         base = pl.multiple_of((chunk * rows + t * 8) * x_size, 8 * x_size)
@@ -104,8 +107,8 @@
                 low = field[pl.ds(base + j, 8, stride=x_size), :]
                 high = field[pl.ds(base + x_size - WIDTH + j, 8, stride=x_size), :]
                 at = pl.ds(pl.multiple_of(j * rows + t * 8, 8), 8)
-                to_a[at, :] = jnp.where(even, high, low)
-                to_b[at, :] = jnp.where(even, low, high)
+                to_a[at, :] = jnp.where(after, high, low)
+                to_b[at, :] = jnp.where(after, low, high)
         return carry
 
     lax.fori_loop(0, rows // 8, one, 0, unroll=4)
@@ -122,16 +125,16 @@
         lax.fori_loop(0, levels // 8, one_wind, 0, unroll=4)
 
 
-def join_packs(even, from_a, from_b):
-    south = jnp.where(even, from_b, from_a)
-    north = jnp.where(even, from_a, from_b)
+def join_packs(after, from_a, from_b):
+    south = jnp.where(after, from_b, from_a)
+    north = jnp.where(after, from_a, from_b)
     return jnp.where((lane_index(south.shape) & (GROUP - 1)) < WIDTH, south, north)
 
 
 def wind_kernel(x_size, rows, wind, factor, pack_a, pack_b, *outs):
     speed_x, ahead_y, behind_y, edge_ahead, edge_behind, scales = outs
     levels = speed_x.shape[1]
-    even_y = even_index("gy")
+    after_y = after_in_a("gy")
     for x in range(x_size):
         mapped = factor[pl.ds(x, 1), :]
         for k, divisor in enumerate(DIVISORS):
@@ -148,7 +151,7 @@
         base = base + levels * x_size
         lane = lane_index(before.shape)
         there = pl.ds(pl.multiple_of(rows + t * 8, 8), 8)
-        halo = join_packs(even_y, pack_a[there, :], pack_b[there, :])
+        halo = join_packs(after_y, pack_a[there, :], pack_b[there, :])
         forward, backward = None, None
         for x in range(x_size):
             row = wind[pl.ds(base + x, 8, stride=x_size), :]
@@ -217,7 +220,7 @@
         out, to_a, to_b, packed = refs
     levels, y_size = edge_ahead.shape
     chunk_rows = base_ref.shape[0] // (CHUNKS * x_size)
-    even_x, even_y = even_index("gx"), even_index("gy")
+    after_x, after_y = after_in_a("gx"), after_in_a("gy")
 
     def block(g, carry):
         corner = pl.multiple_of((chunk * chunk_rows + g * levels) * x_size, levels * x_size)
@@ -234,7 +237,7 @@
                 product = stencil_product(halves, inner_matrix, slice(2 * pair * y_size, 2 * (pair + 1) * y_size))
                 for j, part in enumerate(parts[2 * pair : 2 * pair + 2]):
                     part[p * PIECE : (p + 1) * PIECE, :] = product[:, j * y_size : (j + 1) * y_size]
-        halo = join_packs(even_y, pack_a[pl.ds(here, levels), :], pack_b[pl.ds(here, levels), :])
+        halo = join_packs(after_y, pack_a[pl.ds(here, levels), :], pack_b[pl.ds(here, levels), :])
         product = stencil_product(split_halves(halo), edge_matrix)
         after, before = edge_ahead[...], edge_behind[...]
         share[...] = (
@@ -251,11 +254,11 @@
 
             def halo_rows(mine, other, j):
                 edge_at = pl.ds(pl.multiple_of(j * chunk_rows + here + t * 8, 8), 8)
-                return jnp.where(even_x, mine[edge_at, :], other[edge_at, :])
+                return jnp.where(after_x, mine[edge_at, :], other[edge_at, :])
 
             def outer_wind(mine, other):
                 wind_at = pl.ds(pl.multiple_of(WIDTH * chunk_rows + t * 8, 8), 8)
-                return jnp.where(even_x, mine[wind_at, :], other[wind_at, :])
+                return jnp.where(after_x, mine[wind_at, :], other[wind_at, :])
 
             def cell(x):
                 if x < 0:
@@ -312,8 +315,8 @@
                         if x >= x_size - WIDTH:
                             j = x - x_size + WIDTH
                             edge_at = pl.ds(pl.multiple_of(j * chunk_rows + here + t * 8, 8), 8)
-                            to_a[edge_at, :] = jnp.where(even_x, new, lows[j])
-                            to_b[edge_at, :] = jnp.where(even_x, lows[j], new)
+                            to_a[edge_at, :] = jnp.where(after_x, new, lows[j])
+                            to_b[edge_at, :] = jnp.where(after_x, lows[j], new)
                 flux_before = flux
                 q = q[1:]
             if not last:
@@ -382,9 +385,9 @@
 
 def exchange(axis, to_a, to_b):
     size = lax.axis_size(axis)
-    pairs_a = [(i, i + 1) for i in range(0, size, 2)]
-    pairs_b = [(i, (i + 1) % size) for i in range(1, size, 2)]
-    both = [pairs + [(j, i) for i, j in pairs] for pairs in (pairs_a, pairs_b)]
+    first = AFTER_FIRST[axis]
+    pairs = [[(i, (i + 1) % size) for i in range(start, size, 2)] for start in (first, 1 - first)]
+    both = [half + [(j, i) for i, j in half] for half in pairs]
     return lax.ppermute(to_a, axis, both[0]), lax.ppermute(to_b, axis, both[1])
 
 

time: 65 us -> 65.5 us (level)
  waiting for transfers between devices: 9.11 us -> 10.8 us
  starting transfers between devices: 28.2 us -> 27 us
    ppermute x12, starting transfers between devices: 22.9 us -> 11.1 us  [exchange(): lax.ppermute(to_b, axis, both[1])]
    ppermute x12, starting transfers between devices: 5.29 us -> 16 us  [exchange(): lax.ppermute(to_a, axis, both[0])]
    ppermute x12, waiting for transfers between devices: 6.58 us -> 8.62 us  [exchange(): lax.ppermute(to_b, axis, both[1])]
  transfers between devices with their start and end apart: 24 -> 24, of which waited for: 6 -> 7; matrix products, arithmetic and copies ran while one was open for 0% -> 0% of each run, Pallas kernels for 29% -> 29%
where the time goes in v2:
time: 65.5 us; the launch traced here: 65.3 us
  starting transfers between devices  27 us (41%)
  Pallas kernels  24.4 us (37%)
  waiting for transfers between devices  10.8 us (16%)
  local copies, waits for them, and re-layouts  1.64 us (3%)
  between operations  1.48 us (2%)
    pallas_call x6, Pallas kernels, per_device(): pl.pallas_call(functools.partial(section_kernel, x_size, k, c, last, city...  19.6 us
    ppermute x12, starting transfers between devices, exchange(): lax.ppermute(to_a, axis, both[0])  16 us
    ppermute x12, starting transfers between devices, exchange(): lax.ppermute(to_b, axis, both[1])  11.1 us
    ppermute x12, waiting for transfers between devices, exchange(): lax.ppermute(to_b, axis, both[1])  8.62 us
    pallas_call x1, Pallas kernels, per_device(): pl.pallas_call(functools.partial(first_rows_kernel, x_size, rows, levels,...  2.28 us
    ppermute x12, waiting for transfers between devices, exchange(): lax.ppermute(to_a, axis, both[0])  2.18 us
    unnamed x22, local copies, waits for them, and re-layouts  1.64 us
    pallas_call x2, Pallas kernels, per_device(): pl.pallas_call(functools.partial(extract_kernel, x_size, c, c == 0), in_s...  1.42 us
  transfers between devices with their start and end apart: 24, of which 7 were waited for; matrix products, arithmetic and copies ran while one was open for 0% of the time, Pallas kernels for 29%

profile of v2, /device:TPU:0, one launch (start us, length us, event | category | flops | bytes accessed | tf_op | source)
XLA Modules:
  0.0 65.3 jit_solution(3810157114573211094)
XLA Ops:
  0.6 2.3 %first_rows.1 = (f32[448,128]{1,0:T(8,128)}, f32[448,128]{1,0:T(8,128)}) custom-call(f32[4096,128]{1,0:T(8,128)} %bitcast.7, f32[2048,128]{1,0:T(8,128)} %bitcast.16), custom_call_target="tpu_custom_call" | custom-call | flops 1000 | bytes 1000 | tf_op jit(solution)/shard_map/first_rows/pallas_call | solution.py:419
  2.9 5.1 %collective-permute-start.4 = (f32[448,128]{1,0:T(8,128)}, f32[448,128]{1,0:T(8,128)S(1)}, u32[]{:S(2)}, u32[]{:S(2)}) collective-permute-start(f32[448,128]{1,0:T(8,128)} %get-tuple-element.36), channel_id=1, source_target_pairs={{8,16},{24,0},{16,8},{0,24},{9,17},{25,1},{17,9},{1,25},{10,18},{2... | collective-permute-start | bytes 688136 | tf_op jit(solution)/shard_map/ppermute | solution.py:391
  8.0 1.6 %copy-done = f32[4,64,16,128]{3,2,1,0:T(8,128)S(1)} copy-done((f32[4,64,16,128]{3,2,1,0:T(8,128)S(1)}, f32[4,64,16,128]{3,2,1,0:T(8,128)}, u32[]{:S(2)}) %copy-start) | copy-done | bytes 2097176
  9.6 0.8 %extract_0.1 = f32[192,128]{1,0:T(8,128)S(1)} custom-call(f32[4096,128]{1,0:T(8,128)S(1)} %bitcast.8, f32[2048,128]{1,0:T(8,128)S(1)} %bitcast.17), custom_call_target="tpu_custom_call" | custom-call | flops 1000 | bytes 1000 | tf_op jit(solution)/shard_map/extract_0/pallas_call | solution.py:437
  10.5 1.7 %collective-permute-start.7 = (f32[192,128]{1,0:T(8,128)S(1)}, f32[192,128]{1,0:T(8,128)S(1)}, u32[]{:S(2)}, u32[]{:S(2)}) collective-permute-start(f32[192,128]{1,0:T(8,128)S(1)} %extract_0.1), channel_id=1, source_target_pairs={{1,2},{3,4},{5,6},{7,0},{2,1},{4,3},{6,5},{0,7},{9,10},{11,12},{13... | collective-permute-start | bytes 294920 | tf_op jit(solution)/shard_map/ppermute | solution.py:391
  12.2 0.6 extract_1.1
  12.8 1.0 %collective-permute-start = (f32[384,128]{1,0:T(8,128)S(1)}, f32[384,128]{1,0:T(8,128)S(1)}, u32[]{:S(2)}, u32[]{:S(2)}) collective-permute-start(f32[384,128]{1,0:T(8,128)S(1)} %get-tuple-element.33), channel_id=1, source_target_pairs={{8,16},{24,0},{16,8},{0,24},{9,17},{25,1},{17,9},{1,25},{10,18},{2... | collective-permute-start | bytes 589832 | tf_op jit(solution)/shard_map/ppermute | solution.py:391
  13.7 2.7 %collective-permute-done.7.pack_b.refs_4_ = f32[192,128]{1,0:T(8,128)S(1)} collective-permute-done((f32[192,128]{1,0:T(8,128)S(1)}, f32[192,128]{1,0:T(8,128)S(1)}, u32[]{:S(2)}, u32[]{:S(2)}) %collective-permute-start.7) | collective-permute-done | bytes 98336 | tf_op jit(solution)/shard_map/ppermute | solution.py:391
  16.5 2.0 %collective-permute-start.1 = (f32[384,128]{1,0:T(8,128)S(1)}, f32[384,128]{1,0:T(8,128)S(1)}, u32[]{:S(2)}, u32[]{:S(2)}) collective-permute-start(f32[384,128]{1,0:T(8,128)S(1)} %get-tuple-element.34), channel_id=1, source_target_pairs={{0,8},{16,24},{8,0},{24,16},{1,9},{17,25},{9,1},{25,17},{2,10},{18... | collective-permute-start | bytes 589832 | tf_op jit(solution)/shard_map/ppermute | solution.py:391
  18.5 0.7 %collective-permute-start.3 = (f32[128,128]{1,0:T(8,128)S(1)}, f32[128,128]{1,0:T(8,128)S(1)}, u32[]{:S(2)}, u32[]{:S(2)}) collective-permute-start(f32[128,128]{1,0:T(8,128)S(1)} %get-tuple-element.35), channel_id=1, source_target_pairs={{1,2},{3,4},{5,6},{7,0},{2,1},{4,3},{6,5},{0,7},{9,10},{11,12},{13... | collective-permute-start | bytes 196616 | tf_op jit(solution)/shard_map/ppermute | solution.py:391
  19.3 1.1 %speeds.1 = (f32[17,64,128]{2,1,0:T(8,128)S(1)}, f32[16,64,128]{2,1,0:T(8,128)S(1)}, f32[16,64,128]{2,1,0:T(8,128)S(1)}, f32[64,128]{1,0:T(8,128)S(1)}, f32[64,1...) custom-call(f32[2048,128]{1,0:T(8,128)S(1)} %bitcast.18, f32[16,128]{1,0:T(8,128)S(1)} %copy-done.6, ...), custom_call_target="tpu_custom_call" | custom-call | flops 1000 | bytes 1000 | tf_op jit(solution)/shard_map/speeds/pallas_call | solution.py:450
  20.5 2.9 %section_0_0.1 = (f32[16,128,128]{2,1,0:T(8,128)S(1)}, f32[384,128]{1,0:T(8,128)S(1)}, f32[384,128]{1,0:T(8,128)S(1)}, f32[128,128]{1,0:T(8,128)S(1)}) custom-call(f32[4096,128]{1,0:T(8,128)S(1)} %bitcast.10, f32[448,128]{1,0:T(8,128)S(1)} %collective-permute-done.4.refs_5_.refs_6_.refs_1_, f32[448,128]{1,0:T(8,128)S(1)} %collective-permute-done.5.refs_6_.refs_7_.refs_2_, ...), custom_call_target="tpu_custom_call" | custom-call | flops 1000 | bytes 1000 | tf_op jit(solution)/shard_map/section_0_0/pallas_call | solution.py:507
  23.4 1.5 %collective-permute-start.16 = (f32[384,128]{1,0:T(8,128)S(1)}, f32[384,128]{1,0:T(8,128)S(1)}, u32[]{:S(2)}, u32[]{:S(2)}) collective-permute-start(f32[384,128]{1,0:T(8,128)S(1)} %get-tuple-element.53), channel_id=1, source_target_pairs={{8,16},{24,0},{16,8},{0,24},{9,17},{25,1},{17,9},{1,25},{10,18},{2... | collective-permute-start | bytes 589832 | tf_op jit(solution)/shard_map/ppermute | solution.py:391
  25.0 1.5 %collective-permute-start.19 = (f32[128,128]{1,0:T(8,128)S(1)}, f32[128,128]{1,0:T(8,128)S(1)}, u32[]{:S(2)}, u32[]{:S(2)}) collective-permute-start(f32[128,128]{1,0:T(8,128)S(1)} %get-tuple-element.55), channel_id=1, source_target_pairs={{1,2},{3,4},{5,6},{7,0},{2,1},{4,3},{6,5},{0,7},{9,10},{11,12},{13... | collective-permute-start | bytes 196616 | tf_op jit(solution)/shard_map/ppermute | solution.py:391
  26.5 1.1 %collective-permute-done.1.refs_2_ = f32[384,128]{1,0:T(8,128)S(1)} collective-permute-done((f32[384,128]{1,0:T(8,128)S(1)}, f32[384,128]{1,0:T(8,128)S(1)}, u32[]{:S(2)}, u32[]{:S(2)}) %collective-permute-start.1) | collective-permute-done | bytes 196640 | tf_op jit(solution)/shard_map/ppermute | solution.py:391
  27.6 2.9 %section_0_1.1 = (f32[16,128,128]{2,1,0:T(8,128)S(1)}, f32[384,128]{1,0:T(8,128)S(1)}, f32[384,128]{1,0:T(8,128)S(1)}, f32[128,128]{1,0:T(8,128)S(1)}) custom-call(f32[4096,128]{1,0:T(8,128)S(1)} %bitcast.11, f32[384,128]{1,0:T(8,128)S(1)} %collective-permute-done.refs_1_, f32[384,128]{1,0:T(8,128)S(1)} %collective-permute-done.1.refs_2_, ...), custom_call_target="tpu_custom_call" | custom-call | flops 1000 | bytes 1000 | tf_op jit(solution)/shard_map/section_0_1/pallas_call | solution.py:507
  30.5 1.4 %collective-permute-start.8 = (f32[384,128]{1,0:T(8,128)S(1)}, f32[384,128]{1,0:T(8,128)S(1)}, u32[]{:S(2)}, u32[]{:S(2)}) collective-permute-start(f32[384,128]{1,0:T(8,128)S(1)} %get-tuple-element.45), channel_id=1, source_target_pairs={{8,16},{24,0},{16,8},{0,24},{9,17},{25,1},{17,9},{1,25},{10,18},{2... | collective-permute-start | bytes 589832 | tf_op jit(solution)/shard_map/ppermute | solution.py:391
  32.0 1.2 %collective-permute-start.9 = (f32[384,128]{1,0:T(8,128)S(1)}, f32[384,128]{1,0:T(8,128)S(1)}, u32[]{:S(2)}, u32[]{:S(2)}) collective-permute-start(f32[384,128]{1,0:T(8,128)S(1)} %get-tuple-element.46), channel_id=1, source_target_pairs={{0,8},{16,24},{8,0},{24,16},{1,9},{17,25},{9,1},{25,17},{2,10},{18... | collective-permute-start | bytes 589832 | tf_op jit(solution)/shard_map/ppermute | solution.py:391
  33.2 1.3 %collective-permute-done.18.refs_4_ = f32[128,128]{1,0:T(8,128)S(1)} collective-permute-done((f32[128,128]{1,0:T(8,128)S(1)}, f32[128,128]{1,0:T(8,128)S(1)}, u32[]{:S(2)}, u32[]{:S(2)}) %collective-permute-start.18) | collective-permute-done | bytes 65568 | tf_op jit(solution)/shard_map/ppermute | solution.py:391
  34.4 2.2 %collective-permute-start.11 = (f32[128,128]{1,0:T(8,128)S(1)}, f32[128,128]{1,0:T(8,128)S(1)}, u32[]{:S(2)}, u32[]{:S(2)}) collective-permute-start(f32[128,128]{1,0:T(8,128)S(1)} %get-tuple-element.47), channel_id=1, source_target_pairs={{1,2},{3,4},{5,6},{7,0},{2,1},{4,3},{6,5},{0,7},{9,10},{11,12},{13... | collective-permute-start | bytes 196616 | tf_op jit(solution)/shard_map/ppermute | solution.py:391
  36.6 0.9 %collective-permute-done.17.refs_3_ = f32[384,128]{1,0:T(8,128)S(1)} collective-permute-done((f32[384,128]{1,0:T(8,128)S(1)}, f32[384,128]{1,0:T(8,128)S(1)}, u32[]{:S(2)}, u32[]{:S(2)}) %collective-permute-start.17) | collective-permute-done | bytes 196640 | tf_op jit(solution)/shard_map/ppermute | solution.py:391
  37.6 2.9 %section_1_0.1 = (f32[16,128,128]{2,1,0:T(8,128)S(1)}, f32[384,128]{1,0:T(8,128)S(1)}, f32[384,128]{1,0:T(8,128)S(1)}, f32[128,128]{1,0:T(8,128)S(1)}) custom-call(f32[16,128,128]{2,1,0:T(8,128)S(1)} %get-tuple-element.52.refs_0_, f32[4096,128]{1,0:T(8,128)S(1)} %bitcast.12, f32[384,128]{1,0:T(8,128)S(1)} %collective-permute-done.16.refs_2_, ...), custom_call_target="tpu_custom_call" | custom-call | flops 1000 | bytes 1000 | tf_op jit(solution)/shard_map/section_1_0/pallas_call | solution.py:507
  40.4 2.0 %collective-permute-start.20 = (f32[384,128]{1,0:T(8,128)S(1)}, f32[384,128]{1,0:T(8,128)S(1)}, u32[]{:S(2)}, u32[]{:S(2)}) collective-permute-start(f32[384,128]{1,0:T(8,128)S(1)} %get-tuple-element.57), channel_id=1, source_target_pairs={{8,16},{24,0},{16,8},{0,24},{9,17},{25,1},{17,9},{1,25},{10,18},{2... | collective-permute-start | bytes 589832 | tf_op jit(solution)/shard_map/ppermute | solution.py:391
  42.9 1.3 %collective-permute-done.9.refs_3_ = f32[384,128]{1,0:T(8,128)S(1)} collective-permute-done((f32[384,128]{1,0:T(8,128)S(1)}, f32[384,128]{1,0:T(8,128)S(1)}, u32[]{:S(2)}, u32[]{:S(2)}) %collective-permute-start.9) | collective-permute-done | bytes 196640 | tf_op jit(solution)/shard_map/ppermute | solution.py:391
  44.2 2.8 %section_1_1.1 = (f32[16,128,128]{2,1,0:T(8,128)S(1)}, f32[384,128]{1,0:T(8,128)S(1)}, f32[384,128]{1,0:T(8,128)S(1)}, f32[128,128]{1,0:T(8,128)S(1)}) custom-call(f32[16,128,128]{2,1,0:T(8,128)S(1)} %get-tuple-element.44.refs_0_, f32[4096,128]{1,0:T(8,128)S(1)} %bitcast.13, f32[384,128]{1,0:T(8,128)S(1)} %collective-permute-done.8.refs_2_, ...), custom_call_target="tpu_custom_call" | custom-call | flops 1000 | bytes 1000 | tf_op jit(solution)/shard_map/section_1_1/pallas_call | solution.py:507
  47.0 3.0 %collective-permute-start.12 = (f32[384,128]{1,0:T(8,128)S(1)}, f32[384,128]{1,0:T(8,128)S(1)}, u32[]{:S(2)}, u32[]{:S(2)}) collective-permute-start(f32[384,128]{1,0:T(8,128)S(1)} %get-tuple-element.49), channel_id=1, source_target_pairs={{8,16},{24,0},{16,8},{0,24},{9,17},{25,1},{17,9},{1,25},{10,18},{2... | collective-permute-start | bytes 589832 | tf_op jit(solution)/shard_map/ppermute | solution.py:391
  50.1 1.8 %collective-permute-start.22 = (f32[128,128]{1,0:T(8,128)S(1)}, f32[128,128]{1,0:T(8,128)S(1)}, u32[]{:S(2)}, u32[]{:S(2)}) collective-permute-start(f32[128,128]{1,0:T(8,128)S(1)} %get-tuple-element.59), channel_id=1, source_target_pairs={{0,1},{2,3},{4,5},{6,7},{1,0},{3,2},{5,4},{7,6},{8,9},{10,11},{12,... | collective-permute-start | bytes 196616 | tf_op jit(solution)/shard_map/ppermute | solution.py:391
  51.9 0.9 %collective-permute-done.22.refs_4_ = f32[128,128]{1,0:T(8,128)S(1)} collective-permute-done((f32[128,128]{1,0:T(8,128)S(1)}, f32[128,128]{1,0:T(8,128)S(1)}, u32[]{:S(2)}, u32[]{:S(2)}) %collective-permute-start.22) | collective-permute-done | bytes 65568 | tf_op jit(solution)/shard_map/ppermute | solution.py:391
  52.8 1.3 %collective-permute-start.15 = (f32[128,128]{1,0:T(8,128)S(1)}, f32[128,128]{1,0:T(8,128)S(1)}, u32[]{:S(2)}, u32[]{:S(2)}) collective-permute-start(f32[128,128]{1,0:T(8,128)S(1)} %get-tuple-element.51), channel_id=1, source_target_pairs={{1,2},{3,4},{5,6},{7,0},{2,1},{4,3},{6,5},{0,7},{9,10},{11,12},{13... | collective-permute-start | bytes 196616 | tf_op jit(solution)/shard_map/ppermute | solution.py:391
  54.8 4.6 %section_2_0.1 = (f32[4096,128]{1,0:T(8,128)}, f32[10,256]{1,0:T(8,128)}, f32[1,256]{1,0:T(1,128)}) custom-call(f32[16,128,128]{2,1,0:T(8,128)S(1)} %get-tuple-element.56.refs_0_, f32[4096,128]{1,0:T(8,128)S(1)} %bitcast.14, f32[384,128]{1,0:T(8,128)S(1)} %collective-permute-done.20.refs_2_, f32[384,128]{1,0:T(8,128)S(1)} %collective-permute-done.21.refs_3_, ...), custom_call_target="tpu_custom_call" | custom-call | flops 1000 | bytes 1000 | tf_op jit(solution)/shard_map/section_2_0/pallas_call | solution.py:507
  59.4 2.5 %collective-permute-done.13.refs_3_ = f32[384,128]{1,0:T(8,128)S(1)} collective-permute-done((f32[384,128]{1,0:T(8,128)S(1)}, f32[384,128]{1,0:T(8,128)S(1)}, u32[]{:S(2)}, u32[]{:S(2)}) %collective-permute-start.13) | collective-permute-done | bytes 196640 | tf_op jit(solution)/shard_map/ppermute | solution.py:391
  61.9 3.4 %section_2_1.1 = f32[4096,128]{1,0:T(8,128)} custom-call(f32[16,128,128]{2,1,0:T(8,128)S(1)} %get-tuple-element.48.refs_0_, f32[4096,128]{1,0:T(8,128)S(1)} %bitcast.15, f32[384,128]{1,0:T(8,128)S(1)} %collective-permute-done.12.refs_2_, f32[384,128]{1,0:T(8,128)S(1)} %collective-permute-done.13.refs_3_, ...), custom_call_target="tpu_custom_call", output_to_operand_aliasing={{}: (16, {})} | custom-call | flops 1000 | bytes 1000 | tf_op jit(solution)/shard_map/section_2_1/pallas_call | solution.py:507
  (48 shorter events, 0.6 us)
Async XLA Ops:
  2.9 17.5 %collective-permute-start.4 = (f32[448,128]{1,0:T(8,128)}, f32[448,128]{1,0:T(8,128)S(1)}, u32[]{:S(2)}, u32[]{:S(2)}) collective-permute-start(f32[448,128]{1,0:T(8,128)} %get-tuple-element.36), channel_id=1, source_target_pairs={{8,16},{24,0},{16,8},{0,24},{9,17},{25,1},{17,9},{1,25},{10,18},{2... | collective-permute-start | bytes 688136 | tf_op jit(solution)/shard_map/ppermute | solution.py:391
  8.0 12.4 %collective-permute-start.5 = (f32[448,128]{1,0:T(8,128)}, f32[448,128]{1,0:T(8,128)S(1)}, u32[]{:S(2)}, u32[]{:S(2)}) collective-permute-start(f32[448,128]{1,0:T(8,128)} %get-tuple-element.37), channel_id=1, source_target_pairs={{0,8},{16,24},{8,0},{24,16},{1,9},{17,25},{9,1},{25,17},{2,10},{18... | collective-permute-start | bytes 688136 | tf_op jit(solution)/shard_map/ppermute | solution.py:391
  10.5 10.0 %copy-start.1 = (f32[4,64,16,128]{3,2,1,0:T(8,128)S(1)}, f32[4,64,16,128]{3,2,1,0:T(8,128)}, u32[]{:S(2)}) copy-start(f32[4,64,16,128]{3,2,1,0:T(8,128)} %param.11) | copy-start | bytes 6291460
  10.5 10.0 %copy-start.3 = (bf16[256,512]{1,0:T(8,128)(2,1)S(1)}, bf16[256,512]{1,0:T(8,128)(2,1)}, u32[]{:S(2)}) copy-start(bf16[256,512]{1,0:T(8,128)(2,1)} %constant.5.clone.refs_14_.refs_15_) | copy-start | bytes 786436
  10.5 10.0 %copy-start.4 = (bf16[256,512]{1,0:T(8,128)(2,1)S(1)}, bf16[256,512]{1,0:T(8,128)(2,1)}, u32[]{:S(2)}) copy-start(bf16[256,512]{1,0:T(8,128)(2,1)} %constant.4.clone.refs_13_.refs_14_) | copy-start | bytes 786436
  10.5 6.0 %collective-permute-start.7 = (f32[192,128]{1,0:T(8,128)S(1)}, f32[192,128]{1,0:T(8,128)S(1)}, u32[]{:S(2)}, u32[]{:S(2)}) collective-permute-start(f32[192,128]{1,0:T(8,128)S(1)} %extract_0.1), channel_id=1, source_target_pairs={{1,2},{3,4},{5,6},{7,0},{2,1},{4,3},{6,5},{0,7},{9,10},{11,12},{13... | collective-permute-start | bytes 294920 | tf_op jit(solution)/shard_map/ppermute | solution.py:391
  12.2 6.3 %collective-permute-start.6 = (f32[192,128]{1,0:T(8,128)S(1)}, f32[192,128]{1,0:T(8,128)S(1)}, u32[]{:S(2)}, u32[]{:S(2)}) collective-permute-start(f32[192,128]{1,0:T(8,128)S(1)} %extract_0.1), channel_id=1, source_target_pairs={{0,1},{2,3},{4,5},{6,7},{1,0},{3,2},{5,4},{7,6},{8,9},{10,11},{12,... | collective-permute-start | bytes 294920 | tf_op jit(solution)/shard_map/ppermute | solution.py:391
  12.8 13.7 %collective-permute-start = (f32[384,128]{1,0:T(8,128)S(1)}, f32[384,128]{1,0:T(8,128)S(1)}, u32[]{:S(2)}, u32[]{:S(2)}) collective-permute-start(f32[384,128]{1,0:T(8,128)S(1)} %get-tuple-element.33), channel_id=1, source_target_pairs={{8,16},{24,0},{16,8},{0,24},{9,17},{25,1},{17,9},{1,25},{10,18},{2... | collective-permute-start | bytes 589832 | tf_op jit(solution)/shard_map/ppermute | solution.py:391
  16.5 11.2 %collective-permute-start.1 = (f32[384,128]{1,0:T(8,128)S(1)}, f32[384,128]{1,0:T(8,128)S(1)}, u32[]{:S(2)}, u32[]{:S(2)}) collective-permute-start(f32[384,128]{1,0:T(8,128)S(1)} %get-tuple-element.34), channel_id=1, source_target_pairs={{0,8},{16,24},{8,0},{24,16},{1,9},{17,25},{9,1},{25,17},{2,10},{18... | collective-permute-start | bytes 589832 | tf_op jit(solution)/shard_map/ppermute | solution.py:391
  18.5 6.5 %collective-permute-start.3 = (f32[128,128]{1,0:T(8,128)S(1)}, f32[128,128]{1,0:T(8,128)S(1)}, u32[]{:S(2)}, u32[]{:S(2)}) collective-permute-start(f32[128,128]{1,0:T(8,128)S(1)} %get-tuple-element.35), channel_id=1, source_target_pairs={{1,2},{3,4},{5,6},{7,0},{2,1},{4,3},{6,5},{0,7},{9,10},{11,12},{13... | collective-permute-start | bytes 196616 | tf_op jit(solution)/shard_map/ppermute | solution.py:391
  20.4 4.6 %collective-permute-start.2 = (f32[128,128]{1,0:T(8,128)S(1)}, f32[128,128]{1,0:T(8,128)S(1)}, u32[]{:S(2)}, u32[]{:S(2)}) collective-permute-start(f32[128,128]{1,0:T(8,128)S(1)} %get-tuple-element.35), channel_id=1, source_target_pairs={{0,1},{2,3},{4,5},{6,7},{1,0},{3,2},{5,4},{7,6},{8,9},{10,11},{12,... | collective-permute-start | bytes 196616 | tf_op jit(solution)/shard_map/ppermute | solution.py:391
  23.4 13.2 %collective-permute-start.16 = (f32[384,128]{1,0:T(8,128)S(1)}, f32[384,128]{1,0:T(8,128)S(1)}, u32[]{:S(2)}, u32[]{:S(2)}) collective-permute-start(f32[384,128]{1,0:T(8,128)S(1)} %get-tuple-element.53), channel_id=1, source_target_pairs={{8,16},{24,0},{16,8},{0,24},{9,17},{25,1},{17,9},{1,25},{10,18},{2... | collective-permute-start | bytes 589832 | tf_op jit(solution)/shard_map/ppermute | solution.py:391
  25.0 12.6 %collective-permute-start.17 = (f32[384,128]{1,0:T(8,128)S(1)}, f32[384,128]{1,0:T(8,128)S(1)}, u32[]{:S(2)}, u32[]{:S(2)}) collective-permute-start(f32[384,128]{1,0:T(8,128)S(1)} %get-tuple-element.54), channel_id=1, source_target_pairs={{0,8},{16,24},{8,0},{24,16},{1,9},{17,25},{9,1},{25,17},{2,10},{18... | collective-permute-start | bytes 589832 | tf_op jit(solution)/shard_map/ppermute | solution.py:391
  25.0 8.2 %collective-permute-start.19 = (f32[128,128]{1,0:T(8,128)S(1)}, f32[128,128]{1,0:T(8,128)S(1)}, u32[]{:S(2)}, u32[]{:S(2)}) collective-permute-start(f32[128,128]{1,0:T(8,128)S(1)} %get-tuple-element.55), channel_id=1, source_target_pairs={{1,2},{3,4},{5,6},{7,0},{2,1},{4,3},{6,5},{0,7},{9,10},{11,12},{13... | collective-permute-start | bytes 196616 | tf_op jit(solution)/shard_map/ppermute | solution.py:391
  30.5 12.3 %collective-permute-start.8 = (f32[384,128]{1,0:T(8,128)S(1)}, f32[384,128]{1,0:T(8,128)S(1)}, u32[]{:S(2)}, u32[]{:S(2)}) collective-permute-start(f32[384,128]{1,0:T(8,128)S(1)} %get-tuple-element.45), channel_id=1, source_target_pairs={{8,16},{24,0},{16,8},{0,24},{9,17},{25,1},{17,9},{1,25},{10,18},{2... | collective-permute-start | bytes 589832 | tf_op jit(solution)/shard_map/ppermute | solution.py:391
  32.0 12.2 %collective-permute-start.9 = (f32[384,128]{1,0:T(8,128)S(1)}, f32[384,128]{1,0:T(8,128)S(1)}, u32[]{:S(2)}, u32[]{:S(2)}) collective-permute-start(f32[384,128]{1,0:T(8,128)S(1)} %get-tuple-element.46), channel_id=1, source_target_pairs={{0,8},{16,24},{8,0},{24,16},{1,9},{17,25},{9,1},{25,17},{2,10},{18... | collective-permute-start | bytes 589832 | tf_op jit(solution)/shard_map/ppermute | solution.py:391
  33.2 1.3 %collective-permute-start.18 = (f32[128,128]{1,0:T(8,128)S(1)}, f32[128,128]{1,0:T(8,128)S(1)}, u32[]{:S(2)}, u32[]{:S(2)}) collective-permute-start(f32[128,128]{1,0:T(8,128)S(1)} %get-tuple-element.55), channel_id=1, source_target_pairs={{0,1},{2,3},{4,5},{6,7},{1,0},{3,2},{5,4},{7,6},{8,9},{10,11},{12,... | collective-permute-start | bytes 196616 | tf_op jit(solution)/shard_map/ppermute | solution.py:391
  34.4 8.0 %collective-permute-start.11 = (f32[128,128]{1,0:T(8,128)S(1)}, f32[128,128]{1,0:T(8,128)S(1)}, u32[]{:S(2)}, u32[]{:S(2)}) collective-permute-start(f32[128,128]{1,0:T(8,128)S(1)} %get-tuple-element.47), channel_id=1, source_target_pairs={{1,2},{3,4},{5,6},{7,0},{2,1},{4,3},{6,5},{0,7},{9,10},{11,12},{13... | collective-permute-start | bytes 196616 | tf_op jit(solution)/shard_map/ppermute | solution.py:391
  36.6 5.8 %collective-permute-start.10 = (f32[128,128]{1,0:T(8,128)S(1)}, f32[128,128]{1,0:T(8,128)S(1)}, u32[]{:S(2)}, u32[]{:S(2)}) collective-permute-start(f32[128,128]{1,0:T(8,128)S(1)} %get-tuple-element.47), channel_id=1, source_target_pairs={{0,1},{2,3},{4,5},{6,7},{1,0},{3,2},{5,4},{7,6},{8,9},{10,11},{12,... | collective-permute-start | bytes 196616 | tf_op jit(solution)/shard_map/ppermute | solution.py:391
  40.4 13.6 %collective-permute-start.20 = (f32[384,128]{1,0:T(8,128)S(1)}, f32[384,128]{1,0:T(8,128)S(1)}, u32[]{:S(2)}, u32[]{:S(2)}) collective-permute-start(f32[384,128]{1,0:T(8,128)S(1)} %get-tuple-element.57), channel_id=1, source_target_pairs={{8,16},{24,0},{16,8},{0,24},{9,17},{25,1},{17,9},{1,25},{10,18},{2... | collective-permute-start | bytes 589832 | tf_op jit(solution)/shard_map/ppermute | solution.py:391
  42.4 12.3 %collective-permute-start.21 = (f32[384,128]{1,0:T(8,128)S(1)}, f32[384,128]{1,0:T(8,128)S(1)}, u32[]{:S(2)}, u32[]{:S(2)}) collective-permute-start(f32[384,128]{1,0:T(8,128)S(1)} %get-tuple-element.58), channel_id=1, source_target_pairs={{0,8},{16,24},{8,0},{24,16},{1,9},{17,25},{9,1},{25,17},{2,10},{18... | collective-permute-start | bytes 589832 | tf_op jit(solution)/shard_map/ppermute | solution.py:391
  42.4 7.6 %collective-permute-start.23 = (f32[128,128]{1,0:T(8,128)S(1)}, f32[128,128]{1,0:T(8,128)S(1)}, u32[]{:S(2)}, u32[]{:S(2)}) collective-permute-start(f32[128,128]{1,0:T(8,128)S(1)} %get-tuple-element.59), channel_id=1, source_target_pairs={{1,2},{3,4},{5,6},{7,0},{2,1},{4,3},{6,5},{0,7},{9,10},{11,12},{13... | collective-permute-start | bytes 196616 | tf_op jit(solution)/shard_map/ppermute | solution.py:391
  44.2 10.6 %copy-start.5 = (f32[10,256]{1,0:T(8,128)S(1)}, f32[10,256]{1,0:T(8,128)}, u32[]{:S(2)}) copy-start(f32[10,256]{1,0:T(8,128)} %refs_20_.1) | copy-start | bytes 30724
  44.2 10.6 %copy-start.7 = (f32[10,10]{1,0:T(8,128)S(1)}, f32[10,10]{1,0:T(8,128)}, u32[]{:S(2)}) copy-start(f32[10,10]{1,0:T(8,128)} %refs_19_.1) | copy-start | bytes 1204
  44.2 10.6 %copy-start.8 = (s32[256]{0:T(256)S(1)}, s32[256]{0:T(256)}, u32[]{:S(2)}) copy-start(s32[256]{0:T(256)} %param.15) | copy-start | bytes 3076
  44.2 10.6 %copy-start.9 = (s32[256]{0:T(256)S(1)}, s32[256]{0:T(256)}, u32[]{:S(2)}) copy-start(s32[256]{0:T(256)} %param.16) | copy-start | bytes 3076
  44.2 10.6 %copy-start.10 = (f32[256]{0:T(256)S(1)}, f32[256]{0:T(256)}, u32[]{:S(2)}) copy-start(f32[256]{0:T(256)} %param.19) | copy-start | bytes 3076
  47.0 12.4 %collective-permute-start.12 = (f32[384,128]{1,0:T(8,128)S(1)}, f32[384,128]{1,0:T(8,128)S(1)}, u32[]{:S(2)}, u32[]{:S(2)}) collective-permute-start(f32[384,128]{1,0:T(8,128)S(1)} %get-tuple-element.49), channel_id=1, source_target_pairs={{8,16},{24,0},{16,8},{0,24},{9,17},{25,1},{17,9},{1,25},{10,18},{2... | collective-permute-start | bytes 589832 | tf_op jit(solution)/shard_map/ppermute | solution.py:391
  50.1 11.9 %collective-permute-start.13 = (f32[384,128]{1,0:T(8,128)S(1)}, f32[384,128]{1,0:T(8,128)S(1)}, u32[]{:S(2)}, u32[]{:S(2)}) collective-permute-start(f32[384,128]{1,0:T(8,128)S(1)} %get-tuple-element.50), channel_id=1, source_target_pairs={{0,8},{16,24},{8,0},{24,16},{1,9},{17,25},{9,1},{25,17},{2,10},{18... | collective-permute-start | bytes 589832 | tf_op jit(solution)/shard_map/ppermute | solution.py:391
  50.1 2.7 %collective-permute-start.22 = (f32[128,128]{1,0:T(8,128)S(1)}, f32[128,128]{1,0:T(8,128)S(1)}, u32[]{:S(2)}, u32[]{:S(2)}) collective-permute-start(f32[128,128]{1,0:T(8,128)S(1)} %get-tuple-element.59), channel_id=1, source_target_pairs={{0,1},{2,3},{4,5},{6,7},{1,0},{3,2},{5,4},{7,6},{8,9},{10,11},{12,... | collective-permute-start | bytes 196616 | tf_op jit(solution)/shard_map/ppermute | solution.py:391
  52.8 6.6 %collective-permute-start.15 = (f32[128,128]{1,0:T(8,128)S(1)}, f32[128,128]{1,0:T(8,128)S(1)}, u32[]{:S(2)}, u32[]{:S(2)}) collective-permute-start(f32[128,128]{1,0:T(8,128)S(1)} %get-tuple-element.51), channel_id=1, source_target_pairs={{1,2},{3,4},{5,6},{7,0},{2,1},{4,3},{6,5},{0,7},{9,10},{11,12},{13... | collective-permute-start | bytes 196616 | tf_op jit(solution)/shard_map/ppermute | solution.py:391
  54.1 5.3 %collective-permute-start.14 = (f32[128,128]{1,0:T(8,128)S(1)}, f32[128,128]{1,0:T(8,128)S(1)}, u32[]{:S(2)}, u32[]{:S(2)}) collective-permute-start(f32[128,128]{1,0:T(8,128)S(1)} %get-tuple-element.51), channel_id=1, source_target_pairs={{0,1},{2,3},{4,5},{6,7},{1,0},{3,2},{5,4},{7,6},{8,9},{10,11},{12,... | collective-permute-start | bytes 196616 | tf_op jit(solution)/shard_map/ppermute | solution.py:391
  (3 other events, 18.6 us)

commit v3 on v1

--- a/solution.py
+++ b/solution.py
@@ -194,7 +194,77 @@
     return jnp.dot(halves, matrix[:, columns], preferred_element_type=jnp.float32)
 
 
-def section_kernel(x_size, k, chunk, last, with_city, *refs):
+def linear_parts(
+    x_size, first, section, corner, here, levels, pack_a, pack_b, after_y, edge_ahead, edge_behind,
+    inner_matrix, edge_matrix, share, parts,
+):
+    y_size = section.shape[-1]
+    for p in range(levels * x_size // PIECE):
+        n = PIECE // levels
+        if first:
+            lines = [section[pl.ds(corner + x, levels, stride=x_size), :] for x in range(p * n, (p + 1) * n)]
+            values = jnp.concatenate(lines, axis=0)
+        else:
+            values = section[p * n : (p + 1) * n, pl.ds(here, levels), :].reshape(PIECE, y_size)
+        halves = split_halves(values)
+        for pair in range(2):
+            product = stencil_product(halves, inner_matrix, slice(2 * pair * y_size, 2 * (pair + 1) * y_size))
+            for j, part in enumerate(parts[2 * pair : 2 * pair + 2]):
+                part[p * PIECE : (p + 1) * PIECE, :] = product[:, j * y_size : (j + 1) * y_size]
+    halo = join_packs(after_y, pack_a[pl.ds(here, levels), :], pack_b[pl.ds(here, levels), :])
+    product = stencil_product(split_halves(halo), edge_matrix)
+    after, before = edge_ahead[...], edge_behind[...]
+    share[...] = (
+        after * product[:, :y_size]
+        - jnp.abs(after) * product[:, y_size : 2 * y_size]
+        - before * product[:, 2 * y_size : 3 * y_size]
+        + jnp.abs(before) * product[:, 3 * y_size :]
+    )
+
+
+def south_north(x, at, edge_share, edge_lane, levels, ahead_y, behind_y, parts):
+    lines = [part[pl.ds(pl.multiple_of(x * levels, levels) + at.start, 8), :] for part in parts]
+    after, before = ahead_y[x, at, :], behind_y[x, at, :]
+    moved = rolled(edge_share, -(GROUP * x + WIDTH))
+    return (
+        (after * lines[0] - jnp.abs(after) * lines[1])
+        - (before * lines[2] - jnp.abs(before) * lines[3])
+        + jnp.where(edge_lane, moved, 0.0)
+    )
+
+
+def south_north_kernel(
+    section, pack_a, pack_b, ahead_y, behind_y, edge_ahead, edge_behind, inner_matrix, edge_matrix, out, share, *parts
+):
+    x_size, chunk_rows, y_size = section.shape
+    levels = edge_ahead.shape[0]
+    after_y = even_index("gy")
+
+    def block(g, carry):
+        here = pl.multiple_of(g * levels, levels)
+        linear_parts(
+            x_size, False, section, None, here, levels, pack_a, pack_b, after_y, edge_ahead, edge_behind,
+            inner_matrix, edge_matrix, share, parts,
+        )
+
+        def one(t, carry):
+            at = pl.ds(pl.multiple_of(t * 8, 8), 8)
+            lane = lane_index((8, y_size))
+            edge_lane = (lane < WIDTH) | (lane >= y_size - WIDTH)
+            edge_share = share[at, :]
+            for x in range(x_size):
+                out[x, pl.ds(pl.multiple_of(here + t * 8, 8), 8), :] = south_north(
+                    x, at, edge_share, edge_lane, levels, ahead_y, behind_y, parts
+                )
+            return carry
+
+        lax.fori_loop(0, levels // 8, one, 0, unroll=UNROLL)
+        return carry
+
+    lax.fori_loop(0, chunk_rows // levels, block, 0)
+
+
+def section_kernel(x_size, k, chunk, last, with_city, split, *refs):
     refs = list(refs)
     first = k == 0
     section = refs.pop(0)
@@ -203,9 +273,12 @@
     wind_a, wind_b = [refs.pop(0) for _ in range(2)]
     speed_x, ahead_y, behind_y, edge_ahead, edge_behind, scales = [refs.pop(0) for _ in range(6)]
     inner_matrix, edge_matrix = [refs.pop(0) for _ in range(2)]
-    parts = refs[-4:]
-    share = refs[-5]
-    refs = refs[:-5]
+    if split:
+        turned = refs.pop(0)
+    else:
+        parts = refs[-4:]
+        share = refs[-5]
+        refs = refs[:-5]
     if last:
         if with_city:
             city = [refs.pop(0) for _ in range(6)]
@@ -217,32 +290,16 @@
         out, to_a, to_b, packed = refs
     levels, y_size = edge_ahead.shape
     chunk_rows = base_ref.shape[0] // (CHUNKS * x_size)
-    even_x, even_y = even_index("gx"), even_index("gy")
+    even_x, after_y = even_index("gx"), even_index("gy")
 
     def block(g, carry):
         corner = pl.multiple_of((chunk * chunk_rows + g * levels) * x_size, levels * x_size)
         here = pl.multiple_of(g * levels, levels)
-        for p in range(levels * x_size // PIECE):
-            n = PIECE // levels
-            if first:
-                lines = [section[pl.ds(corner + x, levels, stride=x_size), :] for x in range(p * n, (p + 1) * n)]
-                values = jnp.concatenate(lines, axis=0)
-            else:
-                values = section[p * n : (p + 1) * n, pl.ds(here, levels), :].reshape(PIECE, y_size)
-            halves = split_halves(values)
-            for pair in range(2):
-                product = stencil_product(halves, inner_matrix, slice(2 * pair * y_size, 2 * (pair + 1) * y_size))
-                for j, part in enumerate(parts[2 * pair : 2 * pair + 2]):
-                    part[p * PIECE : (p + 1) * PIECE, :] = product[:, j * y_size : (j + 1) * y_size]
-        halo = join_packs(even_y, pack_a[pl.ds(here, levels), :], pack_b[pl.ds(here, levels), :])
-        product = stencil_product(split_halves(halo), edge_matrix)
-        after, before = edge_ahead[...], edge_behind[...]
-        share[...] = (
-            after * product[:, :y_size]
-            - jnp.abs(after) * product[:, y_size : 2 * y_size]
-            - before * product[:, 2 * y_size : 3 * y_size]
-            + jnp.abs(before) * product[:, 3 * y_size :]
-        )
+        if not split:
+            linear_parts(
+                x_size, first, section, corner, here, levels, pack_a, pack_b, after_y, edge_ahead, edge_behind,
+                inner_matrix, edge_matrix, share, parts,
+            )
 
         def one(t, carry):
             at = pl.ds(pl.multiple_of(t * 8, 8), 8)
@@ -266,7 +323,7 @@
 
             lane = lane_index((8, y_size))
             edge_lane = (lane < WIDTH) | (lane >= y_size - WIDTH)
-            edge_share = share[at, :]
+            edge_share = None if split else share[at, :]
             q = [cell(x) for x in range(-3, 2)]
             d1 = [q[i + 1] - q[i] for i in range(4)]
             d2 = [d1[i + 1] - d1[i] for i in range(3)]
@@ -291,15 +348,11 @@
                 flux = speed * (smooth + new_smooth) - jnp.abs(speed) * (new4 - d4)
                 d1, d2, d3, d4, smooth = new1, new2, new3, new4, new_smooth
                 if x >= 0:
-                    lines = [part[pl.ds(pl.multiple_of(x * levels + t * 8, 8), 8), :] for part in parts]
-                    after, before = ahead_y[x, at, :], behind_y[x, at, :]
-                    moved = rolled(edge_share, -(GROUP * x + WIDTH))
-                    divergence = (
-                        (flux - flux_before)
-                        + (after * lines[0] - jnp.abs(after) * lines[1])
-                        - (before * lines[2] - jnp.abs(before) * lines[3])
-                        + jnp.where(edge_lane, moved, 0.0)
-                    )
+                    if split:
+                        turn = turned[x, rows_at, :]
+                    else:
+                        turn = south_north(x, at, edge_share, edge_lane, levels, ahead_y, behind_y, parts)
+                    divergence = (flux - flux_before) + turn
                     base = base_ref[pl.ds(start + x, 8, stride=x_size), :]
                     new = base + scales[k, x] * divergence
                     if last:
@@ -473,6 +526,23 @@
             operands += [*received[c], *winds_beyond, *speeds, *matrices]
             specs = [whole] * len(operands)
             city = last and c == 0
+            split = last and c == CHUNKS - 1
+            scratch = [pltpu.VMEM((levels, y_size), jnp.float32)]
+            scratch += [pltpu.VMEM((levels * x_size, y_size), jnp.float32)] * 4
+            if split:
+                turned = pl.pallas_call(
+                    south_north_kernel,
+                    in_specs=[whole] * 9,
+                    out_specs=whole,
+                    out_shape=f32((x_size, rows, y_size)),
+                    scratch_shapes=scratch,
+                    compiler_params=params,
+                    cost_estimate=cheap,
+                    name="south_north",
+                )(sections[c], *received[c][2:], *speeds[1:5], *matrices)
+                operands += [turned]
+                specs += [whole]
+                scratch = []
             aliases = {}
             flat_c = pl.BlockSpec((levels * x_size, y_size), lambda g, c=c: (c * steps + g, 0))
             if city:
@@ -502,13 +572,12 @@
                     f32((rows, y_size)),
                 ]
             outs = pl.pallas_call(
-                functools.partial(section_kernel, x_size, k, c, last, city),
+                functools.partial(section_kernel, x_size, k, c, last, city, split),
                 grid=(steps,) if last else (),
                 in_specs=specs,
                 out_specs=out_specs,
                 out_shape=out_shape,
-                scratch_shapes=[pltpu.VMEM((levels, y_size), jnp.float32)]
-                + [pltpu.VMEM((levels * x_size, y_size), jnp.float32)] * 4,
+                scratch_shapes=scratch,
                 input_output_aliases=aliases,
                 compiler_params=params,
                 cost_estimate=cheap,

time: 65 us -> 83.9 us (1.29)
  waiting for transfers between devices: 9.11 us -> 23.3 us
  local copies, waits for them, and re-layouts: 1.64 us -> 5.79 us
    ppermute x12, waiting for transfers between devices: 2.53 us -> 12.3 us  [exchange(): lax.ppermute(to_a, axis, both[0])]
    ppermute x12, waiting for transfers between devices: 6.58 us -> 11 us  [exchange(): lax.ppermute(to_b, axis, both[1])]
    unnamed x22 -> x30, local copies, waits for them, and re-layouts: 1.64 us -> 5.79 us
    ppermute x12, starting transfers between devices: 5.29 us -> 8.2 us  [exchange(): lax.ppermute(to_a, axis, both[0])]
    ppermute x12, starting transfers between devices: 22.9 us -> 20.3 us  [exchange(): lax.ppermute(to_b, axis, both[1])]
    pallas_call x0 -> x1, Pallas kernels: none -> 1.91 us  [per_device(): pl.pallas_call(south_north_kernel, in_specs=[whole] * 9, out_specs=whole,...]
    pallas_call x6, Pallas kernels: 19.6 us -> 17.9 us  [per_device(): pl.pallas_call(functools.partial(section_kernel, x_size, k, c, last, city...]
  transfers between devices with their start and end apart: 24 -> 24, of which waited for: 6 -> 7; matrix products, arithmetic and copies ran while one was open for 0% -> 0% of each run, Pallas kernels for 29% -> 23%
where the time goes in v3:
time: 83.9 us; the launch traced here: 83.7 us
  starting transfers between devices  28.5 us (34%)
  Pallas kernels  24.6 us (29%)
  waiting for transfers between devices  23.3 us (28%)
  local copies, waits for them, and re-layouts  5.79 us (7%)
  between operations  1.51 us (2%)
    ppermute x12, starting transfers between devices, exchange(): lax.ppermute(to_b, axis, both[1])  20.3 us
    pallas_call x6, Pallas kernels, per_device(): pl.pallas_call(functools.partial(section_kernel, x_size, k, c, last, city...  17.9 us
    ppermute x12, waiting for transfers between devices, exchange(): lax.ppermute(to_a, axis, both[0])  12.3 us
    ppermute x12, waiting for transfers between devices, exchange(): lax.ppermute(to_b, axis, both[1])  11 us
    ppermute x12, starting transfers between devices, exchange(): lax.ppermute(to_a, axis, both[0])  8.2 us
    unnamed x30, local copies, waits for them, and re-layouts  5.79 us
    pallas_call x1, Pallas kernels, per_device(): pl.pallas_call(functools.partial(first_rows_kernel, x_size, rows, levels,...  2.23 us
    pallas_call x1, Pallas kernels, per_device(): pl.pallas_call(south_north_kernel, in_specs=[whole] * 9, out_specs=whole,...  1.91 us
  transfers between devices with their start and end apart: 24, of which 7 were waited for; matrix products, arithmetic and copies ran while one was open for 0% of the time, Pallas kernels for 23%

profile of v3, /device:TPU:0, one launch (start us, length us, event | category | flops | bytes accessed | tf_op | source)
XLA Modules:
  0.0 83.7 jit_solution(13094072755286549261)
XLA Ops:
  0.6 1.6 %copy-done = f32[4,64,16,128]{3,2,1,0:T(8,128)S(1)} copy-done((f32[4,64,16,128]{3,2,1,0:T(8,128)S(1)}, f32[4,64,16,128]{3,2,1,0:T(8,128)}, u32[]{:S(2)}) %copy-start) | copy-done | bytes 2097176
  2.2 1.2 %copy-done.5 = f32[2,64,16,128]{3,2,1,0:T(8,128)S(1)} copy-done((f32[2,64,16,128]{3,2,1,0:T(8,128)S(1)}, f32[2,64,16,128]{3,2,1,0:T(8,128)}, u32[]{:S(2)}) %copy-start.5) | copy-done | bytes 1048600
  4.3 3.4 %collective-permute-start.7 = (f32[192,128]{1,0:T(8,128)S(1)}, f32[192,128]{1,0:T(8,128)S(1)}, u32[]{:S(2)}, u32[]{:S(2)}) collective-permute-start(f32[192,128]{1,0:T(8,128)S(1)} %extract_0.1), channel_id=1, source_target_pairs={{1,2},{3,4},{5,6},{7,0},{2,1},{4,3},{6,5},{0,7},{9,10},{11,12},{13... | collective-permute-start | bytes 294920 | tf_op jit(solution)/shard_map/ppermute | solution.py:441
  9.7 2.2 %first_rows.1 = (f32[448,128]{1,0:T(8,128)}, f32[448,128]{1,0:T(8,128)}) custom-call(f32[4096,128]{1,0:T(8,128)} %bitcast.7, f32[2048,128]{1,0:T(8,128)} %bitcast.16), custom_call_target="tpu_custom_call" | custom-call | flops 1000 | bytes 1000 | tf_op jit(solution)/shard_map/first_rows/pallas_call | solution.py:469
  11.9 2.3 %collective-permute-start.4 = (f32[448,128]{1,0:T(8,128)}, f32[448,128]{1,0:T(8,128)S(1)}, u32[]{:S(2)}, u32[]{:S(2)}) collective-permute-start(f32[448,128]{1,0:T(8,128)} %get-tuple-element.36), channel_id=1, source_target_pairs={{0,8},{16,24},{8,0},{24,16},{1,9},{17,25},{9,1},{25,17},{2,10},{18... | collective-permute-start | bytes 688136 | tf_op jit(solution)/shard_map/ppermute | solution.py:441
  14.2 2.5 %collective-permute-start.5 = (f32[448,128]{1,0:T(8,128)}, f32[448,128]{1,0:T(8,128)S(1)}, u32[]{:S(2)}, u32[]{:S(2)}) collective-permute-start(f32[448,128]{1,0:T(8,128)} %get-tuple-element.37), channel_id=1, source_target_pairs={{8,16},{24,0},{16,8},{0,24},{9,17},{25,1},{17,9},{1,25},{10,18},{2... | collective-permute-start | bytes 688136 | tf_op jit(solution)/shard_map/ppermute | solution.py:441
  17.4 1.1 %collective-permute-start.1 = (f32[384,128]{1,0:T(8,128)}, f32[384,128]{1,0:T(8,128)S(1)}, u32[]{:S(2)}, u32[]{:S(2)}) collective-permute-start(f32[384,128]{1,0:T(8,128)} %copy-done.13), channel_id=1, source_target_pairs={{8,16},{24,0},{16,8},{0,24},{9,17},{25,1},{17,9},{1,25},{10,18},{2... | collective-permute-start | bytes 589832 | tf_op jit(solution)/shard_map/ppermute | solution.py:441
  18.5 1.3 %collective-permute-done.6.pack_a.refs_3_ = f32[192,128]{1,0:T(8,128)S(1)} collective-permute-done((f32[192,128]{1,0:T(8,128)S(1)}, f32[192,128]{1,0:T(8,128)S(1)}, u32[]{:S(2)}, u32[]{:S(2)}) %collective-permute-start.6) | collective-permute-done | bytes 98336 | tf_op jit(solution)/shard_map/ppermute | solution.py:441
  20.0 1.1 %speeds.1 = (f32[17,64,128]{2,1,0:T(8,128)S(1)}, f32[16,64,128]{2,1,0:T(8,128)S(1)}, f32[16,64,128]{2,1,0:T(8,128)S(1)}, f32[64,128]{1,0:T(8,128)S(1)}, f32[64,1...) custom-call(f32[2048,128]{1,0:T(8,128)S(1)} %bitcast.18, f32[16,128]{1,0:T(8,128)S(1)} %copy-done.8, ...), custom_call_target="tpu_custom_call" | custom-call | flops 1000 | bytes 1000 | tf_op jit(solution)/shard_map/speeds/pallas_call | solution.py:500
  21.1 8.6 %collective-permute-done.refs_1_ = f32[384,128]{1,0:T(8,128)S(1)} collective-permute-done((f32[384,128]{1,0:T(8,128)}, f32[384,128]{1,0:T(8,128)S(1)}, u32[]{:S(2)}, u32[]{:S(2)}) %collective-permute-start) | collective-permute-done | bytes 196640 | tf_op jit(solution)/shard_map/ppermute | solution.py:441
  29.7 5.1 %collective-permute-done.1.refs_2_ = f32[384,128]{1,0:T(8,128)S(1)} collective-permute-done((f32[384,128]{1,0:T(8,128)}, f32[384,128]{1,0:T(8,128)S(1)}, u32[]{:S(2)}, u32[]{:S(2)}) %collective-permute-start.1) | collective-permute-done | bytes 196640 | tf_op jit(solution)/shard_map/ppermute | solution.py:441
  34.9 1.6 %copy-done.1 = f32[4,64,16,128]{3,2,1,0:T(8,128)S(1)} copy-done((f32[4,64,16,128]{3,2,1,0:T(8,128)S(1)}, f32[4,64,16,128]{3,2,1,0:T(8,128)}, u32[]{:S(2)}) %copy-start.1) | copy-done | bytes 2097176
  36.5 2.9 %section_0_1.1 = (f32[16,128,128]{2,1,0:T(8,128)S(1)}, f32[384,128]{1,0:T(8,128)S(1)}, f32[384,128]{1,0:T(8,128)S(1)}, f32[128,128]{1,0:T(8,128)S(1)}) custom-call(f32[4096,128]{1,0:T(8,128)S(1)} %bitcast.10, f32[384,128]{1,0:T(8,128)S(1)} %collective-permute-done.refs_1_, f32[384,128]{1,0:T(8,128)S(1)} %collective-permute-done.1.refs_2_, ...), custom_call_target="tpu_custom_call" | custom-call | flops 1000 | bytes 1000 | tf_op jit(solution)/shard_map/section_0_1/pallas_call | solution.py:574
  40.1 2.6 %collective-permute-start.9 = (f32[384,128]{1,0:T(8,128)S(1)}, f32[384,128]{1,0:T(8,128)S(1)}, u32[]{:S(2)}, u32[]{:S(2)}) collective-permute-start(f32[384,128]{1,0:T(8,128)S(1)} %get-tuple-element.46), channel_id=1, source_target_pairs={{8,16},{24,0},{16,8},{0,24},{9,17},{25,1},{17,9},{1,25},{10,18},{2... | collective-permute-start | bytes 589832 | tf_op jit(solution)/shard_map/ppermute | solution.py:441
  42.7 1.9 %collective-permute-start.11 = (f32[128,128]{1,0:T(8,128)S(1)}, f32[128,128]{1,0:T(8,128)S(1)}, u32[]{:S(2)}, u32[]{:S(2)}) collective-permute-start(f32[128,128]{1,0:T(8,128)S(1)} %get-tuple-element.47), channel_id=1, source_target_pairs={{1,2},{3,4},{5,6},{7,0},{2,1},{4,3},{6,5},{0,7},{9,10},{11,12},{13... | collective-permute-start | bytes 196616 | tf_op jit(solution)/shard_map/ppermute | solution.py:441
  44.7 2.9 %section_0_0.1 = (f32[16,128,128]{2,1,0:T(8,128)S(1)}, f32[384,128]{1,0:T(8,128)S(1)}, f32[384,128]{1,0:T(8,128)S(1)}, f32[128,128]{1,0:T(8,128)S(1)}) custom-call(f32[4096,128]{1,0:T(8,128)S(1)} %bitcast.11, f32[448,128]{1,0:T(8,128)S(1)} %collective-permute-done.4.refs_5_.refs_6_.refs_1_, f32[448,128]{1,0:T(8,128)S(1)} %collective-permute-done.5.refs_6_.refs_7_.refs_2_, ...), custom_call_target="tpu_custom_call" | custom-call | flops 1000 | bytes 1000 | tf_op jit(solution)/shard_map/section_0_0/pallas_call | solution.py:574
  47.7 1.9 %collective-permute-start.17 = (f32[384,128]{1,0:T(8,128)S(1)}, f32[384,128]{1,0:T(8,128)S(1)}, u32[]{:S(2)}, u32[]{:S(2)}) collective-permute-start(f32[384,128]{1,0:T(8,128)S(1)} %get-tuple-element.54), channel_id=1, source_target_pairs={{8,16},{24,0},{16,8},{0,24},{9,17},{25,1},{17,9},{1,25},{10,18},{2... | collective-permute-start | bytes 589832 | tf_op jit(solution)/shard_map/ppermute | solution.py:441
  49.6 1.3 %collective-permute-done.10.refs_4_ = f32[128,128]{1,0:T(8,128)S(1)} collective-permute-done((f32[128,128]{1,0:T(8,128)S(1)}, f32[128,128]{1,0:T(8,128)S(1)}, u32[]{:S(2)}, u32[]{:S(2)}) %collective-permute-start.10) | collective-permute-done | bytes 65568 | tf_op jit(solution)/shard_map/ppermute | solution.py:441
  50.8 0.9 %collective-permute-start.19 = (f32[128,128]{1,0:T(8,128)S(1)}, f32[128,128]{1,0:T(8,128)S(1)}, u32[]{:S(2)}, u32[]{:S(2)}) collective-permute-start(f32[128,128]{1,0:T(8,128)S(1)} %get-tuple-element.55), channel_id=1, source_target_pairs={{1,2},{3,4},{5,6},{7,0},{2,1},{4,3},{6,5},{0,7},{9,10},{11,12},{13... | collective-permute-start | bytes 196616 | tf_op jit(solution)/shard_map/ppermute | solution.py:441
  51.7 2.8 %section_1_1.1 = (f32[16,128,128]{2,1,0:T(8,128)S(1)}, f32[384,128]{1,0:T(8,128)S(1)}, f32[384,128]{1,0:T(8,128)S(1)}, f32[128,128]{1,0:T(8,128)S(1)}) custom-call(f32[16,128,128]{2,1,0:T(8,128)S(1)} %get-tuple-element.44.refs_0_, f32[4096,128]{1,0:T(8,128)S(1)} %bitcast.12, f32[384,128]{1,0:T(8,128)S(1)} %collective-permute-done.8.refs_2_, ...), custom_call_target="tpu_custom_call" | custom-call | flops 1000 | bytes 1000 | tf_op jit(solution)/shard_map/section_1_1/pallas_call | solution.py:574
  54.6 1.8 %collective-permute-start.15 = (f32[128,128]{1,0:T(8,128)S(1)}, f32[128,128]{1,0:T(8,128)S(1)}, u32[]{:S(2)}, u32[]{:S(2)}) collective-permute-start(f32[128,128]{1,0:T(8,128)S(1)} %get-tuple-element.51), channel_id=1, source_target_pairs={{1,2},{3,4},{5,6},{7,0},{2,1},{4,3},{6,5},{0,7},{9,10},{11,12},{13... | collective-permute-start | bytes 196616 | tf_op jit(solution)/shard_map/ppermute | solution.py:441
  56.4 1.7 %collective-permute-start.14 = (f32[128,128]{1,0:T(8,128)S(1)}, f32[128,128]{1,0:T(8,128)S(1)}, u32[]{:S(2)}, u32[]{:S(2)}) collective-permute-start(f32[128,128]{1,0:T(8,128)S(1)} %get-tuple-element.51), channel_id=1, source_target_pairs={{0,1},{2,3},{4,5},{6,7},{1,0},{3,2},{5,4},{7,6},{8,9},{10,11},{12,... | collective-permute-start | bytes 196616 | tf_op jit(solution)/shard_map/ppermute | solution.py:441
  58.0 1.1 %collective-permute-done.16.refs_2_ = f32[384,128]{1,0:T(8,128)S(1)} collective-permute-done((f32[384,128]{1,0:T(8,128)S(1)}, f32[384,128]{1,0:T(8,128)S(1)}, u32[]{:S(2)}, u32[]{:S(2)}) %collective-permute-start.16) | collective-permute-done | bytes 196640 | tf_op jit(solution)/shard_map/ppermute | solution.py:441
  59.1 2.8 %section_1_0.1 = (f32[16,128,128]{2,1,0:T(8,128)S(1)}, f32[384,128]{1,0:T(8,128)S(1)}, f32[384,128]{1,0:T(8,128)S(1)}, f32[128,128]{1,0:T(8,128)S(1)}) custom-call(f32[16,128,128]{2,1,0:T(8,128)S(1)} %get-tuple-element.52.refs_0_, f32[4096,128]{1,0:T(8,128)S(1)} %bitcast.13, f32[384,128]{1,0:T(8,128)S(1)} %collective-permute-done.16.refs_2_, ...), custom_call_target="tpu_custom_call" | custom-call | flops 1000 | bytes 1000 | tf_op jit(solution)/shard_map/section_1_0/pallas_call | solution.py:574
  62.0 1.8 %collective-permute-start.20 = (f32[384,128]{1,0:T(8,128)S(1)}, f32[384,128]{1,0:T(8,128)S(1)}, u32[]{:S(2)}, u32[]{:S(2)}) collective-permute-start(f32[384,128]{1,0:T(8,128)S(1)} %get-tuple-element.57), channel_id=1, source_target_pairs={{0,8},{16,24},{8,0},{24,16},{1,9},{17,25},{9,1},{25,17},{2,10},{18... | collective-permute-start | bytes 589832 | tf_op jit(solution)/shard_map/ppermute | solution.py:441
  63.8 1.2 %collective-permute-start.21 = (f32[384,128]{1,0:T(8,128)S(1)}, f32[384,128]{1,0:T(8,128)S(1)}, u32[]{:S(2)}, u32[]{:S(2)}) collective-permute-start(f32[384,128]{1,0:T(8,128)S(1)} %get-tuple-element.58), channel_id=1, source_target_pairs={{8,16},{24,0},{16,8},{0,24},{9,17},{25,1},{17,9},{1,25},{10,18},{2... | collective-permute-start | bytes 589832 | tf_op jit(solution)/shard_map/ppermute | solution.py:441
  65.4 2.3 %collective-permute-start.13 = (f32[384,128]{1,0:T(8,128)S(1)}, f32[384,128]{1,0:T(8,128)S(1)}, u32[]{:S(2)}, u32[]{:S(2)}) collective-permute-start(f32[384,128]{1,0:T(8,128)S(1)} %get-tuple-element.50), channel_id=1, source_target_pairs={{8,16},{24,0},{16,8},{0,24},{9,17},{25,1},{17,9},{1,25},{10,18},{2... | collective-permute-start | bytes 589832 | tf_op jit(solution)/shard_map/ppermute | solution.py:441
  68.3 4.0 %collective-permute-done.23.refs_5_ = f32[128,128]{1,0:T(8,128)S(1)} collective-permute-done((f32[128,128]{1,0:T(8,128)S(1)}, f32[128,128]{1,0:T(8,128)S(1)}, u32[]{:S(2)}, u32[]{:S(2)}) %collective-permute-start.23) | collective-permute-done | bytes 65568 | tf_op jit(solution)/shard_map/ppermute | solution.py:441
  73.4 1.9 %south_north.1.refs_16_ = f32[16,128,128]{2,1,0:T(8,128)S(1)} custom-call(f32[16,128,128]{2,1,0:T(8,128)S(1)} %get-tuple-element.48.section.refs_0_, f32[128,128]{1,0:T(8,128)S(1)} %collective-permute-done.14.pack_a.refs_4_, f32[128,128]{1,0:T(8,128)S(1)} %collective-permute-done.15.pack_b.refs_5_, ...), custom_call_target="tpu_custom_call" | custom-call | flops 1000 | bytes 1000 | tf_op jit(solution)/shard_map/south_north/pallas_call | solution.py:533
  75.4 4.6 %section_2_0.1 = (f32[4096,128]{1,0:T(8,128)}, f32[10,256]{1,0:T(8,128)}, f32[1,256]{1,0:T(1,128)}) custom-call(f32[16,128,128]{2,1,0:T(8,128)S(1)} %get-tuple-element.56.refs_0_, f32[4096,128]{1,0:T(8,128)S(1)} %bitcast.14, f32[384,128]{1,0:T(8,128)S(1)} %collective-permute-done.20.refs_2_, f32[384,128]{1,0:T(8,128)S(1)} %collective-permute-done.21.refs_3_, ...), custom_call_target="tpu_custom_call" | custom-call | flops 1000 | bytes 1000 | tf_op jit(solution)/shard_map/section_2_0/pallas_call | solution.py:574
  80.0 1.9 %collective-permute-done.13.refs_3_ = f32[384,128]{1,0:T(8,128)S(1)} collective-permute-done((f32[384,128]{1,0:T(8,128)S(1)}, f32[384,128]{1,0:T(8,128)S(1)}, u32[]{:S(2)}, u32[]{:S(2)}) %collective-permute-start.13) | collective-permute-done | bytes 196640 | tf_op jit(solution)/shard_map/ppermute | solution.py:441
  81.9 1.8 %section_2_1.1 = f32[4096,128]{1,0:T(8,128)} custom-call(f32[16,128,128]{2,1,0:T(8,128)S(1)} %get-tuple-element.48.section.refs_0_, f32[4096,128]{1,0:T(8,128)S(1)} %bitcast.15, f32[384,128]{1,0:T(8,128)S(1)} %collective-permute-done.12.refs_2_, f32[384,128]{1,0:T(8,128)S(1)} %collective-permute-done.13.refs_3_, ...), custom_call_target="tpu_custom_call", output_to_operand_aliasing={{}: (17, {})} | custom-call | flops 1000 | bytes 1000 | tf_op jit(solution)/shard_map/section_2_1/pallas_call | solution.py:574
  (57 shorter events, 5.9 us)
Async XLA Ops:
  4.3 14.2 %collective-permute-start.7 = (f32[192,128]{1,0:T(8,128)S(1)}, f32[192,128]{1,0:T(8,128)S(1)}, u32[]{:S(2)}, u32[]{:S(2)}) collective-permute-start(f32[192,128]{1,0:T(8,128)S(1)} %extract_0.1), channel_id=1, source_target_pairs={{1,2},{3,4},{5,6},{7,0},{2,1},{4,3},{6,5},{0,7},{9,10},{11,12},{13... | collective-permute-start | bytes 294920 | tf_op jit(solution)/shard_map/ppermute | solution.py:441
  9.6 25.2 %copy-start.3 = (bf16[256,512]{1,0:T(8,128)(2,1)S(1)}, bf16[256,512]{1,0:T(8,128)(2,1)}, u32[]{:S(2)}) copy-start(bf16[256,512]{1,0:T(8,128)(2,1)} %constant.5.clone.refs_14_.refs_15_.edge_matrix) | copy-start | bytes 786436
  9.6 25.2 %copy-start.4 = (bf16[256,512]{1,0:T(8,128)(2,1)S(1)}, bf16[256,512]{1,0:T(8,128)(2,1)}, u32[]{:S(2)}) copy-start(bf16[256,512]{1,0:T(8,128)(2,1)} %constant.4.clone.refs_13_.refs_14_.inner_matrix) | copy-start | bytes 786436
  9.6 7.7 %collective-permute-start.3 = (f32[128,128]{1,0:T(8,128)S(1)}, f32[128,128]{1,0:T(8,128)S(1)}, u32[]{:S(2)}, u32[]{:S(2)}) collective-permute-start(f32[128,128]{1,0:T(8,128)S(1)} %get-tuple-element.35), channel_id=1, source_target_pairs={{1,2},{3,4},{5,6},{7,0},{2,1},{4,3},{6,5},{0,7},{9,10},{11,12},{13... | collective-permute-start | bytes 196616 | tf_op jit(solution)/shard_map/ppermute | solution.py:441
  11.9 22.9 %collective-permute-start.4 = (f32[448,128]{1,0:T(8,128)}, f32[448,128]{1,0:T(8,128)S(1)}, u32[]{:S(2)}, u32[]{:S(2)}) collective-permute-start(f32[448,128]{1,0:T(8,128)} %get-tuple-element.36), channel_id=1, source_target_pairs={{0,8},{16,24},{8,0},{24,16},{1,9},{17,25},{9,1},{25,17},{2,10},{18... | collective-permute-start | bytes 688136 | tf_op jit(solution)/shard_map/ppermute | solution.py:441
  14.2 20.6 %collective-permute-start.5 = (f32[448,128]{1,0:T(8,128)}, f32[448,128]{1,0:T(8,128)S(1)}, u32[]{:S(2)}, u32[]{:S(2)}) collective-permute-start(f32[448,128]{1,0:T(8,128)} %get-tuple-element.37), channel_id=1, source_target_pairs={{8,16},{24,0},{16,8},{0,24},{9,17},{25,1},{17,9},{1,25},{10,18},{2... | collective-permute-start | bytes 688136 | tf_op jit(solution)/shard_map/ppermute | solution.py:441
  16.7 13.0 %collective-permute-start = (f32[384,128]{1,0:T(8,128)}, f32[384,128]{1,0:T(8,128)S(1)}, u32[]{:S(2)}, u32[]{:S(2)}) collective-permute-start(f32[384,128]{1,0:T(8,128)} %copy-done.14), channel_id=1, source_target_pairs={{0,8},{16,24},{8,0},{24,16},{1,9},{17,25},{9,1},{25,17},{2,10},{18... | collective-permute-start | bytes 589832 | tf_op jit(solution)/shard_map/ppermute | solution.py:441
  17.4 17.5 %collective-permute-start.1 = (f32[384,128]{1,0:T(8,128)}, f32[384,128]{1,0:T(8,128)S(1)}, u32[]{:S(2)}, u32[]{:S(2)}) collective-permute-start(f32[384,128]{1,0:T(8,128)} %copy-done.13), channel_id=1, source_target_pairs={{8,16},{24,0},{16,8},{0,24},{9,17},{25,1},{17,9},{1,25},{10,18},{2... | collective-permute-start | bytes 589832 | tf_op jit(solution)/shard_map/ppermute | solution.py:441
  18.5 1.3 %collective-permute-start.6 = (f32[192,128]{1,0:T(8,128)S(1)}, f32[192,128]{1,0:T(8,128)S(1)}, u32[]{:S(2)}, u32[]{:S(2)}) collective-permute-start(f32[192,128]{1,0:T(8,128)S(1)} %extract_0.1), channel_id=1, source_target_pairs={{0,1},{2,3},{4,5},{6,7},{1,0},{3,2},{5,4},{7,6},{8,9},{10,11},{12,... | collective-permute-start | bytes 294920 | tf_op jit(solution)/shard_map/ppermute | solution.py:441
  19.8 1.3 %collective-permute-start.2 = (f32[128,128]{1,0:T(8,128)S(1)}, f32[128,128]{1,0:T(8,128)S(1)}, u32[]{:S(2)}, u32[]{:S(2)}) collective-permute-start(f32[128,128]{1,0:T(8,128)S(1)} %get-tuple-element.35), channel_id=1, source_target_pairs={{0,1},{2,3},{4,5},{6,7},{1,0},{3,2},{5,4},{7,6},{8,9},{10,11},{12,... | collective-permute-start | bytes 196616 | tf_op jit(solution)/shard_map/ppermute | solution.py:441
  39.4 12.3 %collective-permute-start.8 = (f32[384,128]{1,0:T(8,128)S(1)}, f32[384,128]{1,0:T(8,128)S(1)}, u32[]{:S(2)}, u32[]{:S(2)}) collective-permute-start(f32[384,128]{1,0:T(8,128)S(1)} %get-tuple-element.45), channel_id=1, source_target_pairs={{0,8},{16,24},{8,0},{24,16},{1,9},{17,25},{9,1},{25,17},{2,10},{18... | collective-permute-start | bytes 589832 | tf_op jit(solution)/shard_map/ppermute | solution.py:441
  40.1 11.7 %collective-permute-start.9 = (f32[384,128]{1,0:T(8,128)S(1)}, f32[384,128]{1,0:T(8,128)S(1)}, u32[]{:S(2)}, u32[]{:S(2)}) collective-permute-start(f32[384,128]{1,0:T(8,128)S(1)} %get-tuple-element.46), channel_id=1, source_target_pairs={{8,16},{24,0},{16,8},{0,24},{9,17},{25,1},{17,9},{1,25},{10,18},{2... | collective-permute-start | bytes 589832 | tf_op jit(solution)/shard_map/ppermute | solution.py:441
  42.7 6.9 %collective-permute-start.11 = (f32[128,128]{1,0:T(8,128)S(1)}, f32[128,128]{1,0:T(8,128)S(1)}, u32[]{:S(2)}, u32[]{:S(2)}) collective-permute-start(f32[128,128]{1,0:T(8,128)S(1)} %get-tuple-element.47), channel_id=1, source_target_pairs={{1,2},{3,4},{5,6},{7,0},{2,1},{4,3},{6,5},{0,7},{9,10},{11,12},{13... | collective-permute-start | bytes 196616 | tf_op jit(solution)/shard_map/ppermute | solution.py:441
  47.6 11.5 %collective-permute-start.16 = (f32[384,128]{1,0:T(8,128)S(1)}, f32[384,128]{1,0:T(8,128)S(1)}, u32[]{:S(2)}, u32[]{:S(2)}) collective-permute-start(f32[384,128]{1,0:T(8,128)S(1)} %get-tuple-element.53), channel_id=1, source_target_pairs={{0,8},{16,24},{8,0},{24,16},{1,9},{17,25},{9,1},{25,17},{2,10},{18... | collective-permute-start | bytes 589832 | tf_op jit(solution)/shard_map/ppermute | solution.py:441
  47.7 11.5 %collective-permute-start.17 = (f32[384,128]{1,0:T(8,128)S(1)}, f32[384,128]{1,0:T(8,128)S(1)}, u32[]{:S(2)}, u32[]{:S(2)}) collective-permute-start(f32[384,128]{1,0:T(8,128)S(1)} %get-tuple-element.54), channel_id=1, source_target_pairs={{8,16},{24,0},{16,8},{0,24},{9,17},{25,1},{17,9},{1,25},{10,18},{2... | collective-permute-start | bytes 589832 | tf_op jit(solution)/shard_map/ppermute | solution.py:441
  49.6 1.3 %collective-permute-start.10 = (f32[128,128]{1,0:T(8,128)S(1)}, f32[128,128]{1,0:T(8,128)S(1)}, u32[]{:S(2)}, u32[]{:S(2)}) collective-permute-start(f32[128,128]{1,0:T(8,128)S(1)} %get-tuple-element.47), channel_id=1, source_target_pairs={{0,1},{2,3},{4,5},{6,7},{1,0},{3,2},{5,4},{7,6},{8,9},{10,11},{12,... | collective-permute-start | bytes 196616 | tf_op jit(solution)/shard_map/ppermute | solution.py:441
  50.8 5.6 %collective-permute-start.19 = (f32[128,128]{1,0:T(8,128)S(1)}, f32[128,128]{1,0:T(8,128)S(1)}, u32[]{:S(2)}, u32[]{:S(2)}) collective-permute-start(f32[128,128]{1,0:T(8,128)S(1)} %get-tuple-element.55), channel_id=1, source_target_pairs={{1,2},{3,4},{5,6},{7,0},{2,1},{4,3},{6,5},{0,7},{9,10},{11,12},{13... | collective-permute-start | bytes 196616 | tf_op jit(solution)/shard_map/ppermute | solution.py:441
  51.7 6.3 %collective-permute-start.18 = (f32[128,128]{1,0:T(8,128)S(1)}, f32[128,128]{1,0:T(8,128)S(1)}, u32[]{:S(2)}, u32[]{:S(2)}) collective-permute-start(f32[128,128]{1,0:T(8,128)S(1)} %get-tuple-element.55), channel_id=1, source_target_pairs={{0,1},{2,3},{4,5},{6,7},{1,0},{3,2},{5,4},{7,6},{8,9},{10,11},{12,... | collective-permute-start | bytes 196616 | tf_op jit(solution)/shard_map/ppermute | solution.py:441
  54.6 10.8 %collective-permute-start.15 = (f32[128,128]{1,0:T(8,128)S(1)}, f32[128,128]{1,0:T(8,128)S(1)}, u32[]{:S(2)}, u32[]{:S(2)}) collective-permute-start(f32[128,128]{1,0:T(8,128)S(1)} %get-tuple-element.51), channel_id=1, source_target_pairs={{1,2},{3,4},{5,6},{7,0},{2,1},{4,3},{6,5},{0,7},{9,10},{11,12},{13... | collective-permute-start | bytes 196616 | tf_op jit(solution)/shard_map/ppermute | solution.py:441
  56.4 11.3 %collective-permute-start.14 = (f32[128,128]{1,0:T(8,128)S(1)}, f32[128,128]{1,0:T(8,128)S(1)}, u32[]{:S(2)}, u32[]{:S(2)}) collective-permute-start(f32[128,128]{1,0:T(8,128)S(1)} %get-tuple-element.51), channel_id=1, source_target_pairs={{0,1},{2,3},{4,5},{6,7},{1,0},{3,2},{5,4},{7,6},{8,9},{10,11},{12,... | collective-permute-start | bytes 196616 | tf_op jit(solution)/shard_map/ppermute | solution.py:441
  62.0 13.4 %copy-start.2 = (f32[4,64,16,128]{3,2,1,0:T(8,128)S(1)}, f32[4,64,16,128]{3,2,1,0:T(8,128)}, u32[]{:S(2)}) copy-start(f32[4,64,16,128]{3,2,1,0:T(8,128)} %param.11) | copy-start | bytes 6291460
  62.0 13.4 %copy-start.7 = (f32[10,256]{1,0:T(8,128)S(1)}, f32[10,256]{1,0:T(8,128)}, u32[]{:S(2)}) copy-start(f32[10,256]{1,0:T(8,128)} %refs_20_.1) | copy-start | bytes 30724
  62.0 13.4 %copy-start.9 = (f32[10,10]{1,0:T(8,128)S(1)}, f32[10,10]{1,0:T(8,128)}, u32[]{:S(2)}) copy-start(f32[10,10]{1,0:T(8,128)} %refs_19_.1) | copy-start | bytes 1204
  62.0 13.4 %copy-start.10 = (s32[256]{0:T(256)S(1)}, s32[256]{0:T(256)}, u32[]{:S(2)}) copy-start(s32[256]{0:T(256)} %param.15) | copy-start | bytes 3076
  62.0 13.4 %copy-start.11 = (s32[256]{0:T(256)S(1)}, s32[256]{0:T(256)}, u32[]{:S(2)}) copy-start(s32[256]{0:T(256)} %param.16) | copy-start | bytes 3076
  62.0 13.4 %copy-start.12 = (f32[256]{0:T(256)S(1)}, f32[256]{0:T(256)}, u32[]{:S(2)}) copy-start(f32[256]{0:T(256)} %param.19) | copy-start | bytes 3076
  62.0 13.3 %collective-permute-start.20 = (f32[384,128]{1,0:T(8,128)S(1)}, f32[384,128]{1,0:T(8,128)S(1)}, u32[]{:S(2)}, u32[]{:S(2)}) collective-permute-start(f32[384,128]{1,0:T(8,128)S(1)} %get-tuple-element.57), channel_id=1, source_target_pairs={{0,8},{16,24},{8,0},{24,16},{1,9},{17,25},{9,1},{25,17},{2,10},{18... | collective-permute-start | bytes 589832 | tf_op jit(solution)/shard_map/ppermute | solution.py:441
  63.8 11.5 %collective-permute-start.21 = (f32[384,128]{1,0:T(8,128)S(1)}, f32[384,128]{1,0:T(8,128)S(1)}, u32[]{:S(2)}, u32[]{:S(2)}) collective-permute-start(f32[384,128]{1,0:T(8,128)S(1)} %get-tuple-element.58), channel_id=1, source_target_pairs={{8,16},{24,0},{16,8},{0,24},{9,17},{25,1},{17,9},{1,25},{10,18},{2... | collective-permute-start | bytes 589832 | tf_op jit(solution)/shard_map/ppermute | solution.py:441
  65.0 15.0 %collective-permute-start.12 = (f32[384,128]{1,0:T(8,128)S(1)}, f32[384,128]{1,0:T(8,128)S(1)}, u32[]{:S(2)}, u32[]{:S(2)}) collective-permute-start(f32[384,128]{1,0:T(8,128)S(1)} %get-tuple-element.49), channel_id=1, source_target_pairs={{0,8},{16,24},{8,0},{24,16},{1,9},{17,25},{9,1},{25,17},{2,10},{18... | collective-permute-start | bytes 589832 | tf_op jit(solution)/shard_map/ppermute | solution.py:441
  65.4 16.5 %collective-permute-start.13 = (f32[384,128]{1,0:T(8,128)S(1)}, f32[384,128]{1,0:T(8,128)S(1)}, u32[]{:S(2)}, u32[]{:S(2)}) collective-permute-start(f32[384,128]{1,0:T(8,128)S(1)} %get-tuple-element.50), channel_id=1, source_target_pairs={{8,16},{24,0},{16,8},{0,24},{9,17},{25,1},{17,9},{1,25},{10,18},{2... | collective-permute-start | bytes 589832 | tf_op jit(solution)/shard_map/ppermute | solution.py:441
  67.7 4.6 %collective-permute-start.23 = (f32[128,128]{1,0:T(8,128)S(1)}, f32[128,128]{1,0:T(8,128)S(1)}, u32[]{:S(2)}, u32[]{:S(2)}) collective-permute-start(f32[128,128]{1,0:T(8,128)S(1)} %get-tuple-element.59), channel_id=1, source_target_pairs={{1,2},{3,4},{5,6},{7,0},{2,1},{4,3},{6,5},{0,7},{9,10},{11,12},{13... | collective-permute-start | bytes 196616 | tf_op jit(solution)/shard_map/ppermute | solution.py:441
  72.3 3.0 %collective-permute-start.22 = (f32[128,128]{1,0:T(8,128)S(1)}, f32[128,128]{1,0:T(8,128)S(1)}, u32[]{:S(2)}, u32[]{:S(2)}) collective-permute-start(f32[128,128]{1,0:T(8,128)S(1)} %get-tuple-element.59), channel_id=1, source_target_pairs={{0,1},{2,3},{4,5},{6,7},{1,0},{3,2},{5,4},{7,6},{8,9},{10,11},{12,... | collective-permute-start | bytes 196616 | tf_op jit(solution)/shard_map/ppermute | solution.py:441
  (7 other events, 27.8 us)

commit v4 on v3

--- a/solution.py
+++ b/solution.py
@@ -530,6 +530,7 @@
             scratch = [pltpu.VMEM((levels, y_size), jnp.float32)]
             scratch += [pltpu.VMEM((levels * x_size, y_size), jnp.float32)] * 4
             if split:
+                tied, indoor_out = lax.optimization_barrier((sections[c], indoor_out))
                 turned = pl.pallas_call(
                     south_north_kernel,
                     in_specs=[whole] * 9,
@@ -539,7 +540,7 @@
                     compiler_params=params,
                     cost_estimate=cheap,
                     name="south_north",
-                )(sections[c], *received[c][2:], *speeds[1:5], *matrices)
+                )(tied, *received[c][2:], *speeds[1:5], *matrices)
                 operands += [turned]
                 specs += [whole]
                 scratch = []

time: 83.9 us -> 63.8 us (0.76)
  waiting for transfers between devices: 23.3 us -> 7.5 us
  local copies, waits for them, and re-layouts: 5.79 us -> 1.64 us
    ppermute x12, waiting for transfers between devices: 12.3 us -> 2.53 us  [exchange(): lax.ppermute(to_a, axis, both[0])]
    ppermute x12, waiting for transfers between devices: 11 us -> 4.97 us  [exchange(): lax.ppermute(to_b, axis, both[1])]
    unnamed x30 -> x22, local copies, waits for them, and re-layouts: 5.79 us -> 1.64 us
    ppermute x12, starting transfers between devices: 8.2 us -> 5.09 us  [exchange(): lax.ppermute(to_a, axis, both[0])]
    ppermute x12, starting transfers between devices: 20.3 us -> 23.1 us  [exchange(): lax.ppermute(to_b, axis, both[1])]
  transfers between devices with their start and end apart: 24 -> 24, of which waited for: 7 -> 5; matrix products, arithmetic and copies ran while one was open for 0% -> 0% of each run, Pallas kernels for 23% -> 32%
where the time goes in v4:
time: 63.8 us; the launch traced here: 63.6 us
  starting transfers between devices  28.1 us (44%)
  Pallas kernels  24.8 us (39%)
  waiting for transfers between devices  7.5 us (12%)
  local copies, waits for them, and re-layouts  1.64 us (3%)
  between operations  1.51 us (2%)
    ppermute x12, starting transfers between devices, exchange(): lax.ppermute(to_b, axis, both[1])  23.1 us
    pallas_call x6, Pallas kernels, per_device(): pl.pallas_call(functools.partial(section_kernel, x_size, k, c, last, city...  18.1 us
    ppermute x12, starting transfers between devices, exchange(): lax.ppermute(to_a, axis, both[0])  5.09 us
    ppermute x12, waiting for transfers between devices, exchange(): lax.ppermute(to_b, axis, both[1])  4.97 us
    ppermute x12, waiting for transfers between devices, exchange(): lax.ppermute(to_a, axis, both[0])  2.53 us
    pallas_call x1, Pallas kernels, per_device(): pl.pallas_call(functools.partial(first_rows_kernel, x_size, rows, levels,...  2.28 us
    pallas_call x1, Pallas kernels, per_device(): pl.pallas_call(south_north_kernel, in_specs=[whole] * 9, out_specs=whole,...  1.91 us
    unnamed x22, local copies, waits for them, and re-layouts  1.64 us
  transfers between devices with their start and end apart: 24, of which 5 were waited for; matrix products, arithmetic and copies ran while one was open for 0% of the time, Pallas kernels for 32%

profile of v4, /device:TPU:0, one launch (start us, length us, event | category | flops | bytes accessed | tf_op | source)
XLA Modules:
  0.0 63.6 jit_solution(6247574283027160862)
XLA Ops:
  0.6 2.3 %first_rows.1 = (f32[448,128]{1,0:T(8,128)}, f32[448,128]{1,0:T(8,128)}) custom-call(f32[4096,128]{1,0:T(8,128)} %bitcast.7, f32[2048,128]{1,0:T(8,128)} %bitcast.16), custom_call_target="tpu_custom_call" | custom-call | flops 1000 | bytes 1000 | tf_op jit(solution)/shard_map/first_rows/pallas_call | solution.py:469
  2.9 3.1 %collective-permute-start.4 = (f32[448,128]{1,0:T(8,128)}, f32[448,128]{1,0:T(8,128)S(1)}, u32[]{:S(2)}, u32[]{:S(2)}) collective-permute-start(f32[448,128]{1,0:T(8,128)} %get-tuple-element.38), channel_id=1, source_target_pairs={{0,8},{16,24},{8,0},{24,16},{1,9},{17,25},{9,1},{25,17},{2,10},{18... | collective-permute-start | bytes 688136 | tf_op jit(solution)/shard_map/ppermute | solution.py:441
  6.0 2.5 %collective-permute-start.5 = (f32[448,128]{1,0:T(8,128)}, f32[448,128]{1,0:T(8,128)S(1)}, u32[]{:S(2)}, u32[]{:S(2)}) collective-permute-start(f32[448,128]{1,0:T(8,128)} %get-tuple-element.39), channel_id=1, source_target_pairs={{8,16},{24,0},{16,8},{0,24},{9,17},{25,1},{17,9},{1,25},{10,18},{2... | collective-permute-start | bytes 688136 | tf_op jit(solution)/shard_map/ppermute | solution.py:441
  8.5 1.6 %copy-done = f32[4,64,16,128]{3,2,1,0:T(8,128)S(1)} copy-done((f32[4,64,16,128]{3,2,1,0:T(8,128)S(1)}, f32[4,64,16,128]{3,2,1,0:T(8,128)}, u32[]{:S(2)}) %copy-start) | copy-done | bytes 2097176
  10.1 0.8 %extract_0.1 = f32[192,128]{1,0:T(8,128)S(1)} custom-call(f32[4096,128]{1,0:T(8,128)S(1)} %bitcast.8, f32[2048,128]{1,0:T(8,128)S(1)} %bitcast.17), custom_call_target="tpu_custom_call" | custom-call | flops 1000 | bytes 1000 | tf_op jit(solution)/shard_map/extract_0/pallas_call | solution.py:487
  11.0 1.4 %collective-permute-start.7 = (f32[192,128]{1,0:T(8,128)S(1)}, f32[192,128]{1,0:T(8,128)S(1)}, u32[]{:S(2)}, u32[]{:S(2)}) collective-permute-start(f32[192,128]{1,0:T(8,128)S(1)} %extract_0.1), channel_id=1, source_target_pairs={{1,2},{3,4},{5,6},{7,0},{2,1},{4,3},{6,5},{0,7},{9,10},{11,12},{13... | collective-permute-start | bytes 294920 | tf_op jit(solution)/shard_map/ppermute | solution.py:441
  12.4 0.3 collective-permute-start.6
  12.7 0.6 extract_1.1
  13.2 0.7 %collective-permute-start = (f32[384,128]{1,0:T(8,128)S(1)}, f32[384,128]{1,0:T(8,128)S(1)}, u32[]{:S(2)}, u32[]{:S(2)}) collective-permute-start(f32[384,128]{1,0:T(8,128)S(1)} %get-tuple-element.35), channel_id=1, source_target_pairs={{0,8},{16,24},{8,0},{24,16},{1,9},{17,25},{9,1},{25,17},{2,10},{18... | collective-permute-start | bytes 589832 | tf_op jit(solution)/shard_map/ppermute | solution.py:441
  14.0 3.0 %collective-permute-done.7.pack_b.refs_4_ = f32[192,128]{1,0:T(8,128)S(1)} collective-permute-done((f32[192,128]{1,0:T(8,128)S(1)}, f32[192,128]{1,0:T(8,128)S(1)}, u32[]{:S(2)}, u32[]{:S(2)}) %collective-permute-start.7) | collective-permute-done | bytes 98336 | tf_op jit(solution)/shard_map/ppermute | solution.py:441
  16.9 1.3 %collective-permute-start.1 = (f32[384,128]{1,0:T(8,128)S(1)}, f32[384,128]{1,0:T(8,128)S(1)}, u32[]{:S(2)}, u32[]{:S(2)}) collective-permute-start(f32[384,128]{1,0:T(8,128)S(1)} %get-tuple-element.36), channel_id=1, source_target_pairs={{8,16},{24,0},{16,8},{0,24},{9,17},{25,1},{17,9},{1,25},{10,18},{2... | collective-permute-start | bytes 589832 | tf_op jit(solution)/shard_map/ppermute | solution.py:441
  18.3 1.0 %collective-permute-start.3 = (f32[128,128]{1,0:T(8,128)S(1)}, f32[128,128]{1,0:T(8,128)S(1)}, u32[]{:S(2)}, u32[]{:S(2)}) collective-permute-start(f32[128,128]{1,0:T(8,128)S(1)} %get-tuple-element.37), channel_id=1, source_target_pairs={{1,2},{3,4},{5,6},{7,0},{2,1},{4,3},{6,5},{0,7},{9,10},{11,12},{13... | collective-permute-start | bytes 196616 | tf_op jit(solution)/shard_map/ppermute | solution.py:441
  19.3 1.1 %speeds.1 = (f32[17,64,128]{2,1,0:T(8,128)S(1)}, f32[16,64,128]{2,1,0:T(8,128)S(1)}, f32[16,64,128]{2,1,0:T(8,128)S(1)}, f32[64,128]{1,0:T(8,128)S(1)}, f32[64,1...) custom-call(f32[2048,128]{1,0:T(8,128)S(1)} %bitcast.18, f32[16,128]{1,0:T(8,128)S(1)} %copy-done.6, ...), custom_call_target="tpu_custom_call" | custom-call | flops 1000 | bytes 1000 | tf_op jit(solution)/shard_map/speeds/pallas_call | solution.py:500
  20.5 3.0 %section_0_0.1 = (f32[16,128,128]{2,1,0:T(8,128)S(1)}, f32[384,128]{1,0:T(8,128)S(1)}, f32[384,128]{1,0:T(8,128)S(1)}, f32[128,128]{1,0:T(8,128)S(1)}) custom-call(f32[4096,128]{1,0:T(8,128)S(1)} %bitcast.10, f32[448,128]{1,0:T(8,128)S(1)} %collective-permute-done.4.refs_5_.refs_6_.refs_1_, f32[448,128]{1,0:T(8,128)S(1)} %collective-permute-done.5.refs_6_.refs_7_.refs_2_, ...), custom_call_target="tpu_custom_call" | custom-call | flops 1000 | bytes 1000 | tf_op jit(solution)/shard_map/section_0_0/pallas_call | solution.py:575
  23.5 3.0 %collective-permute-start.17 = (f32[384,128]{1,0:T(8,128)S(1)}, f32[384,128]{1,0:T(8,128)S(1)}, u32[]{:S(2)}, u32[]{:S(2)}) collective-permute-start(f32[384,128]{1,0:T(8,128)S(1)} %get-tuple-element.56), channel_id=1, source_target_pairs={{8,16},{24,0},{16,8},{0,24},{9,17},{25,1},{17,9},{1,25},{10,18},{2... | collective-permute-start | bytes 589832 | tf_op jit(solution)/shard_map/ppermute | solution.py:441
  26.5 0.9 %collective-permute-start.19 = (f32[128,128]{1,0:T(8,128)S(1)}, f32[128,128]{1,0:T(8,128)S(1)}, u32[]{:S(2)}, u32[]{:S(2)}) collective-permute-start(f32[128,128]{1,0:T(8,128)S(1)} %get-tuple-element.57), channel_id=1, source_target_pairs={{1,2},{3,4},{5,6},{7,0},{2,1},{4,3},{6,5},{0,7},{9,10},{11,12},{13... | collective-permute-start | bytes 196616 | tf_op jit(solution)/shard_map/ppermute | solution.py:441
  27.6 2.9 %section_0_1.1 = (f32[16,128,128]{2,1,0:T(8,128)S(1)}, f32[384,128]{1,0:T(8,128)S(1)}, f32[384,128]{1,0:T(8,128)S(1)}, f32[128,128]{1,0:T(8,128)S(1)}) custom-call(f32[4096,128]{1,0:T(8,128)S(1)} %bitcast.11, f32[384,128]{1,0:T(8,128)S(1)} %collective-permute-done.refs_1_, f32[384,128]{1,0:T(8,128)S(1)} %collective-permute-done.1.refs_2_, ...), custom_call_target="tpu_custom_call" | custom-call | flops 1000 | bytes 1000 | tf_op jit(solution)/shard_map/section_0_1/pallas_call | solution.py:575
  30.5 0.7 %collective-permute-start.8 = (f32[384,128]{1,0:T(8,128)S(1)}, f32[384,128]{1,0:T(8,128)S(1)}, u32[]{:S(2)}, u32[]{:S(2)}) collective-permute-start(f32[384,128]{1,0:T(8,128)S(1)} %get-tuple-element.47), channel_id=1, source_target_pairs={{0,8},{16,24},{8,0},{24,16},{1,9},{17,25},{9,1},{25,17},{2,10},{18... | collective-permute-start | bytes 589832 | tf_op jit(solution)/shard_map/ppermute | solution.py:441
  31.2 2.5 %collective-permute-start.9 = (f32[384,128]{1,0:T(8,128)S(1)}, f32[384,128]{1,0:T(8,128)S(1)}, u32[]{:S(2)}, u32[]{:S(2)}) collective-permute-start(f32[384,128]{1,0:T(8,128)S(1)} %get-tuple-element.48), channel_id=1, source_target_pairs={{8,16},{24,0},{16,8},{0,24},{9,17},{25,1},{17,9},{1,25},{10,18},{2... | collective-permute-start | bytes 589832 | tf_op jit(solution)/shard_map/ppermute | solution.py:441
  33.7 1.3 %collective-permute-done.18.refs_4_ = f32[128,128]{1,0:T(8,128)S(1)} collective-permute-done((f32[128,128]{1,0:T(8,128)S(1)}, f32[128,128]{1,0:T(8,128)S(1)}, u32[]{:S(2)}, u32[]{:S(2)}) %collective-permute-start.18) | collective-permute-done | bytes 65568 | tf_op jit(solution)/shard_map/ppermute | solution.py:441
  34.9 2.7 %collective-permute-start.11 = (f32[128,128]{1,0:T(8,128)S(1)}, f32[128,128]{1,0:T(8,128)S(1)}, u32[]{:S(2)}, u32[]{:S(2)}) collective-permute-start(f32[128,128]{1,0:T(8,128)S(1)} %get-tuple-element.49), channel_id=1, source_target_pairs={{1,2},{3,4},{5,6},{7,0},{2,1},{4,3},{6,5},{0,7},{9,10},{11,12},{13... | collective-permute-start | bytes 196616 | tf_op jit(solution)/shard_map/ppermute | solution.py:441
  37.7 2.8 %section_1_0.1 = (f32[16,128,128]{2,1,0:T(8,128)S(1)}, f32[384,128]{1,0:T(8,128)S(1)}, f32[384,128]{1,0:T(8,128)S(1)}, f32[128,128]{1,0:T(8,128)S(1)}) custom-call(f32[16,128,128]{2,1,0:T(8,128)S(1)} %get-tuple-element.54.refs_0_, f32[4096,128]{1,0:T(8,128)S(1)} %bitcast.12, f32[384,128]{1,0:T(8,128)S(1)} %collective-permute-done.16.refs_2_, ...), custom_call_target="tpu_custom_call" | custom-call | flops 1000 | bytes 1000 | tf_op jit(solution)/shard_map/section_1_0/pallas_call | solution.py:575
  40.6 2.3 %collective-permute-start.21 = (f32[384,128]{1,0:T(8,128)S(1)}, f32[384,128]{1,0:T(8,128)S(1)}, u32[]{:S(2)}, u32[]{:S(2)}) collective-permute-start(f32[384,128]{1,0:T(8,128)S(1)} %get-tuple-element.60), channel_id=1, source_target_pairs={{8,16},{24,0},{16,8},{0,24},{9,17},{25,1},{17,9},{1,25},{10,18},{2... | collective-permute-start | bytes 589832 | tf_op jit(solution)/shard_map/ppermute | solution.py:441
  42.9 0.2 collective-permute-start.23
  43.1 1.8 %collective-permute-done.9.refs_3_ = f32[384,128]{1,0:T(8,128)S(1)} collective-permute-done((f32[384,128]{1,0:T(8,128)S(1)}, f32[384,128]{1,0:T(8,128)S(1)}, u32[]{:S(2)}, u32[]{:S(2)}) %collective-permute-start.9) | collective-permute-done | bytes 196640 | tf_op jit(solution)/shard_map/ppermute | solution.py:441
  45.0 2.8 %section_1_1.1 = (f32[16,128,128]{2,1,0:T(8,128)S(1)}, f32[384,128]{1,0:T(8,128)S(1)}, f32[384,128]{1,0:T(8,128)S(1)}, f32[128,128]{1,0:T(8,128)S(1)}) custom-call(f32[16,128,128]{2,1,0:T(8,128)S(1)} %get-tuple-element.46.refs_0_, f32[4096,128]{1,0:T(8,128)S(1)} %bitcast.13, f32[384,128]{1,0:T(8,128)S(1)} %collective-permute-done.8.refs_2_, ...), custom_call_target="tpu_custom_call" | custom-call | flops 1000 | bytes 1000 | tf_op jit(solution)/shard_map/section_1_1/pallas_call | solution.py:575
  48.0 3.4 %collective-permute-start.13 = (f32[384,128]{1,0:T(8,128)S(1)}, f32[384,128]{1,0:T(8,128)S(1)}, u32[]{:S(2)}, u32[]{:S(2)}) collective-permute-start(f32[384,128]{1,0:T(8,128)S(1)} %get-tuple-element.52), channel_id=1, source_target_pairs={{8,16},{24,0},{16,8},{0,24},{9,17},{25,1},{17,9},{1,25},{10,18},{2... | collective-permute-start | bytes 589832 | tf_op jit(solution)/shard_map/ppermute | solution.py:441
  51.4 1.3 %collective-permute-done.22.refs_4_ = f32[128,128]{1,0:T(8,128)S(1)} collective-permute-done((f32[128,128]{1,0:T(8,128)S(1)}, f32[128,128]{1,0:T(8,128)S(1)}, u32[]{:S(2)}, u32[]{:S(2)}) %collective-permute-start.22) | collective-permute-done | bytes 65568 | tf_op jit(solution)/shard_map/ppermute | solution.py:441
  52.6 1.8 %collective-permute-start.15 = (f32[128,128]{1,0:T(8,128)S(1)}, f32[128,128]{1,0:T(8,128)S(1)}, u32[]{:S(2)}, u32[]{:S(2)}) collective-permute-start(f32[128,128]{1,0:T(8,128)S(1)} %get-tuple-element.53), channel_id=1, source_target_pairs={{1,2},{3,4},{5,6},{7,0},{2,1},{4,3},{6,5},{0,7},{9,10},{11,12},{13... | collective-permute-start | bytes 196616 | tf_op jit(solution)/shard_map/ppermute | solution.py:441
  55.2 4.6 %section_2_0.1 = (f32[4096,128]{1,0:T(8,128)}, f32[10,256]{1,0:T(8,128)}, f32[1,256]{1,0:T(1,128)}) custom-call(f32[16,128,128]{2,1,0:T(8,128)S(1)} %get-tuple-element.58.refs_0_, f32[4096,128]{1,0:T(8,128)S(1)} %bitcast.14, f32[384,128]{1,0:T(8,128)S(1)} %collective-permute-done.20.refs_2_, f32[384,128]{1,0:T(8,128)S(1)} %collective-permute-done.21.refs_3_, ...), custom_call_target="tpu_custom_call" | custom-call | flops 1000 | bytes 1000 | tf_op jit(solution)/shard_map/section_2_0/pallas_call | solution.py:575
  59.8 1.9 %south_north.1.refs_16_ = f32[16,128,128]{2,1,0:T(8,128)S(1)} custom-call(f32[16,128,128]{2,1,0:T(8,128)S(1)} %get-tuple-element.63.section.refs_0_, f32[128,128]{1,0:T(8,128)S(1)} %collective-permute-done.14.pack_a.refs_4_, f32[128,128]{1,0:T(8,128)S(1)} %collective-permute-done.15.pack_b.refs_5_, ...), custom_call_target="tpu_custom_call" | custom-call | flops 1000 | bytes 1000 | tf_op jit(solution)/shard_map/south_north/pallas_call | solution.py:534
  61.7 1.9 %section_2_1.1 = f32[4096,128]{1,0:T(8,128)} custom-call(f32[16,128,128]{2,1,0:T(8,128)S(1)} %get-tuple-element.63.section.refs_0_, f32[4096,128]{1,0:T(8,128)S(1)} %bitcast.15, f32[384,128]{1,0:T(8,128)S(1)} %collective-permute-done.12.refs_2_, f32[384,128]{1,0:T(8,128)S(1)} %collective-permute-done.13.refs_3_, ...), custom_call_target="tpu_custom_call", output_to_operand_aliasing={{}: (17, {})} | custom-call | flops 1000 | bytes 1000 | tf_op jit(solution)/shard_map/section_2_1/pallas_call | solution.py:575
  (49 shorter events, 0.5 us)
Async XLA Ops:
  2.9 16.4 %collective-permute-start.4 = (f32[448,128]{1,0:T(8,128)}, f32[448,128]{1,0:T(8,128)S(1)}, u32[]{:S(2)}, u32[]{:S(2)}) collective-permute-start(f32[448,128]{1,0:T(8,128)} %get-tuple-element.38), channel_id=1, source_target_pairs={{0,8},{16,24},{8,0},{24,16},{1,9},{17,25},{9,1},{25,17},{2,10},{18... | collective-permute-start | bytes 688136 | tf_op jit(solution)/shard_map/ppermute | solution.py:441
  6.0 14.5 %collective-permute-start.5 = (f32[448,128]{1,0:T(8,128)}, f32[448,128]{1,0:T(8,128)S(1)}, u32[]{:S(2)}, u32[]{:S(2)}) collective-permute-start(f32[448,128]{1,0:T(8,128)} %get-tuple-element.39), channel_id=1, source_target_pairs={{8,16},{24,0},{16,8},{0,24},{9,17},{25,1},{17,9},{1,25},{10,18},{2... | collective-permute-start | bytes 688136 | tf_op jit(solution)/shard_map/ppermute | solution.py:441
  10.9 9.5 %copy-start.1 = (f32[4,64,16,128]{3,2,1,0:T(8,128)S(1)}, f32[4,64,16,128]{3,2,1,0:T(8,128)}, u32[]{:S(2)}) copy-start(f32[4,64,16,128]{3,2,1,0:T(8,128)} %param.11) | copy-start | bytes 6291460
  11.0 9.5 %copy-start.2 = (bf16[256,512]{1,0:T(8,128)(2,1)S(1)}, bf16[256,512]{1,0:T(8,128)(2,1)}, u32[]{:S(2)}) copy-start(bf16[256,512]{1,0:T(8,128)(2,1)} %constant.5.clone.refs_14_.refs_15_.edge_matrix) | copy-start | bytes 786436
  11.0 9.5 %copy-start.3 = (bf16[256,512]{1,0:T(8,128)(2,1)S(1)}, bf16[256,512]{1,0:T(8,128)(2,1)}, u32[]{:S(2)}) copy-start(bf16[256,512]{1,0:T(8,128)(2,1)} %constant.4.clone.refs_13_.refs_14_.inner_matrix) | copy-start | bytes 786436
  11.0 6.0 %collective-permute-start.7 = (f32[192,128]{1,0:T(8,128)S(1)}, f32[192,128]{1,0:T(8,128)S(1)}, u32[]{:S(2)}, u32[]{:S(2)}) collective-permute-start(f32[192,128]{1,0:T(8,128)S(1)} %extract_0.1), channel_id=1, source_target_pairs={{1,2},{3,4},{5,6},{7,0},{2,1},{4,3},{6,5},{0,7},{9,10},{11,12},{13... | collective-permute-start | bytes 294920 | tf_op jit(solution)/shard_map/ppermute | solution.py:441
  12.4 5.9 %collective-permute-start.6 = (f32[192,128]{1,0:T(8,128)S(1)}, f32[192,128]{1,0:T(8,128)S(1)}, u32[]{:S(2)}, u32[]{:S(2)}) collective-permute-start(f32[192,128]{1,0:T(8,128)S(1)} %extract_0.1), channel_id=1, source_target_pairs={{0,1},{2,3},{4,5},{6,7},{1,0},{3,2},{5,4},{7,6},{8,9},{10,11},{12,... | collective-permute-start | bytes 294920 | tf_op jit(solution)/shard_map/ppermute | solution.py:441
  13.2 14.2 %collective-permute-start = (f32[384,128]{1,0:T(8,128)S(1)}, f32[384,128]{1,0:T(8,128)S(1)}, u32[]{:S(2)}, u32[]{:S(2)}) collective-permute-start(f32[384,128]{1,0:T(8,128)S(1)} %get-tuple-element.35), channel_id=1, source_target_pairs={{0,8},{16,24},{8,0},{24,16},{1,9},{17,25},{9,1},{25,17},{2,10},{18... | collective-permute-start | bytes 589832 | tf_op jit(solution)/shard_map/ppermute | solution.py:441
  16.9 10.6 %collective-permute-start.1 = (f32[384,128]{1,0:T(8,128)S(1)}, f32[384,128]{1,0:T(8,128)S(1)}, u32[]{:S(2)}, u32[]{:S(2)}) collective-permute-start(f32[384,128]{1,0:T(8,128)S(1)} %get-tuple-element.36), channel_id=1, source_target_pairs={{8,16},{24,0},{16,8},{0,24},{9,17},{25,1},{17,9},{1,25},{10,18},{2... | collective-permute-start | bytes 589832 | tf_op jit(solution)/shard_map/ppermute | solution.py:441
  18.3 5.3 %collective-permute-start.3 = (f32[128,128]{1,0:T(8,128)S(1)}, f32[128,128]{1,0:T(8,128)S(1)}, u32[]{:S(2)}, u32[]{:S(2)}) collective-permute-start(f32[128,128]{1,0:T(8,128)S(1)} %get-tuple-element.37), channel_id=1, source_target_pairs={{1,2},{3,4},{5,6},{7,0},{2,1},{4,3},{6,5},{0,7},{9,10},{11,12},{13... | collective-permute-start | bytes 196616 | tf_op jit(solution)/shard_map/ppermute | solution.py:441
  19.3 7.2 %collective-permute-start.2 = (f32[128,128]{1,0:T(8,128)S(1)}, f32[128,128]{1,0:T(8,128)S(1)}, u32[]{:S(2)}, u32[]{:S(2)}) collective-permute-start(f32[128,128]{1,0:T(8,128)S(1)} %get-tuple-element.37), channel_id=1, source_target_pairs={{0,1},{2,3},{4,5},{6,7},{1,0},{3,2},{5,4},{7,6},{8,9},{10,11},{12,... | collective-permute-start | bytes 196616 | tf_op jit(solution)/shard_map/ppermute | solution.py:441
  23.5 14.2 %collective-permute-start.16 = (f32[384,128]{1,0:T(8,128)S(1)}, f32[384,128]{1,0:T(8,128)S(1)}, u32[]{:S(2)}, u32[]{:S(2)}) collective-permute-start(f32[384,128]{1,0:T(8,128)S(1)} %get-tuple-element.55), channel_id=1, source_target_pairs={{0,8},{16,24},{8,0},{24,16},{1,9},{17,25},{9,1},{25,17},{2,10},{18... | collective-permute-start | bytes 589832 | tf_op jit(solution)/shard_map/ppermute | solution.py:441
  23.5 14.1 %collective-permute-start.17 = (f32[384,128]{1,0:T(8,128)S(1)}, f32[384,128]{1,0:T(8,128)S(1)}, u32[]{:S(2)}, u32[]{:S(2)}) collective-permute-start(f32[384,128]{1,0:T(8,128)S(1)} %get-tuple-element.56), channel_id=1, source_target_pairs={{8,16},{24,0},{16,8},{0,24},{9,17},{25,1},{17,9},{1,25},{10,18},{2... | collective-permute-start | bytes 589832 | tf_op jit(solution)/shard_map/ppermute | solution.py:441
  26.5 7.1 %collective-permute-start.19 = (f32[128,128]{1,0:T(8,128)S(1)}, f32[128,128]{1,0:T(8,128)S(1)}, u32[]{:S(2)}, u32[]{:S(2)}) collective-permute-start(f32[128,128]{1,0:T(8,128)S(1)} %get-tuple-element.57), channel_id=1, source_target_pairs={{1,2},{3,4},{5,6},{7,0},{2,1},{4,3},{6,5},{0,7},{9,10},{11,12},{13... | collective-permute-start | bytes 196616 | tf_op jit(solution)/shard_map/ppermute | solution.py:441
  30.5 12.6 %collective-permute-start.8 = (f32[384,128]{1,0:T(8,128)S(1)}, f32[384,128]{1,0:T(8,128)S(1)}, u32[]{:S(2)}, u32[]{:S(2)}) collective-permute-start(f32[384,128]{1,0:T(8,128)S(1)} %get-tuple-element.47), channel_id=1, source_target_pairs={{0,8},{16,24},{8,0},{24,16},{1,9},{17,25},{9,1},{25,17},{2,10},{18... | collective-permute-start | bytes 589832 | tf_op jit(solution)/shard_map/ppermute | solution.py:441
  31.2 13.8 %collective-permute-start.9 = (f32[384,128]{1,0:T(8,128)S(1)}, f32[384,128]{1,0:T(8,128)S(1)}, u32[]{:S(2)}, u32[]{:S(2)}) collective-permute-start(f32[384,128]{1,0:T(8,128)S(1)} %get-tuple-element.48), channel_id=1, source_target_pairs={{8,16},{24,0},{16,8},{0,24},{9,17},{25,1},{17,9},{1,25},{10,18},{2... | collective-permute-start | bytes 589832 | tf_op jit(solution)/shard_map/ppermute | solution.py:441
  33.7 1.3 %collective-permute-start.18 = (f32[128,128]{1,0:T(8,128)S(1)}, f32[128,128]{1,0:T(8,128)S(1)}, u32[]{:S(2)}, u32[]{:S(2)}) collective-permute-start(f32[128,128]{1,0:T(8,128)S(1)} %get-tuple-element.57), channel_id=1, source_target_pairs={{0,1},{2,3},{4,5},{6,7},{1,0},{3,2},{5,4},{7,6},{8,9},{10,11},{12,... | collective-permute-start | bytes 196616 | tf_op jit(solution)/shard_map/ppermute | solution.py:441
  34.9 5.6 %collective-permute-start.11 = (f32[128,128]{1,0:T(8,128)S(1)}, f32[128,128]{1,0:T(8,128)S(1)}, u32[]{:S(2)}, u32[]{:S(2)}) collective-permute-start(f32[128,128]{1,0:T(8,128)S(1)} %get-tuple-element.49), channel_id=1, source_target_pairs={{1,2},{3,4},{5,6},{7,0},{2,1},{4,3},{6,5},{0,7},{9,10},{11,12},{13... | collective-permute-start | bytes 196616 | tf_op jit(solution)/shard_map/ppermute | solution.py:441
  37.7 5.2 %collective-permute-start.10 = (f32[128,128]{1,0:T(8,128)S(1)}, f32[128,128]{1,0:T(8,128)S(1)}, u32[]{:S(2)}, u32[]{:S(2)}) collective-permute-start(f32[128,128]{1,0:T(8,128)S(1)} %get-tuple-element.49), channel_id=1, source_target_pairs={{0,1},{2,3},{4,5},{6,7},{1,0},{3,2},{5,4},{7,6},{8,9},{10,11},{12,... | collective-permute-start | bytes 196616 | tf_op jit(solution)/shard_map/ppermute | solution.py:441
  40.5 13.9 %collective-permute-start.20 = (f32[384,128]{1,0:T(8,128)S(1)}, f32[384,128]{1,0:T(8,128)S(1)}, u32[]{:S(2)}, u32[]{:S(2)}) collective-permute-start(f32[384,128]{1,0:T(8,128)S(1)} %get-tuple-element.59), channel_id=1, source_target_pairs={{0,8},{16,24},{8,0},{24,16},{1,9},{17,25},{9,1},{25,17},{2,10},{18... | collective-permute-start | bytes 589832 | tf_op jit(solution)/shard_map/ppermute | solution.py:441
  40.6 14.5 %collective-permute-start.21 = (f32[384,128]{1,0:T(8,128)S(1)}, f32[384,128]{1,0:T(8,128)S(1)}, u32[]{:S(2)}, u32[]{:S(2)}) collective-permute-start(f32[384,128]{1,0:T(8,128)S(1)} %get-tuple-element.60), channel_id=1, source_target_pairs={{8,16},{24,0},{16,8},{0,24},{9,17},{25,1},{17,9},{1,25},{10,18},{2... | collective-permute-start | bytes 589832 | tf_op jit(solution)/shard_map/ppermute | solution.py:441
  42.9 8.5 %collective-permute-start.23 = (f32[128,128]{1,0:T(8,128)S(1)}, f32[128,128]{1,0:T(8,128)S(1)}, u32[]{:S(2)}, u32[]{:S(2)}) collective-permute-start(f32[128,128]{1,0:T(8,128)S(1)} %get-tuple-element.61), channel_id=1, source_target_pairs={{1,2},{3,4},{5,6},{7,0},{2,1},{4,3},{6,5},{0,7},{9,10},{11,12},{13... | collective-permute-start | bytes 196616 | tf_op jit(solution)/shard_map/ppermute | solution.py:441
  45.0 10.1 %copy-start.5 = (f32[10,256]{1,0:T(8,128)S(1)}, f32[10,256]{1,0:T(8,128)}, u32[]{:S(2)}) copy-start(f32[10,256]{1,0:T(8,128)} %refs_20_.1) | copy-start | bytes 30724
  45.0 10.2 %copy-start.7 = (f32[10,10]{1,0:T(8,128)S(1)}, f32[10,10]{1,0:T(8,128)}, u32[]{:S(2)}) copy-start(f32[10,10]{1,0:T(8,128)} %refs_19_.1) | copy-start | bytes 1204
  45.0 10.2 %copy-start.8 = (s32[256]{0:T(256)S(1)}, s32[256]{0:T(256)}, u32[]{:S(2)}) copy-start(s32[256]{0:T(256)} %param.15) | copy-start | bytes 3076
  45.0 10.2 %copy-start.9 = (s32[256]{0:T(256)S(1)}, s32[256]{0:T(256)}, u32[]{:S(2)}) copy-start(s32[256]{0:T(256)} %param.16) | copy-start | bytes 3076
  45.0 10.2 %copy-start.10 = (f32[256]{0:T(256)S(1)}, f32[256]{0:T(256)}, u32[]{:S(2)}) copy-start(f32[256]{0:T(256)} %param.19) | copy-start | bytes 3076
  47.8 13.9 %collective-permute-start.12 = (f32[384,128]{1,0:T(8,128)S(1)}, f32[384,128]{1,0:T(8,128)S(1)}, u32[]{:S(2)}, u32[]{:S(2)}) collective-permute-start(f32[384,128]{1,0:T(8,128)S(1)} %get-tuple-element.51), channel_id=1, source_target_pairs={{0,8},{16,24},{8,0},{24,16},{1,9},{17,25},{9,1},{25,17},{2,10},{18... | collective-permute-start | bytes 589832 | tf_op jit(solution)/shard_map/ppermute | solution.py:441
  48.0 13.8 %collective-permute-start.13 = (f32[384,128]{1,0:T(8,128)S(1)}, f32[384,128]{1,0:T(8,128)S(1)}, u32[]{:S(2)}, u32[]{:S(2)}) collective-permute-start(f32[384,128]{1,0:T(8,128)S(1)} %get-tuple-element.52), channel_id=1, source_target_pairs={{8,16},{24,0},{16,8},{0,24},{9,17},{25,1},{17,9},{1,25},{10,18},{2... | collective-permute-start | bytes 589832 | tf_op jit(solution)/shard_map/ppermute | solution.py:441
  51.3 1.3 %collective-permute-start.22 = (f32[128,128]{1,0:T(8,128)S(1)}, f32[128,128]{1,0:T(8,128)S(1)}, u32[]{:S(2)}, u32[]{:S(2)}) collective-permute-start(f32[128,128]{1,0:T(8,128)S(1)} %get-tuple-element.61), channel_id=1, source_target_pairs={{0,1},{2,3},{4,5},{6,7},{1,0},{3,2},{5,4},{7,6},{8,9},{10,11},{12,... | collective-permute-start | bytes 196616 | tf_op jit(solution)/shard_map/ppermute | solution.py:441
  52.6 7.2 %collective-permute-start.15 = (f32[128,128]{1,0:T(8,128)S(1)}, f32[128,128]{1,0:T(8,128)S(1)}, u32[]{:S(2)}, u32[]{:S(2)}) collective-permute-start(f32[128,128]{1,0:T(8,128)S(1)} %get-tuple-element.53), channel_id=1, source_target_pairs={{1,2},{3,4},{5,6},{7,0},{2,1},{4,3},{6,5},{0,7},{9,10},{11,12},{13... | collective-permute-start | bytes 196616 | tf_op jit(solution)/shard_map/ppermute | solution.py:441
  54.4 5.4 %collective-permute-start.14 = (f32[128,128]{1,0:T(8,128)S(1)}, f32[128,128]{1,0:T(8,128)S(1)}, u32[]{:S(2)}, u32[]{:S(2)}) collective-permute-start(f32[128,128]{1,0:T(8,128)S(1)} %get-tuple-element.53), channel_id=1, source_target_pairs={{0,1},{2,3},{4,5},{6,7},{1,0},{3,2},{5,4},{7,6},{8,9},{10,11},{12,... | collective-permute-start | bytes 196616 | tf_op jit(solution)/shard_map/ppermute | solution.py:441
  (3 other events, 18.7 us)
